TPU v7x, 32 devices: a whole 2x2x4 slice. The times are simulated.
32 devices in a mesh: dp: 8 (over y, x, core), mp: 4 (over z).
Axes of the slice: x: 2, y: 2, z: 4, core: 2. Of those that a mesh axis runs over, the one named last changes fastest.
Arguments:
- query_states: bfloat16 [64, 128, 768], P(('dp', 'mp'))
- passage_states: bfloat16 [32, 512, 768], P(('dp', 'mp'))
- query_lengths: int32 [64], P('dp'), may hold values from 16 to 128, as said below
- passage_lengths: int32 [32], P('dp'), may hold values from 64 to 512, as said below
- query_count: int32 [32], replicated, may hold values from 0 to 2, as said below
- passage_count: int32 [32], replicated, may hold values from 0 to 1, as said below
- positive: int32 [64], P(('dp', 'mp')), may hold values from 0 to 31, as said below
- query_key_value_matrix: bfloat16 [2, 3, 768, 768], P(None, None, None, 'mp'), may hold values from -0.21875 to 0.21875
- qv_bias: bfloat16 [2, 2, 768], P(None, None, 'mp'), may hold values from -4 to 4
- out_weight: bfloat16 [2, 768, 768], P(None, 'mp'), may hold values from -0.4375 to 0.4375
- out_bias: bfloat16 [2, 768], replicated, may hold values from -1.5 to 1.5
- norm_gain: bfloat16 [2, 2, 768], replicated, may hold values from 0.5 to 1.5
- norm_bias: bfloat16 [2, 2, 768], replicated, may hold values from -1.5 to 1.5
- up_matrix: bfloat16 [2, 768, 3072], P(None, None, 'mp'), may hold values from -0.21875 to 0.21875
- up_bias: bfloat16 [2, 3072], P(None, 'mp'), may hold values from -4 to 4
- down_matrix: bfloat16 [2, 3072, 768], P(None, 'mp'), may hold values from -0.109375 to 0.109375
- down_bias: bfloat16 [2, 768], replicated, may hold values from -1.5 to 1.5
Outputs:
- loss: float32 [], replicated
- query_grad: float32 [64, 128, 768], P(('dp', 'mp'))
- passage_grad: float32 [32, 512, 768], P(('dp', 'mp'))
- qkv_weight_grad: float32 [2, 3, 768, 768], P(None, None, None, 'mp')
- qv_bias_grad: float32 [2, 2, 768], P(None, None, 'mp')
- out_weight_grad: float32 [2, 768, 768], P(None, 'mp')
- out_bias_grad: float32 [2, 768], replicated
- norm_gain_grad: float32 [2, 2, 768], replicated
- norm_bias_grad: float32 [2, 2, 768], replicated
- up_weight_grad: float32 [2, 768, 3072], P(None, None, 'mp')
- up_bias_grad: float32 [2, 3072], P(None, 'mp')
- down_weight_grad: float32 [2, 3072, 768], P(None, 'mp')
- down_bias_grad: float32 [2, 768], replicated
Inputs may be any that keep to these rules, and one draw needn't show every extreme that they name: `query_count`: live queries of each device are its first slots; some device has 2. `passage_count`: live passages of each device are its first slots; the last device has 1. Each index names a live passage; some query's positive is the last passage. `query_lengths`: valid tokens come first; some query has all 128. `passage_lengths`: valid tokens come first; some passage has all 512.
All inputs are finite; a program needn't handle non-finite values.
Results may differ from a plain program's by a relative error of at most 0.017.
Values may be sent and summed in bfloat16 or wider, within the bound.
A program may use at most 256 MiB of HBM per device.

v0:
```python
import math

import jax
import jax.numpy as jnp
from jax import lax
from jax.sharding import PartitionSpec as P

HEAD_DIM = 64
LAYERS = 2


EPS_NORM = 1e-12
INV_TEMP = 50.0
PRECISE_MODE = lax.Precision.HIGHEST
NEG_FILL = -1e30
RSQRT_TWO = 1.0 / math.sqrt(2.0)
RSQRT_TWOPI = 1.0 / math.sqrt(2.0 * math.pi)


def norm_forward(summed, gain, bias):
    average = jnp.mean(summed, axis=-1, keepdims=True)
    centered = summed - average
    inv_std = lax.rsqrt(jnp.mean(centered * centered, axis=-1, keepdims=True) + EPS_NORM)
    normed = centered * inv_std
    return (normed * gain + bias, normed, inv_std)


def norm_backward(grad_out, normed, inv_std, gain):
    grad_normed = grad_out * gain
    grad_in = inv_std * (
        grad_normed
        - jnp.mean(grad_normed, axis=-1, keepdims=True)
        - normed * jnp.mean(grad_normed * normed, axis=-1, keepdims=True)
    )
    return (grad_in, jnp.sum(grad_out * normed, axis=(0, 1)), jnp.sum(grad_out, axis=(0, 1)))


def gelu_value(inner_rows):
    return 0.5 * inner_rows * (1.0 + jax.scipy.special.erf(inner_rows * RSQRT_TWO))


def gelu_slope(inner_rows):
    return (
        0.5 * (1.0 + jax.scipy.special.erf(inner_rows * RSQRT_TWO))
        + inner_rows * jnp.exp(-0.5 * inner_rows * inner_rows) * RSQRT_TWOPI
    )


def key_mask(lengths, seq_len):
    return (jnp.arange(seq_len, dtype=jnp.int32)[None, :] < lengths[:, None])[:, None, None, :]


def attention_scores(query_rows, incoming_keys, lengths):
    scores = jnp.einsum(
        "sqhe,skhe->shqk", query_rows, incoming_keys, preferred_element_type=jnp.float32
    ) * HEAD_DIM ** (-0.5)
    return jnp.where(key_mask(lengths, query_rows.shape[1]), scores, NEG_FILL)


def attention_forward(query_rows, incoming_keys, incoming_values, lengths):
    scores = attention_scores(query_rows, incoming_keys, lengths)
    top_score = jnp.max(scores, axis=-1, keepdims=True)
    expo = jnp.exp(scores - top_score)
    total = jnp.sum(expo, axis=-1, keepdims=True)
    probs = (expo / total).astype(jnp.bfloat16)
    attended_values = jnp.einsum(
        "shqk,skhe->sqhe", probs, incoming_values, preferred_element_type=jnp.float32
    ).astype(jnp.bfloat16)
    return (attended_values, top_score + jnp.log(total))


def attention_backward(
    query_rows, incoming_keys, incoming_values, lengths, log_total, grad_context
):
    scale_factor = HEAD_DIM ** (-0.5)
    probs = jnp.exp(attention_scores(query_rows, incoming_keys, lengths) - log_total)
    grad_values = jnp.einsum(
        "shqk,sqhe->skhe",
        probs.astype(jnp.bfloat16),
        grad_context,
        preferred_element_type=jnp.float32,
    ).astype(jnp.bfloat16)
    grad_probs = jnp.einsum(
        "sqhe,skhe->shqk", grad_context, incoming_values, preferred_element_type=jnp.float32
    )
    grad_scores = (
        probs * (grad_probs - jnp.sum(probs * grad_probs, axis=-1, keepdims=True))
    ).astype(jnp.bfloat16)
    grad_queries = (
        jnp.einsum(
            "shqk,skhe->sqhe", grad_scores, incoming_keys, preferred_element_type=jnp.float32
        )
        * scale_factor
    ).astype(jnp.bfloat16)
    grad_keys = (
        jnp.einsum("shqk,sqhe->skhe", grad_scores, query_rows, preferred_element_type=jnp.float32)
        * scale_factor
    ).astype(jnp.bfloat16)
    return (grad_queries, grad_keys, grad_values)


def gather_rows(pair):
    return (
        lax.all_gather(pair[0], "mp", axis=0, tiled=True),
        lax.all_gather(pair[1], "mp", axis=0, tiled=True),
    )


def sum_rows(pair):
    return (
        lax.psum_scatter(pair[0], "mp", scatter_dimension=0, tiled=True),
        lax.psum_scatter(pair[1], "mp", scatter_dimension=0, tiled=True),
    )


def gather_grads(pair):
    return (
        lax.all_gather(pair[0], "mp", axis=0, tiled=True),
        lax.all_gather(pair[1], "mp", axis=0, tiled=True),
    )


def sum_grads(pair):
    return (
        lax.psum_scatter(
            pair[0].astype(jnp.bfloat16), "mp", scatter_dimension=0, tiled=True
        ).astype(jnp.float32),
        lax.psum_scatter(
            pair[1].astype(jnp.bfloat16), "mp", scatter_dimension=0, tiled=True
        ).astype(jnp.float32),
    )


def layer_forward(layer_number, states, group_lengths, params):
    (
        query_key_value_matrix,
        qv_bias,
        out_weight,
        out_bias,
        norm_gain,
        norm_bias,
        up_matrix,
        up_bias,
        down_matrix,
        down_bias,
    ) = params
    rows_in = gather_rows((states[0].astype(jnp.bfloat16), states[1].astype(jnp.bfloat16)))
    attn_saved = []
    partials = []
    for length_bucket in range(2):
        collected_rows = rows_in[length_bucket]
        num_seqs, seq_len, width = collected_rows.shape
        head_shape = (num_seqs, seq_len, query_key_value_matrix.shape[-1] // HEAD_DIM, HEAD_DIM)
        projected = jnp.einsum(
            "yxr,urg->uyxg",
            collected_rows,
            query_key_value_matrix[layer_number],
            preferred_element_type=jnp.float32,
        )
        query_rows = (
            (projected[0] + qv_bias[layer_number, 0]).astype(jnp.bfloat16).reshape(head_shape)
        )
        incoming_keys = projected[1].astype(jnp.bfloat16).reshape(head_shape)
        incoming_values = (
            (projected[2] + qv_bias[layer_number, 1]).astype(jnp.bfloat16).reshape(head_shape)
        )
        attended_values, log_total = attention_forward(
            query_rows, incoming_keys, incoming_values, group_lengths[length_bucket]
        )
        attended_flat = attended_values.reshape(num_seqs, seq_len, -1)
        partials.append(
            jnp.einsum(
                "yhe,eu->yhu",
                attended_flat,
                out_weight[layer_number],
                preferred_element_type=jnp.float32,
            )
        )
        attn_saved.append(
            (collected_rows, query_rows, incoming_keys, incoming_values, log_total, attended_flat)
        )
    branch = sum_rows((partials[0], partials[1]))
    hidden_list = []
    norm_first = []
    for length_bucket in range(2):
        hidden_rows, normed, inv_std = norm_forward(
            states[length_bucket] + branch[length_bucket] + out_bias[layer_number],
            norm_gain[layer_number, 0],
            norm_bias[layer_number, 0],
        )
        hidden_list.append(hidden_rows)
        norm_first.append((normed, inv_std))
    middle_rows = gather_rows(
        (hidden_list[0].astype(jnp.bfloat16), hidden_list[1].astype(jnp.bfloat16))
    )
    inner_list = []
    partials = []
    for length_bucket in range(2):
        inner_rows = (
            jnp.einsum(
                "igy,yv->igv",
                middle_rows[length_bucket],
                up_matrix[layer_number],
                preferred_element_type=jnp.float32,
            )
            + up_bias[layer_number]
        )
        activated_rows = gelu_value(inner_rows).astype(jnp.bfloat16)
        partials.append(
            jnp.einsum(
                "cka,ax->ckx",
                activated_rows,
                down_matrix[layer_number],
                preferred_element_type=jnp.float32,
            )
        )
        inner_list.append(inner_rows)
    ffn = sum_rows((partials[0], partials[1]))
    outputs = []
    norm_second = []
    for length_bucket in range(2):
        result, normed, inv_std = norm_forward(
            hidden_list[length_bucket] + ffn[length_bucket] + down_bias[layer_number],
            norm_gain[layer_number, 1],
            norm_bias[layer_number, 1],
        )
        outputs.append(result)
        norm_second.append((normed, inv_std))
    return (outputs, (attn_saved, norm_first, middle_rows, inner_list, norm_second))


def layer_backward(layer_number, grad_states, saved, group_lengths, params):
    (
        query_key_value_matrix,
        qv_bias,
        out_weight,
        out_bias,
        norm_gain,
        norm_bias,
        up_matrix,
        up_bias,
        down_matrix,
        down_bias,
    ) = params
    attn_saved, norm_first, middle_rows, inner_list, norm_second = saved
    grad_two = []
    gain_two = 0.0
    bias_two = 0.0
    down_b_grad = 0.0
    for length_bucket in range(2):
        grad_sum, gain_part, bias_part = norm_backward(
            grad_states[length_bucket],
            norm_second[length_bucket][0],
            norm_second[length_bucket][1],
            norm_gain[layer_number, 1],
        )
        grad_two.append(grad_sum)
        gain_two = gain_two + gain_part
        bias_two = bias_two + bias_part
    low_two = (grad_two[0].astype(jnp.bfloat16), grad_two[1].astype(jnp.bfloat16))
    for length_bucket in range(2):
        down_b_grad = down_b_grad + jnp.sum(low_two[length_bucket], axis=(0, 1), dtype=jnp.float32)
    feedforward_gradients = gather_grads(low_two)
    down_w_grad = 0.0
    up_w_grad = 0.0
    up_b_grad = 0.0
    partials = []
    for length_bucket in range(2):
        inner_rows = inner_list[length_bucket]
        activated_rows = gelu_value(inner_rows).astype(jnp.bfloat16)
        down_w_grad = down_w_grad + jnp.einsum(
            "zeo,zey->oy",
            activated_rows,
            feedforward_gradients[length_bucket],
            preferred_element_type=jnp.float32,
        )
        grad_acted = jnp.einsum(
            "kpe,ge->kpg",
            feedforward_gradients[length_bucket],
            down_matrix[layer_number],
            preferred_element_type=jnp.float32,
        )
        inner_gradient = (grad_acted * gelu_slope(inner_rows)).astype(jnp.bfloat16)
        up_b_grad = up_b_grad + jnp.sum(inner_gradient, axis=(0, 1), dtype=jnp.float32)
        up_w_grad = up_w_grad + jnp.einsum(
            "ohy,ohn->yn",
            middle_rows[length_bucket],
            inner_gradient,
            preferred_element_type=jnp.float32,
        )
        partials.append(
            jnp.einsum(
                "zme,ce->zmc",
                inner_gradient,
                up_matrix[layer_number],
                preferred_element_type=jnp.float32,
            )
        )
    back_mid = sum_grads((partials[0], partials[1]))
    grad_one = []
    gain_one = 0.0
    bias_one = 0.0
    for length_bucket in range(2):
        grad_sum, gain_part, bias_part = norm_backward(
            back_mid[length_bucket] + grad_two[length_bucket],
            norm_first[length_bucket][0],
            norm_first[length_bucket][1],
            norm_gain[layer_number, 0],
        )
        grad_one.append(grad_sum)
        gain_one = gain_one + gain_part
        bias_one = bias_one + bias_part
    low_one = (grad_one[0].astype(jnp.bfloat16), grad_one[1].astype(jnp.bfloat16))
    out_b_grad = 0.0
    for length_bucket in range(2):
        out_b_grad = out_b_grad + jnp.sum(low_one[length_bucket], axis=(0, 1), dtype=jnp.float32)
    attention_gradients = gather_grads(low_one)
    out_w_grad = 0.0
    qkv_w_grad = 0.0
    qv_b_grad = 0.0
    partials = []
    for length_bucket in range(2):
        collected_rows, query_rows, incoming_keys, incoming_values, log_total, attended_flat = (
            attn_saved[length_bucket]
        )
        num_seqs, seq_len, width = collected_rows.shape
        out_w_grad = out_w_grad + jnp.einsum(
            "oar,oax->rx",
            attended_flat,
            attention_gradients[length_bucket],
            preferred_element_type=jnp.float32,
        )
        grad_context = (
            jnp.einsum(
                "nuq,tq->nut",
                attention_gradients[length_bucket],
                out_weight[layer_number],
                preferred_element_type=jnp.float32,
            )
            .astype(jnp.bfloat16)
            .reshape(query_rows.shape)
        )
        grad_queries, grad_keys, grad_values = attention_backward(
            query_rows,
            incoming_keys,
            incoming_values,
            group_lengths[length_bucket],
            log_total,
            grad_context,
        )
        stacked_rows = jnp.stack([grad_queries, grad_keys, grad_values]).reshape(
            3, num_seqs, seq_len, -1
        )
        qkv_w_grad = qkv_w_grad + jnp.einsum(
            "bak,gbah->gkh", collected_rows, stacked_rows, preferred_element_type=jnp.float32
        )
        qv_b_grad = qv_b_grad + jnp.stack(
            [
                jnp.sum(stacked_rows[0], axis=(0, 1), dtype=jnp.float32),
                jnp.sum(stacked_rows[2], axis=(0, 1), dtype=jnp.float32),
            ]
        )
        partials.append(
            jnp.einsum(
                "keux,knx->eun",
                stacked_rows,
                query_key_value_matrix[layer_number],
                preferred_element_type=jnp.float32,
            )
        )
    back_in = sum_grads((partials[0], partials[1]))
    grad_inputs = [back_in[0] + grad_one[0], back_in[1] + grad_one[1]]
    sharded = (qkv_w_grad, qv_b_grad, out_w_grad, up_w_grad, up_b_grad, down_w_grad)
    shared = (
        out_b_grad,
        jnp.stack([gain_one, gain_two]),
        jnp.stack([bias_one, bias_two]),
        down_b_grad,
    )
    return (grad_inputs, sharded, shared)


def local(
    query_states,
    passage_states,
    query_lengths,
    passage_lengths,
    query_count,
    passage_count,
    positive,
    query_key_value_matrix,
    qv_bias,
    out_weight,
    out_bias,
    norm_gain,
    norm_bias,
    up_matrix,
    up_bias,
    down_matrix,
    down_bias,
):
    params = (
        query_key_value_matrix,
        qv_bias,
        out_weight,
        out_bias,
        norm_gain.astype(jnp.float32),
        norm_bias.astype(jnp.float32),
        up_matrix,
        up_bias.astype(jnp.float32),
        down_matrix,
        down_bias.astype(jnp.float32),
    )
    params = (
        params[0],
        qv_bias.astype(jnp.float32),
        params[2],
        out_bias.astype(jnp.float32),
        params[4],
        params[5],
        params[6],
        params[7],
        params[8],
        params[9],
    )
    mp_rank = lax.axis_index("mp")
    my_rank = lax.axis_index(("dp", "mp"))
    query_slots, query_len, width = query_states.shape
    pass_slots = passage_states.shape[0]
    group_lengths = (query_lengths, passage_lengths)
    local_lengths = (
        lax.dynamic_slice_in_dim(query_lengths, mp_rank * query_slots, query_slots),
        lax.dynamic_slice_in_dim(passage_lengths, mp_rank * pass_slots, pass_slots),
    )
    states = [query_states.astype(jnp.float32), passage_states.astype(jnp.float32)]
    kept = []
    for layer_number in range(LAYERS):
        states, saved = layer_forward(layer_number, states, group_lengths, params)
        kept.append(saved)
    token_masks = []
    normed_list = []
    inv_list = []
    for length_bucket in range(2):
        seq_len = states[length_bucket].shape[1]
        live_tok = (
            jnp.arange(seq_len, dtype=jnp.int32)[None, :] < local_lengths[length_bucket][:, None]
        ).astype(jnp.float32) / local_lengths[length_bucket][:, None].astype(jnp.float32)
        pooled = jnp.sum(states[length_bucket] * live_tok[:, :, None], axis=1)
        inv_norm = lax.rsqrt(jnp.sum(pooled * pooled, axis=-1, keepdims=True) + 1e-06)
        token_masks.append(live_tok)
        normed_list.append(pooled * inv_norm)
        inv_list.append(inv_norm)
    query_norm = normed_list[0]
    pass_all = lax.all_gather(normed_list[1], ("dp", "mp"), axis=0, tiled=True)
    num_pass = pass_all.shape[0]
    sims = INV_TEMP * jnp.dot(query_norm, pass_all.T, precision=PRECISE_MODE)
    pass_ids = jnp.arange(num_pass, dtype=jnp.int32)
    live_pass = pass_ids % pass_slots < passage_count[pass_ids // pass_slots]
    masked = jnp.where(live_pass[None, :], sims, NEG_FILL)
    top_score = jnp.max(masked, axis=1, keepdims=True)
    expo = jnp.exp(masked - top_score)
    total = jnp.sum(expo, axis=1, keepdims=True)
    log_total = top_score[:, 0] + jnp.log(total[:, 0])
    is_positive = (pass_ids[None, :] == positive[:, None]).astype(jnp.float32)
    pos_score = jnp.sum(is_positive * sims, axis=1)
    live_query = (jnp.arange(query_slots, dtype=jnp.int32) < query_count[my_rank]).astype(
        jnp.float32
    )
    live_total = jnp.sum(query_count).astype(jnp.float32)
    local_loss = jnp.sum(live_query * (log_total - pos_score))
    grad_scale = float(query_slots * lax.axis_size("dp") * lax.axis_size("mp") * query_len)
    grad_sims = (grad_scale * live_query / live_total)[:, None] * (expo / total - is_positive)
    grad_qnorm = INV_TEMP * jnp.dot(grad_sims, pass_all, precision=PRECISE_MODE)
    grad_pnorm = lax.psum_scatter(
        INV_TEMP * jnp.dot(grad_sims.T, query_norm, precision=PRECISE_MODE),
        ("dp", "mp"),
        scatter_dimension=0,
        tiled=True,
    )
    grad_states = []
    for length_bucket, grad_norm in enumerate((grad_qnorm, grad_pnorm)):
        normed = normed_list[length_bucket]
        grad_pooled = inv_list[length_bucket] * (
            grad_norm - normed * jnp.sum(normed * grad_norm, axis=-1, keepdims=True)
        )
        grad_states.append(token_masks[length_bucket][:, :, None] * grad_pooled[:, None, :])
    sharded_list = [None] * LAYERS
    shared_list = [None] * LAYERS
    total_loss = 0.0
    for layer_number in reversed(range(LAYERS)):
        grad_states, sharded, shared = layer_backward(
            layer_number, grad_states, kept[layer_number], group_lengths, params
        )
        sharded_list[layer_number] = sharded
        shared_list[layer_number] = shared
    local_sharded = [
        jnp.stack([sharded_list[idx][member] for idx in range(LAYERS)]) for member in range(6)
    ]
    local_shared = [
        jnp.stack([shared_list[idx][member] for idx in range(LAYERS)]) for member in range(4)
    ]
    stacked_sharded = lax.psum(
        (
            local_sharded[0],
            local_sharded[1],
            local_sharded[2],
            local_sharded[3],
            local_sharded[4],
            local_sharded[5],
        ),
        "dp",
    )
    summed_shared = lax.psum(
        (local_shared[0], local_shared[1], local_shared[2], local_shared[3], local_loss),
        ("dp", "mp"),
    )
    stacked_shared = summed_shared[:4]
    total_loss = summed_shared[4]
    loss = total_loss / live_total
    return (
        loss,
        grad_states[0],
        grad_states[1],
        stacked_sharded[0],
        stacked_sharded[1],
        stacked_sharded[2],
        stacked_shared[0],
        stacked_shared[1],
        stacked_shared[2],
        stacked_sharded[3],
        stacked_sharded[4],
        stacked_sharded[5],
        stacked_shared[3],
    )


def solution(mesh):
    placed = (
        P(("dp", "mp"), None, None),
        P(("dp", "mp"), None, None),
        P("dp"),
        P("dp"),
        P(),
        P(),
        P(("dp", "mp")),
        P(None, None, None, "mp"),
        P(None, None, "mp"),
        P(None, "mp", None),
        P(),
        P(),
        P(),
        P(None, None, "mp"),
        P(None, "mp"),
        P(None, "mp", None),
        P(),
    )
    return jax.shard_map(
        local,
        mesh=mesh,
        in_specs=placed,
        out_specs=(
            P(),
            P(("dp", "mp"), None, None),
            P(("dp", "mp"), None, None),
            P(None, None, None, "mp"),
            P(None, None, "mp"),
            P(None, "mp", None),
            P(),
            P(),
            P(),
            P(None, None, "mp"),
            P(None, "mp"),
            P(None, "mp", None),
            P(),
        ),
        check_vma=False,
    )
```

profile of v0, /device:TPU:0, one launch (start us, length us, event | category | flops | bytes accessed | tf_op | source)
XLA Modules:
  0.0 2352.8 jit_solution(17284021530161120344)
XLA Ops:
  10.3 39.1 %all-gather.19.cloned.1.call-done = bf16[8,128,768]{2,1,0:T(8,128)(2,1)} async-done(((bf16[2,128,768]{2,1,0:T(8,128)(2,1)}), bf16[8,128,768]{2,1,0:T(8,128)(2,1)}) %all-gather.19.cloned.1.call-update) | async-done | bytes 1572880 | tf_op jit(solution)/shard_map/all_gather | solution.py:104
  58.0 55.4 %all-gather.27.cloned.1.call-done = bf16[4,512,768]{2,1,0:T(8,128)(2,1)} async-done(((bf16[1,512,768]{2,1,0:T(8,128)(2,1)}), bf16[4,512,768]{2,1,0:T(8,128)(2,1)}) %all-gather.27.cloned.1.call-update) | async-done | bytes 3145744 | tf_op jit(solution)/shard_map/all_gather | solution.py:105
  135.8 39.4 %reduce-scatter.17.cloned.1.call-done = f32[2,128,768]{2,1,0:T(8,128)} async-done(((f32[8,128,768]{2,1,0:T(8,128)}), f32[2,128,768]{2,1,0:T(8,128)}) %reduce-scatter.17.cloned.1.call-update) | async-done | bytes 786448 | tf_op jit(solution)/shard_map/reduce_scatter | solution.py:111
  177.9 110.3 %reduce-scatter.25.cloned.1.call-done = f32[1,512,768]{2,1,0:T(8,128)} async-done(((f32[4,512,768]{2,1,0:T(8,128)}), f32[1,512,768]{2,1,0:T(8,128)}) %reduce-scatter.25.cloned.1.call-update) | async-done | bytes 1572880 | tf_op jit(solution)/shard_map/reduce_scatter | solution.py:112
  292.2 35.7 %all-gather.21.cloned.1.call-done = bf16[8,128,768]{2,1,0:T(8,128)(2,1)} async-done(((bf16[2,128,768]{2,1,0:T(8,128)(2,1)}), bf16[8,128,768]{2,1,0:T(8,128)(2,1)}) %all-gather.21.cloned.1.call-update) | async-done | bytes 1572880 | tf_op jit(solution)/shard_map/all_gather | solution.py:104
  327.8 5.0 multiply_convert_fusion.5
  337.2 55.0 %all-gather.29.cloned.1.call-done = bf16[4,512,768]{2,1,0:T(8,128)(2,1)} async-done(((bf16[1,512,768]{2,1,0:T(8,128)(2,1)}), bf16[4,512,768]{2,1,0:T(8,128)(2,1)}) %all-gather.29.cloned.1.call-update) | async-done | bytes 3145744 | tf_op jit(solution)/shard_map/all_gather | solution.py:105
  392.2 6.7 multiply_convert_fusion.3
  406.4 47.6 %reduce-scatter.19.cloned.1.call-done = f32[2,128,768]{2,1,0:T(8,128)} async-done(((f32[8,128,768]{2,1,0:T(8,128)}), f32[2,128,768]{2,1,0:T(8,128)}) %reduce-scatter.19.cloned.1.call-update) | async-done | bytes 786448 | tf_op jit(solution)/shard_map/reduce_scatter | solution.py:111
  457.4 109.7 %reduce-scatter.27.cloned.1.call-done = f32[1,512,768]{2,1,0:T(8,128)} async-done(((f32[4,512,768]{2,1,0:T(8,128)}), f32[1,512,768]{2,1,0:T(8,128)}) %reduce-scatter.27.cloned.1.call-update) | async-done | bytes 1572880 | tf_op jit(solution)/shard_map/reduce_scatter | solution.py:112
  571.0 36.0 %all-gather.23.cloned.1.call-done = bf16[8,128,768]{2,1,0:T(8,128)(2,1)} async-done(((bf16[2,128,768]{2,1,0:T(8,128)(2,1)}), bf16[8,128,768]{2,1,0:T(8,128)(2,1)}) %all-gather.23.cloned.1.call-update) | async-done | bytes 1572880 | tf_op jit(solution)/shard_map/all_gather | solution.py:104
  615.4 55.9 %all-gather.31.cloned.1.call-done = bf16[4,512,768]{2,1,0:T(8,128)(2,1)} async-done(((bf16[1,512,768]{2,1,0:T(8,128)(2,1)}), bf16[4,512,768]{2,1,0:T(8,128)(2,1)}) %all-gather.31.cloned.1.call-update) | async-done | bytes 3145744 | tf_op jit(solution)/shard_map/all_gather | solution.py:105
  692.1 41.1 %reduce-scatter.21.cloned.1.call-done = f32[2,128,768]{2,1,0:T(8,128)} async-done(((f32[8,128,768]{2,1,0:T(8,128)}), f32[2,128,768]{2,1,0:T(8,128)}) %reduce-scatter.21.cloned.1.call-update) | async-done | bytes 786448 | tf_op jit(solution)/shard_map/reduce_scatter | solution.py:111
  737.2 108.9 %reduce-scatter.29.cloned.1.call-done = f32[1,512,768]{2,1,0:T(8,128)} async-done(((f32[4,512,768]{2,1,0:T(8,128)}), f32[1,512,768]{2,1,0:T(8,128)}) %reduce-scatter.29.cloned.1.call-update) | async-done | bytes 1572880 | tf_op jit(solution)/shard_map/reduce_scatter | solution.py:112
  851.5 34.4 %all-gather.25.cloned.1.call-done = bf16[8,128,768]{2,1,0:T(8,128)(2,1)} async-done(((bf16[2,128,768]{2,1,0:T(8,128)(2,1)}), bf16[8,128,768]{2,1,0:T(8,128)(2,1)}) %all-gather.25.cloned.1.call-update) | async-done | bytes 1572880 | tf_op jit(solution)/shard_map/all_gather | solution.py:104
  885.9 5.1 multiply_convert_fusion.4
  895.3 55.0 %all-gather.33.cloned.1.call-done = bf16[4,512,768]{2,1,0:T(8,128)(2,1)} async-done(((bf16[1,512,768]{2,1,0:T(8,128)(2,1)}), bf16[4,512,768]{2,1,0:T(8,128)(2,1)}) %all-gather.33.cloned.1.call-update) | async-done | bytes 3145744 | tf_op jit(solution)/shard_map/all_gather | solution.py:105
  950.3 6.8 multiply_convert_fusion.2
  958.7 4.5 fusion.103
  975.3 36.6 %reduce-scatter.23.cloned.1.call-done = f32[2,128,768]{2,1,0:T(8,128)} async-done(((f32[8,128,768]{2,1,0:T(8,128)}), f32[2,128,768]{2,1,0:T(8,128)}) %reduce-scatter.23.cloned.1.call-update) | async-done | bytes 786448 | tf_op jit(solution)/shard_map/reduce_scatter | solution.py:111
  1016.1 108.8 %reduce-scatter.31.cloned.1.call-done = f32[1,512,768]{2,1,0:T(8,128)} async-done(((f32[4,512,768]{2,1,0:T(8,128)}), f32[1,512,768]{2,1,0:T(8,128)}) %reduce-scatter.31.cloned.1.call-update) | async-done | bytes 1572880 | tf_op jit(solution)/shard_map/reduce_scatter | solution.py:112
  1131.9 68.2 %all-gather.1 = f32[32,1,768]{2,1,0:T(1,128)S(1)} all-gather(f32[1,1,768]{2,1,0:T(1,128)S(1)} %reshape.1152), channel_id=2, replica_groups=mesh['dp'=8,'mp'=4] {'dp','mp'}, dimensions={0}, use_global_device_ids=true | all-gather | bytes 101376 | tf_op jit(solution)/shard_map/all_gather | solution.py:454
  1214.1 114.1 %all-reduce.7.cloned.1.call-done = f32[32,768]{1,0:T(8,128)} async-done(((f32[32,768]{1,0:T(8,128)}), f32[32,768]{1,0:T(8,128)}) %all-reduce.7.cloned.1.call-update) | async-done | bytes 98320
  1337.1 31.0 %all-gather.35.cloned.1.call-done = bf16[8,128,768]{2,1,0:T(8,128)(2,1)} async-done(((bf16[2,128,768]{2,1,0:T(8,128)(2,1)}), bf16[8,128,768]{2,1,0:T(8,128)(2,1)}) %all-gather.35.cloned.1.call-update) | async-done | bytes 1572880 | tf_op jit(solution)/shard_map/all_gather | solution.py:118
  1368.1 5.6 convert_reduce_fusion.2
  1377.5 55.1 %all-gather.43.cloned.1.call-done = bf16[4,512,768]{2,1,0:T(8,128)(2,1)} async-done(((bf16[1,512,768]{2,1,0:T(8,128)(2,1)}), bf16[4,512,768]{2,1,0:T(8,128)(2,1)}) %all-gather.43.cloned.1.call-update) | async-done | bytes 3145744 | tf_op jit(solution)/shard_map/all_gather | solution.py:119
  1432.6 7.7 convert_reduce_fusion
  1446.0 23.3 reduce-scatter.33.cloned.1.call-done
  1474.7 56.8 %reduce-scatter.41.cloned.1.call-done = bf16[1,512,768]{2,1,0:T(8,128)(2,1)} async-done(((bf16[4,512,768]{2,1,0:T(8,128)(2,1)}), bf16[1,512,768]{2,1,0:T(8,128)(2,1)}) %reduce-scatter.41.cloned.1.call-update) | async-done | bytes 786448 | tf_op jit(solution)/shard_map/reduce_scatter | solution.py:128
  1541.1 29.1 %all-gather.37.cloned.1.call-done = bf16[8,128,768]{2,1,0:T(8,128)(2,1)} async-done(((bf16[2,128,768]{2,1,0:T(8,128)(2,1)}), bf16[8,128,768]{2,1,0:T(8,128)(2,1)}) %all-gather.37.cloned.1.call-update) | async-done | bytes 1572880 | tf_op jit(solution)/shard_map/all_gather | solution.py:118
  1580.2 54.5 %all-gather.45.cloned.1.call-done = bf16[4,512,768]{2,1,0:T(8,128)(2,1)} async-done(((bf16[1,512,768]{2,1,0:T(8,128)(2,1)}), bf16[4,512,768]{2,1,0:T(8,128)(2,1)}) %all-gather.45.cloned.1.call-update) | async-done | bytes 3145744 | tf_op jit(solution)/shard_map/all_gather | solution.py:119
  1637.9 11.7 multiply_reduce_fusion.1
  1649.6 7.2 multiply_convert_fusion.1
  1676.7 56.3 %reduce-scatter.43.cloned.1.call-done = bf16[1,512,768]{2,1,0:T(8,128)(2,1)} async-done(((bf16[4,512,768]{2,1,0:T(8,128)(2,1)}), bf16[1,512,768]{2,1,0:T(8,128)(2,1)}) %reduce-scatter.43.cloned.1.call-update) | async-done | bytes 786448 | tf_op jit(solution)/shard_map/reduce_scatter | solution.py:128
  1739.1 32.5 %all-gather.39.cloned.1.call-done = bf16[8,128,768]{2,1,0:T(8,128)(2,1)} async-done(((bf16[2,128,768]{2,1,0:T(8,128)(2,1)}), bf16[8,128,768]{2,1,0:T(8,128)(2,1)}) %all-gather.39.cloned.1.call-update) | async-done | bytes 1572880 | tf_op jit(solution)/shard_map/all_gather | solution.py:118
  1771.6 5.6 convert_reduce_fusion.3
  1781.0 55.0 %all-gather.47.cloned.1.call-done = bf16[4,512,768]{2,1,0:T(8,128)(2,1)} async-done(((bf16[1,512,768]{2,1,0:T(8,128)(2,1)}), bf16[4,512,768]{2,1,0:T(8,128)(2,1)}) %all-gather.47.cloned.1.call-update) | async-done | bytes 3145744 | tf_op jit(solution)/shard_map/all_gather | solution.py:119
  1836.0 7.8 convert_reduce_fusion.1
  1849.6 23.2 reduce-scatter.37.cloned.1.call-done
  1876.9 58.1 %reduce-scatter.45.cloned.1.call-done = bf16[1,512,768]{2,1,0:T(8,128)(2,1)} async-done(((bf16[4,512,768]{2,1,0:T(8,128)(2,1)}), bf16[1,512,768]{2,1,0:T(8,128)(2,1)}) %reduce-scatter.45.cloned.1.call-update) | async-done | bytes 786448 | tf_op jit(solution)/shard_map/reduce_scatter | solution.py:128
  1952.9 21.2 all-gather.41.cloned.1.call-done
  1984.8 53.8 %all-gather.49.cloned.1.call-done = bf16[4,512,768]{2,1,0:T(8,128)(2,1)} async-done(((bf16[1,512,768]{2,1,0:T(8,128)(2,1)}), bf16[4,512,768]{2,1,0:T(8,128)(2,1)}) %all-gather.49.cloned.1.call-update) | async-done | bytes 3145744 | tf_op jit(solution)/shard_map/all_gather | solution.py:119
  2041.7 11.8 multiply_reduce_fusion
  2053.5 7.2 multiply_convert_fusion
  2074.0 6.5 fusion.51
  2123.9 40.7 %all-reduce.1 = (f32[]{:T(128)}, f32[2,768]{1,0:T(2,128)}, f32[2,2,768]{2,1,0:T(2,128)}, f32[2,2,768]{2,1,0:T(2,128)}, f32[2,768]{1,0:T(2,128)}) all-reduce(f32[]{:T(128)} %fusion.208, f32[2,768]{1,0:T(2,128)S(1)} %pad_maximum_fusion.18, f32[2,2,768]{2,1,0:T(2,128)S(1)} %pad_maximum_fusion.16, ...), channel_id=1, replica_groups=mesh['dp'=8,'mp'=4] {'dp','mp'}, use_global_device_ids=true, to_apply=%region_40.41 | all-reduce | flops 9217 | bytes 73736 | tf_op jit(solution)/shard_map/psum | solution.py:513
  2165.4 24.6 %all-reduce.2 = (f32[2,2,192]{2,1,0:T(2,128)}, f32[2,768]{1,0:T(2,128)}) all-reduce(f32[2,2,192]{2,1,0:T(2,128)S(1)} %pad_maximum_fusion.21, f32[2,768]{1,0:T(2,128)S(1)} %pad_maximum_fusion.19), channel_id=1, replica_groups=mesh['dp'=8,'mp'=4] {'dp'}, use_global_device_ids=true, to_apply=%region_82.83 | all-reduce | flops 2304 | bytes 18432 | tf_op jit(solution)/shard_map/psum | solution.py:502
  2192.5 140.7 %all-reduce.9.cloned.1.call-done = (f32[2,3,768,192]{2,3,1,0:T(8,128)}, f32[2,192,768]{2,1,0:T(8,128)}, f32[2,768,768]{2,1,0:T(8,128)}, f32[2,768,768]{2,1,0:T(8,128)}) async-done(((f32[2,3,768,192]{2,3,1,0:T(8,128)}, f32[2,192,768]{2,1,0:T(8,128)}, f32[2,768,768]{2,1,0:T(8,128)}, f32[2,768,768]{2,1,0:T(8,128)}), (f32[2,3,768,192]{2,3,1,0:T(8,128)}, f32[2,192,768]{2,1,0:T(8,128)}, f32[2,768,768]{2,1,0:T(8,128)}, ...) | async-done | bytes 14155792 | tf_op jit(solution)/shard_map/psum | solution.py:502
  (839 shorter events, 324.9 us)
Async XLA Ops:
  7.2 962.0 %copy-start = (s32[32]{0:T(128)S(1)}, s32[32]{0:T(128)}, u32[]{:S(2)}) copy-start(s32[32]{0:T(128)} %param.22) | copy-start | bytes 388
  7.2 42.2 %all-gather.19.cloned.1.call-start = ((), (), s32[]{:S(2)}) async-start(), calls=%async_computation.16 | async-start | bytes 1966080 | tf_op jit(solution)/shard_map/all_gather | solution.py:104
  7.9 105.5 %all-gather.27.cloned.1.call-start = ((), (), s32[]{:S(2)}) async-start(), calls=%async_computation.24 | async-start | bytes 3932160 | tf_op jit(solution)/shard_map/all_gather | solution.py:105
  8.7 166.5 %reduce-scatter.17.cloned.1.call-start = ((), (), s32[]{:S(2)}) async-start(), calls=%async_computation.17 | async-start | bytes 3932160 | tf_op jit(solution)/shard_map/reduce_scatter | solution.py:111
  9.6 115.2 %copy-start.152 = (f32[3,64]{1,0:T(4,128)}, f32[3,64]{1,0:T(4,128)S(1)}, u32[]{:S(2)}) copy-start(f32[3,64]{1,0:T(4,128)S(1)} %add.762) | copy-start | bytes 2308
  57.3 230.9 %reduce-scatter.25.cloned.1.call-start = ((), (), s32[]{:S(2)}) async-start(), calls=%async_computation.25 | async-start | bytes 7864320 | tf_op jit(solution)/shard_map/reduce_scatter | solution.py:112
  133.9 194.0 %all-gather.21.cloned.1.call-start = ((), (), s32[]{:S(2)}) async-start(), calls=%async_computation.18 | async-start | bytes 1966080 | tf_op jit(solution)/shard_map/all_gather | solution.py:104
  135.8 431.3 %copy-start.84 = (f32[768]{0:T(1024)}, f32[768]{0:T(1024)S(1)}, u32[]{:S(2)}) copy-start(f32[768]{0:T(1024)S(1)} %get-tuple-element.177) | copy-start | bytes 9220
  135.8 433.7 %copy-start.110 = (f32[768]{0:T(1024)}, f32[768]{0:T(1024)S(1)}, u32[]{:S(2)}) copy-start(f32[768]{0:T(1024)S(1)} %get-tuple-element.47) | copy-start | bytes 9220
  175.2 113.0 %copy-start.55 = (bf16[1,512,768]{2,1,0:T(8,128)(2,1)S(1)}, bf16[1,512,768]{2,1,0:T(8,128)(2,1)}, u32[]{:S(2)}) copy-start(bf16[1,512,768]{2,1,0:T(8,128)(2,1)} %param.18) | copy-start | bytes 2359300
  176.6 277.4 %copy-start.15 = (f32[2,128,768]{2,1,0:T(8,128)}, f32[2,128,768]{2,1,0:T(8,128)S(1)}, u32[]{:S(2)}) copy-start(f32[2,128,768]{2,1,0:T(8,128)S(1)} %get-tuple-element.108) | copy-start | bytes 2359300
  176.6 277.4 %copy-start.135 = (f32[2,128]{1,0:T(2,128)}, f32[2,128]{1,0:T(2,128)S(1)}, u32[]{:S(2)}) copy-start(f32[2,128]{1,0:T(2,128)S(1)} %broadcast_multiply_fusion.25) | copy-start | bytes 3076
  176.9 277.2 %copy-start.141 = (f32[2,128]{1,0:T(2,128)}, f32[2,128]{1,0:T(2,128)S(1)}, u32[]{:S(2)}) copy-start(f32[2,128]{1,0:T(2,128)S(1)} %add_rsqrt_fusion.7) | copy-start | bytes 3076
  177.9 214.3 %all-gather.29.cloned.1.call-start = ((), (), s32[]{:S(2)}) async-start(), calls=%async_computation.26 | async-start | bytes 3932160 | tf_op jit(solution)/shard_map/all_gather | solution.py:105
  289.9 277.2 %copy-start.4 = (f32[1,512,768]{2,1,0:T(8,128)}, f32[1,512,768]{2,1,0:T(8,128)S(1)}, u32[]{:S(2)}) copy-start(f32[1,512,768]{2,1,0:T(8,128)S(1)} %get-tuple-element.116) | copy-start | bytes 4718596
  289.9 277.2 %copy-start.113 = (f32[512]{0:T(512)}, f32[512]{0:T(512)S(1)}, u32[]{:S(2)}) copy-start(f32[512]{0:T(512)S(1)} %broadcast_multiply_fusion.13) | copy-start | bytes 6148
  290.3 276.9 %copy-start.128 = (f32[512]{0:T(512)}, f32[512]{0:T(512)S(1)}, u32[]{:S(2)}) copy-start(f32[512]{0:T(512)S(1)} %add_rsqrt_fusion.3) | copy-start | bytes 6148
  291.5 162.6 %reduce-scatter.19.cloned.1.call-start = ((), (), s32[]{:S(2)}) async-start(), calls=%async_computation.19 | async-start | bytes 3932160 | tf_op jit(solution)/shard_map/reduce_scatter | solution.py:111
  337.1 230.0 %reduce-scatter.27.cloned.1.call-start = ((), (), s32[]{:S(2)}) async-start(), calls=%async_computation.27 | async-start | bytes 7864320 | tf_op jit(solution)/shard_map/reduce_scatter | solution.py:112
  405.1 201.8 %all-gather.23.cloned.1.call-start = ((), (), s32[]{:S(2)}) async-start(), calls=%async_computation.20 | async-start | bytes 1966080 | tf_op jit(solution)/shard_map/all_gather | solution.py:104
  455.5 113.6 %copy-start.137 = (f32[2,128]{1,0:T(2,128)}, f32[2,128]{1,0:T(2,128)S(1)}, u32[]{:S(2)}) copy-start(f32[2,128]{1,0:T(2,128)S(1)} %broadcast_multiply_fusion.24) | copy-start | bytes 3076
  455.8 113.4 %copy-start.144 = (f32[2,128]{1,0:T(2,128)}, f32[2,128]{1,0:T(2,128)S(1)}, u32[]{:S(2)}) copy-start(f32[2,128]{1,0:T(2,128)S(1)} %add_rsqrt_fusion.6) | copy-start | bytes 3076
  457.4 214.0 %all-gather.31.cloned.1.call-start = ((), (), s32[]{:S(2)}) async-start(), calls=%async_computation.28 | async-start | bytes 3932160 | tf_op jit(solution)/shard_map/all_gather | solution.py:105
  570.7 162.4 %reduce-scatter.21.cloned.1.call-start = ((), (), s32[]{:S(2)}) async-start(), calls=%async_computation.21 | async-start | bytes 3932160 | tf_op jit(solution)/shard_map/reduce_scatter | solution.py:111
  570.9 112.0 %copy-start.154 = (f32[3,64]{1,0:T(4,128)}, f32[3,64]{1,0:T(4,128)S(1)}, u32[]{:S(2)}) copy-start(f32[3,64]{1,0:T(4,128)S(1)} %add.788) | copy-start | bytes 2308
  615.2 230.9 %reduce-scatter.29.cloned.1.call-start = ((), (), s32[]{:S(2)}) async-start(), calls=%async_computation.29 | async-start | bytes 7864320 | tf_op jit(solution)/shard_map/reduce_scatter | solution.py:112
  692.0 193.9 %all-gather.25.cloned.1.call-start = ((), (), s32[]{:S(2)}) async-start(), calls=%async_computation.22 | async-start | bytes 1966080 | tf_op jit(solution)/shard_map/all_gather | solution.py:104
  737.2 213.2 %all-gather.33.cloned.1.call-start = ((), (), s32[]{:S(2)}) async-start(), calls=%async_computation.30 | async-start | bytes 3932160 | tf_op jit(solution)/shard_map/all_gather | solution.py:105
  851.2 160.8 %reduce-scatter.23.cloned.1.call-start = ((), (), s32[]{:S(2)}) async-start(), calls=%async_computation.23 | async-start | bytes 3932160 | tf_op jit(solution)/shard_map/reduce_scatter | solution.py:111
  895.2 229.7 %reduce-scatter.31.cloned.1.call-start = ((), (), s32[]{:S(2)}) async-start(), calls=%async_computation.31 | async-start | bytes 7864320 | tf_op jit(solution)/shard_map/reduce_scatter | solution.py:112
  963.3 364.8 %all-reduce.7.cloned.1.call-start = ((), (), s32[]{:S(2)}) async-start(), calls=%async_computation.48 | async-start | bytes 196608
  1211.1 157.0 %all-gather.35.cloned.1.call-start = ((), (), s32[]{:S(2)}) async-start(), calls=%async_computation.32 | async-start | bytes 1966080 | tf_op jit(solution)/shard_map/all_gather | solution.py:118
  1214.0 218.6 %all-gather.43.cloned.1.call-start = ((), (), s32[]{:S(2)}) async-start(), calls=%async_computation.40 | async-start | bytes 3932160 | tf_op jit(solution)/shard_map/all_gather | solution.py:119
  1336.6 132.7 %reduce-scatter.33.cloned.1.call-start = ((), (), s32[]{:S(2)}) async-start(), calls=%async_computation.33 | async-start | bytes 1966080 | tf_op jit(solution)/shard_map/reduce_scatter | solution.py:125
  1377.4 154.0 %reduce-scatter.41.cloned.1.call-start = ((), (), s32[]{:S(2)}) async-start(), calls=%async_computation.41 | async-start | bytes 3932160 | tf_op jit(solution)/shard_map/reduce_scatter | solution.py:128
  1446.0 124.2 %all-gather.37.cloned.1.call-start = ((), (), s32[]{:S(2)}) async-start(), calls=%async_computation.34 | async-start | bytes 1966080 | tf_op jit(solution)/shard_map/all_gather | solution.py:118
  1474.6 160.1 %all-gather.45.cloned.1.call-start = ((), (), s32[]{:S(2)}) async-start(), calls=%async_computation.42 | async-start | bytes 3932160 | tf_op jit(solution)/shard_map/all_gather | solution.py:119
  1538.2 132.7 %reduce-scatter.35.cloned.1.call-start = ((), (), s32[]{:S(2)}) async-start(), calls=%async_computation.35 | async-start | bytes 1966080 | tf_op jit(solution)/shard_map/reduce_scatter | solution.py:125
  1580.0 153.0 %reduce-scatter.43.cloned.1.call-start = ((), (), s32[]{:S(2)}) async-start(), calls=%async_computation.43 | async-start | bytes 3932160 | tf_op jit(solution)/shard_map/reduce_scatter | solution.py:128
  1670.2 101.3 %all-gather.39.cloned.1.call-start = ((), (), s32[]{:S(2)}) async-start(), calls=%async_computation.36 | async-start | bytes 1966080 | tf_op jit(solution)/shard_map/all_gather | solution.py:118
  1676.7 159.3 %all-gather.47.cloned.1.call-start = ((), (), s32[]{:S(2)}) async-start(), calls=%async_computation.44 | async-start | bytes 3932160 | tf_op jit(solution)/shard_map/all_gather | solution.py:119
  1738.8 134.0 %reduce-scatter.37.cloned.1.call-start = ((), (), s32[]{:S(2)}) async-start(), calls=%async_computation.37 | async-start | bytes 1966080 | tf_op jit(solution)/shard_map/reduce_scatter | solution.py:125
  1780.9 154.0 %reduce-scatter.45.cloned.1.call-start = ((), (), s32[]{:S(2)}) async-start(), calls=%async_computation.45 | async-start | bytes 3932160 | tf_op jit(solution)/shard_map/reduce_scatter | solution.py:128
  1849.5 124.6 %all-gather.41.cloned.1.call-start = ((), (), s32[]{:S(2)}) async-start(), calls=%async_computation.38 | async-start | bytes 1966080 | tf_op jit(solution)/shard_map/all_gather | solution.py:118
  1876.8 161.8 %all-gather.49.cloned.1.call-start = ((), (), s32[]{:S(2)}) async-start(), calls=%async_computation.46 | async-start | bytes 3932160 | tf_op jit(solution)/shard_map/all_gather | solution.py:119
  1940.8 180.4 %reduce-scatter.39.cloned.1.call-start = ((), (), s32[]{:S(2)}) async-start(), calls=%async_computation.39 | async-start | bytes 1966080 | tf_op jit(solution)/shard_map/reduce_scatter | solution.py:125
  1984.6 205.4 %reduce-scatter.47.cloned.1.call-start = ((), (), s32[]{:S(2)}) async-start(), calls=%async_computation.47 | async-start | bytes 3932160 | tf_op jit(solution)/shard_map/reduce_scatter | solution.py:128
  2073.7 259.5 %all-reduce.9.cloned.1.call-start = ((), (), s32[]{:S(2)}) async-start(), calls=%async_computation.49 | async-start | bytes 28311552 | tf_op jit(solution)/shard_map/psum | solution.py:502
  (244 other events, 2310.4 us)
Sparse Core Ops, SparseCore 0:
  9.6 39.7 all-gather.18
  51.0 62.3 all-gather.26
  116.3 58.8 reduce-scatter.16
  177.4 110.7 reduce-scatter.24
  290.2 37.6 all-gather.20
  329.8 62.3 all-gather.28
  395.1 58.8 reduce-scatter.18
  456.3 110.7 reduce-scatter.26
  569.3 37.6 all-gather.22
  608.9 62.3 all-gather.30
  674.2 58.8 reduce-scatter.20
  735.3 110.7 reduce-scatter.28
  848.3 37.6 all-gather.24
  887.9 62.3 all-gather.32
  953.0 58.8 reduce-scatter.22
  1014.1 110.7 reduce-scatter.30
  1211.3 116.8 all-reduce.6
  1330.1 37.9 all-gather.34
  1370.2 62.3 all-gather.42
  1435.4 33.9 reduce-scatter.32
  1472.2 59.2 reduce-scatter.40
  1533.0 37.1 all-gather.36
  1572.3 62.3 all-gather.44
  1636.9 33.9 reduce-scatter.34
  1673.7 59.2 reduce-scatter.42
  1734.4 37.1 all-gather.38
  1773.5 62.3 all-gather.46
  1838.8 33.9 reduce-scatter.36
  1875.7 59.2 reduce-scatter.44
  1936.9 37.1 all-gather.40
  1976.2 62.3 all-gather.48
  2040.9 33.9 reduce-scatter.38
  2077.1 59.2 reduce-scatter.46
  2141.5 191.7 all-reduce.8
where the time goes:
time: 2360 us; the launch traced here: 2350 us
  waiting for transfers between devices  1780 us (75%)
  matrix products  229 us (10%)
  blocking collectives  133 us (6%)
  other arithmetic  123 us (5%)
  local copies, waits for them, and re-layouts  65.4 us (3%)
    reduce_scatter x4, waiting for transfers between devices, sum_rows(): lax.psum_scatter(pair[1], 'mp', scatter_dimension=0, tiled=True)  438 us
    all_gather x4, waiting for transfers between devices, gather_rows(): lax.all_gather(pair[1], 'mp', axis=0, tiled=True)  221 us
    all_gather x4, waiting for transfers between devices, gather_grads(): lax.all_gather(pair[1], 'mp', axis=0, tiled=True)  218 us
    reduce_scatter x4, waiting for transfers between devices, sum_grads(): lax.psum_scatter(pair[1].astype(jnp.bfloat16), 'mp', scatter_dimension=0,...  171 us
    reduce_scatter x4, waiting for transfers between devices, sum_rows(): lax.psum_scatter(pair[0], 'mp', scatter_dimension=0, tiled=True)  165 us
    all_gather x4, waiting for transfers between devices, gather_rows(): lax.all_gather(pair[0], 'mp', axis=0, tiled=True)  145 us
    psum x1, waiting for transfers between devices, local(): lax.psum((local_sharded[0], local_sharded[1], local_sharded[2], local_sha...  141 us
    unnamed x35, waiting for transfers between devices  116 us
  transfers between devices with their start and end apart: 34, of which 32 were waited for; matrix products, arithmetic and copies ran while one was open for 15% of the time, Pallas kernels for 0%

commit v1 on v0

v1 whole, which is shorter than its diff:
```python
import math

import jax
import jax.numpy as jnp
from jax import lax
from jax.sharding import PartitionSpec as P

HEAD_DIM = 64
EPS_NORM = 1e-12
INV_TEMP = 50.0
PRECISE_MODE = lax.Precision.HIGHEST
NEG_FILL = -1e30
RSQRT_TWO = 1.0 / math.sqrt(2.0)
RSQRT_TWOPI = 1.0 / math.sqrt(2.0 * math.pi)
F32 = jnp.float32
BF16 = jnp.bfloat16

CORE, XBIT, YBIT = 1, 2, 4
GROUP = 8


def flip(value, bit):
    size = lax.axis_size("dp")
    return lax.ppermute(value, "dp", [(i, i ^ bit) for i in range(size)])


def flip_mp(value, bit):
    size = lax.axis_size("mp")
    return lax.ppermute(value, "mp", [(i, i ^ bit) for i in range(size)])


def ring(value):
    size = lax.axis_size("mp")
    return lax.ppermute(value, "mp", [(i, (i + 1) % size) for i in range(size)])


def spots():
    index = lax.axis_index("dp")
    return index % 2, (index // 2) % 2, (index // 4) % 2


def swap_if(cond, first, second):
    return jnp.where(cond, second, first), jnp.where(cond, first, second)


def gather_plane(piece):
    core, px, py = spots()
    half = piece.shape[-2] // 2
    along_x = flip(piece, XBIT)
    along_y = flip(piece, YBIT)
    diag_a = flip(along_x[..., :half, :], YBIT)
    diag_b = flip(along_y[..., half:, :], XBIT)
    diag = jnp.concatenate([diag_a, diag_b], axis=-2)
    q0, q1 = swap_if(px == 1, piece, along_x)
    q2, q3 = swap_if(px == 1, along_y, diag)
    low = jnp.concatenate([q0, q1], axis=-2)
    high = jnp.concatenate([q2, q3], axis=-2)
    low, high = swap_if(py == 1, low, high)
    mine = jnp.concatenate([low, high], axis=-2)
    other = flip(mine, CORE)
    first, second = swap_if(core == 1, mine, other)
    return jnp.concatenate([first, second], axis=-2)


def gather_weights(shard):
    core, px, py = spots()
    rows = shard.shape[0] // GROUP
    mine = lax.dynamic_slice_in_dim(shard, (core * 4 + py * 2 + px) * rows, rows)
    pieces = []
    current = mine
    for _ in range(lax.axis_size("mp") - 1):
        current = ring(current)
        pieces.append(current)
    foreign = gather_plane(jnp.stack(pieces))
    return jnp.concatenate([shard[None], foreign])


def add_low(left, right):
    return (left.astype(F32) + right.astype(F32)).astype(BF16)


def pick(value, axis, index):
    return lax.dynamic_index_in_dim(value, index, axis=axis, keepdims=False)


def reduce_gradient(grad):
    core, px, py = spots()
    ways, rows, width = grad.shape
    split = width // 2
    blocks = grad.reshape(ways, 2, 2, 2, rows // GROUP, width)
    got = flip(pick(blocks, 1, 1 - core), CORE)
    blocks = add_low(pick(blocks, 1, core), got)
    left, right = blocks[..., :split], blocks[..., split:]
    got_left = flip(pick(left, 2, 1 - px), XBIT)
    got_right = flip(pick(right, 1, 1 - py), YBIT)
    left = add_low(pick(left, 2, px), got_left)
    right = add_low(pick(right, 1, py), got_right)
    got_left = flip(pick(left, 1, 1 - py), YBIT)
    got_right = flip(pick(right, 1, 1 - px), XBIT)
    left = add_low(pick(left, 1, py), got_left)
    right = add_low(pick(right, 1, px), got_right)
    block = jnp.concatenate([left, right], axis=-1)
    total = block[1]
    for step in range(2, ways + 1):
        total = add_low(ring(total), block[step % ways])
    bit = GROUP
    while bit < lax.axis_size("dp"):
        total = add_low(total, flip(total, bit))
        bit *= 2
    return gather_plane(total).astype(F32)


def gather_all(rows):
    bit = 1
    while bit < lax.axis_size("mp"):
        other = flip_mp(rows, bit)
        upper = (lax.axis_index("mp") // bit) % 2 == 1
        rows = jnp.concatenate(swap_if(upper, rows, other))
        bit *= 2
    bit = 1
    while bit < lax.axis_size("dp"):
        other = flip(rows, bit)
        upper = (lax.axis_index("dp") // bit) % 2 == 1
        rows = jnp.concatenate(swap_if(upper, rows, other))
        bit *= 2
    return rows


def sum_all(value):
    bit = 1
    while bit < lax.axis_size("dp"):
        value = value + flip(value, bit)
        bit *= 2
    bit = 1
    while bit < lax.axis_size("mp"):
        value = value + flip_mp(value, bit)
        bit *= 2
    return value


def norm_forward(summed, gain, bias):
    average = jnp.mean(summed, axis=-1, keepdims=True)
    centered = summed - average
    inv_std = lax.rsqrt(jnp.mean(centered * centered, axis=-1, keepdims=True) + EPS_NORM)
    normed = centered * inv_std
    return normed * gain + bias, normed, inv_std


def norm_backward(grad_out, normed, inv_std, gain):
    grad_normed = grad_out * gain
    grad_in = inv_std * (
        grad_normed
        - jnp.mean(grad_normed, axis=-1, keepdims=True)
        - normed * jnp.mean(grad_normed * normed, axis=-1, keepdims=True)
    )
    return grad_in, jnp.sum(grad_out * normed, axis=0), jnp.sum(grad_out, axis=0)


def gelu_value(inner):
    return 0.5 * inner * (1.0 + lax.erf(inner * RSQRT_TWO))


def gelu_slope(inner):
    return 0.5 * (1.0 + lax.erf(inner * RSQRT_TWO)) + inner * jnp.exp(
        -0.5 * inner * inner
    ) * RSQRT_TWOPI


def mm(spec, left, right):
    return jnp.einsum(spec, left, right, preferred_element_type=F32)


def scores_of(q, k, lengths):
    scores = mm("sqhe,skhe->shqk", q, k) * HEAD_DIM ** (-0.5)
    keep = jnp.arange(k.shape[1], dtype=jnp.int32)[None, :] < lengths[:, None]
    return jnp.where(keep[:, None, None, :], scores, NEG_FILL)


def attention_forward(q, k, v, lengths):
    scores = scores_of(q, k, lengths)
    top = jnp.max(scores, axis=-1, keepdims=True)
    expo = jnp.exp(scores - top)
    total = jnp.sum(expo, axis=-1, keepdims=True)
    probs = (expo / total).astype(BF16)
    return mm("shqk,skhe->sqhe", probs, v).astype(BF16), top + jnp.log(total)


def attention_backward(q, k, v, lengths, log_total, grad_context):
    scale = HEAD_DIM ** (-0.5)
    probs = jnp.exp(scores_of(q, k, lengths) - log_total)
    dv = mm("shqk,sqhe->skhe", probs.astype(BF16), grad_context).astype(BF16)
    dp = mm("sqhe,skhe->shqk", grad_context, v)
    ds = (probs * (dp - jnp.sum(probs * dp, axis=-1, keepdims=True))).astype(BF16)
    dq = (mm("shqk,skhe->sqhe", ds, k) * scale).astype(BF16)
    dk = (mm("shqk,sqhe->skhe", ds, q) * scale).astype(BF16)
    return dq, dk, dv


def buckets(rows, shapes):
    parts = []
    start = 0
    for count, length in shapes:
        stop = start + count * length
        parts.append(rows[start:stop].reshape(count, length, -1, HEAD_DIM))
        start = stop
    return parts


def unbucket(parts):
    return jnp.concatenate([part.reshape(-1, part.shape[2] * HEAD_DIM) for part in parts])


def layer_forward(x, attn_w, up_w, down_w, small, shapes, lengths):
    ways, rows, width = attn_w.shape
    part = rows // 4
    xr = x.astype(BF16)
    tokens = x.shape[0]
    q, k, v = (
        mm("td,zkd->tzk", xr, attn_w[:, i * part : (i + 1) * part]).reshape(tokens, -1)
        for i in range(3)
    )
    q = (q + small["q_bias"]).astype(BF16)
    k = k.astype(BF16)
    v = (v + small["v_bias"]).astype(BF16)
    contexts, logs = [], []
    for qs, ks, vs, lens in zip(
        buckets(q, shapes), buckets(k, shapes), buckets(v, shapes), lengths
    ):
        context, log_total = attention_forward(qs, ks, vs, lens)
        contexts.append(context)
        logs.append(log_total)
    ctx = unbucket(contexts)
    attn = mm("tc,cd->td", ctx, attn_w[:, 3 * part :].reshape(-1, width)) + small["out_bias"]
    h, n1, r1 = norm_forward(x + attn, small["gain"][0], small["bias"][0])
    hr = h.astype(BF16)
    u = mm("td,zdk->tzk", hr, up_w).reshape(tokens, -1) + small["up_bias"]
    a = gelu_value(u).astype(BF16)
    f = mm("tk,kd->td", a, down_w.reshape(-1, width)) + small["down_bias"]
    y, n2, r2 = norm_forward(h + f, small["gain"][1], small["bias"][1])
    return y, (xr, q, k, v, logs, ctx, n1, r1, hr, u, a, n2, r2)


def layer_backward(dy, saved, attn_w, up_w, down_w, small, shapes, lengths):
    xr, q, k, v, logs, ctx, n1, r1, hr, u, a, n2, r2 = saved
    ways, rows, width = attn_w.shape
    part = rows // 4
    tokens = dy.shape[0]
    dz2, gain_two, bias_two = norm_backward(dy, n2, r2, small["gain"][1])
    df = dz2.astype(BF16)
    down_b = jnp.sum(df, axis=0, dtype=F32)
    a4 = a.reshape(tokens, ways, -1)
    down_g = mm("tzk,td->zkd", a4, df).astype(BF16)
    da = mm("td,kd->tk", df, down_w.reshape(-1, width))
    du = (da * gelu_slope(u)).astype(BF16)
    up_b = jnp.sum(du, axis=0, dtype=F32)
    du4 = du.reshape(tokens, ways, -1)
    up_g = mm("td,tzk->zdk", hr, du4).astype(BF16)
    dh = dz2 + mm("tzk,zdk->td", du4, up_w)
    dz1, gain_one, bias_one = norm_backward(dh, n1, r1, small["gain"][0])
    dattn = dz1.astype(BF16)
    out_b = jnp.sum(dattn, axis=0, dtype=F32)
    out_g = mm("tzk,td->zkd", ctx.reshape(tokens, ways, -1), dattn)
    dctx = mm("td,cd->tc", dattn, attn_w[:, 3 * part :].reshape(-1, width)).astype(BF16)
    grads = ([], [], [])
    for qs, ks, vs, lens, log_total, gs in zip(
        buckets(q, shapes),
        buckets(k, shapes),
        buckets(v, shapes),
        lengths,
        logs,
        buckets(dctx, shapes),
    ):
        for store, value in zip(grads, attention_backward(qs, ks, vs, lens, log_total, gs)):
            store.append(value)
    dq, dk, dv = (unbucket(store).reshape(tokens, ways, -1) for store in grads)
    attn_g = jnp.concatenate(
        [mm("tzk,td->zkd", dq, xr), mm("tzk,td->zkd", dk, xr), mm("tzk,td->zkd", dv, xr), out_g],
        axis=1,
    ).astype(BF16)
    dx = dz1
    for i, grad in enumerate((dq, dk, dv)):
        dx = dx + mm("tzk,zkd->td", grad, attn_w[:, i * part : (i + 1) * part])
    qv_b = jnp.stack(
        [jnp.sum(dq, axis=0, dtype=F32).reshape(-1), jnp.sum(dv, axis=0, dtype=F32).reshape(-1)]
    )
    shared = (out_b, jnp.stack([gain_one, gain_two]), jnp.stack([bias_one, bias_two]), down_b)
    return dx, (attn_g, up_g, down_g), (qv_b, up_b, shared)


def to_absolute(rows):
    me = lax.axis_index("mp")
    ways = rows.shape[-2]
    wide = jnp.concatenate([rows, rows], axis=-2)
    flipped = jnp.flip(wide, axis=-2)
    return lax.dynamic_slice_in_dim(flipped, ways - 1 - me, ways, axis=-2)


def local(
    query_states,
    passage_states,
    query_lengths,
    passage_lengths,
    query_count,
    passage_count,
    positive,
    query_key_value_matrix,
    qv_bias,
    out_weight,
    out_bias,
    norm_gain,
    norm_bias,
    up_matrix,
    up_bias,
    down_matrix,
    down_bias,
):
    layers = query_key_value_matrix.shape[0]
    width = query_states.shape[-1]
    ways = lax.axis_size("mp")
    mp_rank = lax.axis_index("mp")
    my_rank = lax.axis_index("dp") * ways + mp_rank
    q_slots, q_len, _ = query_states.shape
    p_slots, p_len, _ = passage_states.shape
    shapes = ((q_slots, q_len), (p_slots, p_len))
    lengths = (
        lax.dynamic_slice_in_dim(query_lengths, mp_rank * q_slots, q_slots),
        lax.dynamic_slice_in_dim(passage_lengths, mp_rank * p_slots, p_slots),
    )
    part = qv_bias.shape[-1]

    tiny = jnp.concatenate([qv_bias.reshape(layers * 2, part), up_bias.reshape(layers * 4, part)])
    tiny_all = [tiny]
    for _ in range(ways - 1):
        tiny_all.append(ring(tiny_all[-1]))
    tiny_all = jnp.stack(tiny_all).astype(F32)

    weights = []
    for l in range(layers):
        qkv_t = jnp.swapaxes(query_key_value_matrix[l], 1, 2).reshape(3 * part, width)
        attn_w = gather_weights(jnp.concatenate([qkv_t, out_weight[l]]))
        up_w = gather_weights(up_matrix[l])
        down_w = gather_weights(down_matrix[l])
        small = {
            "q_bias": tiny_all[:, 2 * l].reshape(-1),
            "v_bias": tiny_all[:, 2 * l + 1].reshape(-1),
            "up_bias": tiny_all[:, 2 * layers + 4 * l : 2 * layers + 4 * (l + 1)].reshape(-1),
            "out_bias": out_bias[l].astype(F32),
            "down_bias": down_bias[l].astype(F32),
            "gain": norm_gain[l].astype(F32),
            "bias": norm_bias[l].astype(F32),
        }
        weights.append((attn_w, up_w, down_w, small))

    x = jnp.concatenate(
        [query_states.reshape(-1, width), passage_states.reshape(-1, width)]
    ).astype(F32)
    kept = []
    for l in range(layers):
        x, saved = layer_forward(x, *weights[l], shapes, lengths)
        kept.append(saved)

    masks, embeds, invs = [], [], []
    start = 0
    for (count, length), lens in zip(shapes, lengths):
        y = x[start : start + count * length].reshape(count, length, width)
        start += count * length
        live = jnp.arange(length, dtype=jnp.int32)[None, :] < lens[:, None]
        mask = live.astype(F32) / lens[:, None].astype(F32)
        pooled = jnp.sum(y * mask[:, :, None], axis=1)
        inv = lax.rsqrt(jnp.sum(pooled * pooled, axis=-1, keepdims=True) + 1e-06)
        masks.append(mask)
        embeds.append(pooled * inv)
        invs.append(inv)

    marks = jnp.zeros((1, width), F32).at[0, :q_slots].set(positive.astype(F32))
    everything = gather_all(jnp.concatenate([embeds[0], embeds[1], marks])[None])
    nq = everything[:, :q_slots].reshape(-1, width)
    np_ = everything[:, q_slots : q_slots + p_slots].reshape(-1, width)
    pos = everything[:, q_slots + p_slots, :q_slots].reshape(-1).astype(jnp.int32)
    num_q, num_p = nq.shape[0], np_.shape[0]
    sims = INV_TEMP * jnp.dot(nq, np_.T, precision=PRECISE_MODE)
    live_p = (jnp.arange(p_slots)[None, :] < passage_count[:, None]).reshape(-1)
    live_q = (jnp.arange(q_slots)[None, :] < query_count[:, None]).reshape(-1).astype(F32)
    masked = jnp.where(live_p[None, :], sims, NEG_FILL)
    top = jnp.max(masked, axis=1, keepdims=True)
    expo = jnp.exp(masked - top)
    total = jnp.sum(expo, axis=1, keepdims=True)
    lse = top[:, 0] + jnp.log(total[:, 0])
    is_pos = (jnp.arange(num_p, dtype=jnp.int32)[None, :] == pos[:, None]).astype(F32)
    pos_score = jnp.sum(is_pos * sims, axis=1)
    live_total = jnp.sum(query_count).astype(F32)
    loss = jnp.sum(live_q * (lse - pos_score)) / live_total
    grad_scale = float(num_q * q_len)
    ds = (grad_scale * live_q / live_total)[:, None] * (expo / total - is_pos)
    my_ds = lax.dynamic_slice_in_dim(ds, my_rank * q_slots, q_slots, axis=0)
    my_dst = lax.dynamic_slice_in_dim(ds.T, my_rank * p_slots, p_slots, axis=0)
    dnq = INV_TEMP * jnp.dot(my_ds, np_, precision=PRECISE_MODE)
    dnp = INV_TEMP * jnp.dot(my_dst, nq, precision=PRECISE_MODE)
    dys = []
    for grad, normed, inv, mask in zip((dnq, dnp), embeds, invs, masks):
        pooled_grad = inv * (grad - normed * jnp.sum(normed * grad, axis=-1, keepdims=True))
        dys.append((mask[:, :, None] * pooled_grad[:, None, :]).reshape(-1, width))
    dy = jnp.concatenate(dys)

    summed = [None] * layers
    smalls = [None] * layers
    for l in reversed(range(layers)):
        dy, big, (qv_b, up_b, shared) = layer_backward(
            dy, kept[l], *weights[l], shapes, lengths
        )
        summed[l] = tuple(reduce_gradient(item) for item in big)
        qv_abs = to_absolute(qv_b.reshape(2, ways, part)).reshape(-1)
        up_abs = to_absolute(up_b.reshape(ways, -1)).reshape(-1)
        flat = jnp.concatenate([qv_abs, up_abs] + [item.reshape(-1) for item in shared])
        smalls[l] = sum_all(flat.reshape(-1, width))

    query_grad = dy[: q_slots * q_len].reshape(query_states.shape)
    passage_grad = dy[q_slots * q_len :].reshape(passage_states.shape)
    attn_out = jnp.stack([s[0] for s in summed])
    qkv_grad = jnp.swapaxes(attn_out[:, : 3 * part].reshape(layers, 3, part, width), 2, 3)
    out_grad = attn_out[:, 3 * part :]
    up_grad = jnp.stack([s[1] for s in summed])
    down_grad = jnp.stack([s[2] for s in summed])
    small_all = jnp.stack(smalls)
    hidden = up_bias.shape[-1]
    cut = lambda lo, hi: small_all[:, lo:hi]
    qv_rows = cut(0, 2)
    qv_grad = lax.dynamic_slice_in_dim(qv_rows, mp_rank * part, part, axis=2)
    up_rows = cut(2, 2 + ways * hidden // width).reshape(layers, -1)
    up_b_grad = lax.dynamic_slice_in_dim(up_rows, mp_rank * hidden, hidden, axis=1)
    base = 2 + ways * hidden // width
    return (
        loss,
        query_grad,
        passage_grad,
        qkv_grad,
        qv_grad,
        out_grad,
        cut(base, base + 1)[:, 0],
        cut(base + 1, base + 3),
        cut(base + 3, base + 5),
        up_grad,
        up_b_grad,
        down_grad,
        cut(base + 5, base + 6)[:, 0],
    )


def solution(mesh):
    placed = (
        P(("dp", "mp"), None, None),
        P(("dp", "mp"), None, None),
        P("dp"),
        P("dp"),
        P(),
        P(),
        P(("dp", "mp")),
        P(None, None, None, "mp"),
        P(None, None, "mp"),
        P(None, "mp", None),
        P(),
        P(),
        P(),
        P(None, None, "mp"),
        P(None, "mp"),
        P(None, "mp", None),
        P(),
    )
    return jax.shard_map(
        local,
        mesh=mesh,
        in_specs=placed,
        out_specs=(
            P(),
            P(("dp", "mp"), None, None),
            P(("dp", "mp"), None, None),
            P(None, None, None, "mp"),
            P(None, None, "mp"),
            P(None, "mp", None),
            P(),
            P(),
            P(),
            P(None, None, "mp"),
            P(None, "mp"),
            P(None, "mp", None),
            P(),
        ),
        check_vma=False,
    )
```

time: 2360 us -> 862 us (0.37)
  waiting for transfers between devices: 1780 us -> 233 us
  blocking collectives: 133 us -> 0 us
  starting transfers between devices: 3.84 us -> 132 us
  local copies, waits for them, and re-layouts: 65.4 us -> 164 us
  matrix products: 229 us -> 193 us
    reduce_scatter x16 -> x0, waiting for transfers between devices: 821 us -> none  [the longest x4 438 us: sum_rows(): lax.psum_scatter(pair[1], 'mp', scatter_dimension=0, tiled=True)]
    all_gather x16 -> x0, waiting for transfers between devices: 699 us -> none  [the longest x4 221 us: gather_rows(): lax.all_gather(pair[1], 'mp', axis=0, tiled=True)]
    ppermute x0 -> x144, waiting for transfers between devices: none -> 233 us  [the longest x99 160 us: flip(): return lax.ppermute(value, 'dp', [(i, i ^ bit) for i in range(size)])]
    psum x1 -> x0, waiting for transfers between devices: 141 us -> none  [local(): lax.psum((local_sharded[0], local_sharded[1], local_sharded[2], local_sha...]
    ppermute x0 -> x144, starting transfers between devices: none -> 132 us  [the longest x99 97 us: flip(): return lax.ppermute(value, 'dp', [(i, i ^ bit) for i in range(size)])]
    unnamed x35 -> x0, waiting for transfers between devices: 116 us -> none
    all_gather x1 -> x0, blocking collectives: 68.2 us -> none  [local(): pass_all = lax.all_gather(normed_list[1], ('dp', 'mp'), axis=0, tiled=True)]
    psum x2 -> x0, blocking collectives: 65.3 us -> none  [the longest x1 40.7 us: local(): lax.psum((local_shared[0], local_shared[1], local_shared[2], local_shared...]
  transfers between devices with their start and end apart: 34 -> 144, of which waited for: 32 -> 69; matrix products, arithmetic and copies ran while one was open for 15% -> 28% of each run, Pallas kernels for 0% -> 0%
where the time goes in v1:
time: 862 us; the launch traced here: 854 us
  waiting for transfers between devices  233 us (27%)
  matrix products  193 us (22%)
  local copies, waits for them, and re-layouts  164 us (19%)
  starting transfers between devices  132 us (15%)
  other arithmetic  122 us (14%)
  between operations  9.7 us (1%)
    dot_general x60, matrix products, mm(): return jnp.einsum(spec, left, right, preferred_element_type=F32)  191 us
    ppermute x99, waiting for transfers between devices, flip(): return lax.ppermute(value, 'dp', [(i, i ^ bit) for i in range(size)])  160 us
    ppermute x99, starting transfers between devices, flip(): return lax.ppermute(value, 'dp', [(i, i ^ bit) for i in range(size)])  97 us
    ppermute x39, waiting for transfers between devices, ring(): return lax.ppermute(value, 'mp', [(i, (i + 1) % size) for i in range(size)])  71 us
    unnamed x531, local copies, waits for them, and re-layouts  45.7 us
    ppermute x39, starting transfers between devices, ring(): return lax.ppermute(value, 'mp', [(i, (i + 1) % size) for i in range(size)])  27.8 us
    dynamic_slice x12, local copies, waits for them, and re-layouts, pick(): return lax.dynamic_index_in_dim(value, index, axis=axis, keepdims=False)  20.6 us
    reshape x2, local copies, waits for them, and re-layouts, layer_forward(): u = mm('td,zdk->tzk', hr, up_w).reshape(tokens, -1) + small['up_bias']  19.2 us
  transfers between devices with their start and end apart: 144, of which 69 were waited for; matrix products, arithmetic and copies ran while one was open for 28% of the time, Pallas kernels for 0%

profile of v1, /device:TPU:0, one launch (start us, length us, event | category | flops | bytes accessed | tf_op | source)
XLA Modules:
  0.0 854.4 jit_solution(4899444705039375747)
XLA Ops:
  23.0 3.7 collective-permute-done.9
  81.1 7.4 collective-permute-done.38
  90.8 7.3 collective-permute-done.30
  100.1 7.4 collective-permute-done.22
  111.7 3.7 collective-permute-done.14
  117.6 4.7 collective-permute-done.3
  127.0 5.2 collective-permute-done.16
  132.3 6.7 collective-permute-done.5
  149.3 5.2 collective-permute-done.15
  156.8 3.6 collective-permute-done.4
  167.9 4.4 collective-permute-done.6
  198.8 3.7 fusion.306
  217.1 8.2 multiply_convert_fusion.3
  225.4 3.7 broadcast_select_fusion.7
  229.2 4.6 fusion.309
  275.5 8.8 %multiply_convert_fusion.2 = (bf16[768,4,768]{0,2,1:T(8,128)(2,1)S(1)}, f32[768,4,768]{0,2,1:T(8,128)}) fusion(f32[4,768]{1,0:T(4,128)S(1)} %copy-done.194, bf16[3,384,768]{2,1,0:T(8,128)(2,1)S(1)} %get-tuple-element.117, bf16[3,384,768]{2,1,0:T(8,128)(2,1)S(1)} %get-tuple-element.116, bf16[1,768,768]{2,1,0:T(8,128)(2,1)S(1)} %copy-done.112, ...), kind=kOutput, calls=%fused_computation.32 | convolution fusion | flops 3655139328 | bytes 21258240 | tf_op jit(solution)/shard_map/td,zdk->tzk/dot_general | solution.py:170
  284.4 5.2 fusion.313
  295.8 4.2 maximum_maximum_fusion.2
  312.6 9.6 %copy.97 = f32[768,3072]{1,0:T(8,128)} copy(f32[768,3072]{0,1:T(8,128)} %bitcast.684) | data formatting | bytes 18874368 | tf_op jit(solution)/shard_map/reshape | solution.py:236
  322.2 9.6 %copy.113 = f32[768,3072]{1,0:T(8,128)} copy(f32[768,3072]{0,1:T(8,128)} %bitcast.681) | data formatting | bytes 18874368 | tf_op jit(solution)/shard_map/reshape | solution.py:236
  334.1 5.3 collective-permute-done.55
  356.2 11.1 %convert_reduce_fusion = (f32[3072]{0:T(1024)}, bf16[768,3072]{1,0:T(8,128)(2,1)}) fusion(f32[768,3072]{1,0:T(8,128)S(1)} %copy-done.19, f32[3072]{0:T(1024)S(1)} %copy-done.193, bf16[3072,768]{1,0:T(8,128)(2,1)} %bitcast.713, f32[768,768]{1,0:T(8,128)S(1)} %get-tuple-element.85), kind=kOutput, calls=%fused_computation.30 | convolution fusion | flops 3655136256 | bytes 21258240 | tf_op jit(solution)/shard_map/td,kd->tk/dot_general | solution.py:170
  367.4 8.0 multiply_reduce_fusion.3
  383.1 6.7 multiply_reduce_fusion.1
  392.2 9.9 %multiply_convert_fusion.1 = bf16[12,512,512]{1,2,0:T(8,128)(2,1)S(1)} fusion(f32[12,512,512]{1,2,0:T(8,128)} %get-tuple-element.276, f32[12,512,512]{1,2,0:T(8,128)} %copy-done.1, f32[12,512]{1,0:T(8,128)S(1)} %copy-done.150, f32[12,512]{1,0:T(8,128)S(1)} %copy-done.130), kind=kLoop, calls=%fused_computation.5 | loop fusion | flops 12582912 | bytes 31506432 | tf_op jit(solution)/shard_map/convert_element_type | solution.py:193
  420.3 11.7 %convert_reduce_fusion.1 = (f32[3072]{0:T(1024)}, bf16[768,3072]{1,0:T(8,128)(2,1)}) fusion(f32[768,3072]{1,0:T(8,128)S(1)} %bitcast.683, f32[3072]{0:T(1024)S(1)} %copy-done.192, bf16[3072,768]{1,0:T(8,128)(2,1)} %bitcast.709, f32[768,768]{1,0:T(8,128)S(1)} %get-tuple-element.89), kind=kOutput, calls=%fused_computation.31 | convolution fusion | flops 3655136256 | bytes 21258240 | tf_op jit(solution)/shard_map/td,kd->tk/dot_general | solution.py:170
  432.1 7.7 multiply_reduce_fusion.5
  444.3 6.1 multiply_reduce_fusion
  450.3 7.1 multiply_convert_fusion
  465.9 6.6 fusion.67
  481.2 4.2 fusion.139
  488.9 4.5 fusion.142
  503.4 8.5 fusion.42
  512.0 6.1 fusion.45
  518.2 5.5 convolution_convert_fusion
  523.7 5.6 convolution_convert_fusion.1
  590.5 4.7 bitcast_add_fusion
  599.4 5.1 constant_dynamic-slice_fusion.6
  651.2 11.2 %collective-permute-done.57 = bf16[4,2,96,384]{3,2,0,1:T(8,128)(2,1)S(1)} collective-permute-done((bf16[4,2,96,384]{3,2,0,1:T(8,128)(2,1)S(1)}, bf16[4,2,96,384]{3,2,0,1:T(8,128)(2,1)S(1)}, u32[]{:S(2)}, u32[]{:S(2)}) %collective-permute-start.57) | collective-permute-done | bytes 589856 | tf_op jit(solution)/shard_map/ppermute | solution.py:24
  668.2 7.0 collective-permute-done.106
  680.7 7.1 collective-permute-done.93
  693.4 7.0 collective-permute-done.132
  705.9 7.1 collective-permute-done.119
  718.7 4.9 collective-permute-done.71
  725.9 4.0 collective-permute-done.58
  732.2 4.0 collective-permute-done.107
  738.5 4.0 collective-permute-done.94
  815.3 4.2 collective-permute-done.139
  (1281 shorter events, 542.8 us)
Async XLA Ops:
  2.1 19.1 %collective-permute-start.8 = (bf16[12,192]{1,0:T(8,128)(2,1)S(1)}, bf16[12,192]{1,0:T(8,128)(2,1)S(1)}, u32[]{:S(2)}, u32[]{:S(2)}) collective-permute-start(bf16[12,192]{1,0:T(8,128)(2,1)S(1)} %get-tuple-element.245), channel_id=1, source_target_pairs={{0,1},{1,2},{2,3},{3,0},{4,5},{5,6},{6,7},{7,4},{8,9},{9,10},{10,1... | collective-permute-start | bytes 13832 | tf_op jit(solution)/shard_map/ppermute | solution.py:34
  7.1 25.1 %collective-permute-start.43 = (bf16[96,768]{1,0:T(8,128)(2,1)S(1)}, bf16[96,768]{1,0:T(8,128)(2,1)S(1)}, u32[]{:S(2)}, u32[]{:S(2)}) collective-permute-start(bf16[96,768]{1,0:T(8,128)(2,1)S(1)} %dynamic-slice_bitcast_fusion.24), channel_id=1, source_target_pairs={{0,1},{1,2},{2,3},{3,0},{4,5},{5,6},{6,7},{7,4},{8,9},{9,10},{10,1... | collective-permute-start | bytes 442376 | tf_op jit(solution)/shard_map/ppermute | solution.py:34
  10.6 21.6 %collective-permute-start.35 = (bf16[96,768]{1,0:T(8,128)(2,1)S(1)}, bf16[96,768]{1,0:T(8,128)(2,1)S(1)}, u32[]{:S(2)}, u32[]{:S(2)}) collective-permute-start(bf16[96,768]{1,0:T(8,128)(2,1)S(1)} %dynamic-slice_bitcast_fusion.25), channel_id=1, source_target_pairs={{0,1},{1,2},{2,3},{3,0},{4,5},{5,6},{6,7},{7,4},{8,9},{9,10},{10,1... | collective-permute-start | bytes 442376 | tf_op jit(solution)/shard_map/ppermute | solution.py:34
  12.5 21.1 %collective-permute-start.27 = (bf16[96,768]{1,0:T(8,128)(2,1)S(1)}, bf16[96,768]{1,0:T(8,128)(2,1)S(1)}, u32[]{:S(2)}, u32[]{:S(2)}) collective-permute-start(bf16[96,768]{1,0:T(8,128)(2,1)S(1)} %fusion.201), channel_id=1, source_target_pairs={{0,1},{1,2},{2,3},{3,0},{4,5},{5,6},{6,7},{7,4},{8,9},{9,10},{10,1... | collective-permute-start | bytes 442376 | tf_op jit(solution)/shard_map/ppermute | solution.py:34
  13.8 24.5 %collective-permute-start.19 = (bf16[96,768]{1,0:T(8,128)(2,1)S(1)}, bf16[96,768]{1,0:T(8,128)(2,1)S(1)}, u32[]{:S(2)}, u32[]{:S(2)}) collective-permute-start(bf16[96,768]{1,0:T(8,128)(2,1)S(1)} %dynamic-slice_bitcast_fusion.26), channel_id=1, source_target_pairs={{0,1},{1,2},{2,3},{3,0},{4,5},{5,6},{6,7},{7,4},{8,9},{9,10},{10,1... | collective-permute-start | bytes 442376 | tf_op jit(solution)/shard_map/ppermute | solution.py:34
  74.3 35.3 %collective-permute-start.48 = (bf16[3,96,768]{2,1,0:T(8,128)(2,1)S(1)}, bf16[3,96,768]{2,1,0:T(8,128)(2,1)S(1)}, u32[]{:S(2)}, u32[]{:S(2)}) collective-permute-start(bf16[3,96,768]{2,1,0:T(8,128)(2,1)S(1)} %pad_maximum_fusion.45), channel_id=1, source_target_pairs={{0,16},{4,20},{8,24},{12,28},{16,0},{20,4},{24,8},{28,12},{1,17},{... | collective-permute-start | bytes 1327112 | tf_op jit(solution)/shard_map/ppermute | solution.py:24
  75.9 35.3 %collective-permute-start.40 = (bf16[3,96,768]{2,1,0:T(8,128)(2,1)S(1)}, bf16[3,96,768]{2,1,0:T(8,128)(2,1)S(1)}, u32[]{:S(2)}, u32[]{:S(2)}) collective-permute-start(bf16[3,96,768]{2,1,0:T(8,128)(2,1)S(1)} %pad_maximum_fusion.44), channel_id=1, source_target_pairs={{0,16},{4,20},{8,24},{12,28},{16,0},{20,4},{24,8},{28,12},{1,17},{... | collective-permute-start | bytes 1327112 | tf_op jit(solution)/shard_map/ppermute | solution.py:24
  77.5 20.5 %collective-permute-start.30 = (bf16[3,96,768]{2,1,0:T(8,128)(2,1)S(1)}, bf16[3,96,768]{2,1,0:T(8,128)(2,1)S(1)}, u32[]{:S(2)}, u32[]{:S(2)}) collective-permute-start(bf16[3,96,768]{2,1,0:T(8,128)(2,1)S(1)} %pad_maximum_fusion.43), channel_id=1, source_target_pairs={{0,8},{4,12},{8,0},{12,4},{16,24},{20,28},{24,16},{28,20},{1,9},{5... | collective-permute-start | bytes 1327112 | tf_op jit(solution)/shard_map/ppermute | solution.py:24
  79.1 38.1 %collective-permute-start.32 = (bf16[3,96,768]{2,1,0:T(8,128)(2,1)S(1)}, bf16[3,96,768]{2,1,0:T(8,128)(2,1)S(1)}, u32[]{:S(2)}, u32[]{:S(2)}) collective-permute-start(bf16[3,96,768]{2,1,0:T(8,128)(2,1)S(1)} %pad_maximum_fusion.43), channel_id=1, source_target_pairs={{0,16},{4,20},{8,24},{12,28},{16,0},{20,4},{24,8},{28,12},{1,17},{... | collective-permute-start | bytes 1327112 | tf_op jit(solution)/shard_map/ppermute | solution.py:24
  88.5 19.0 %collective-permute-start.22 = (bf16[3,96,768]{2,1,0:T(8,128)(2,1)S(1)}, bf16[3,96,768]{2,1,0:T(8,128)(2,1)S(1)}, u32[]{:S(2)}, u32[]{:S(2)}) collective-permute-start(bf16[3,96,768]{2,1,0:T(8,128)(2,1)S(1)} %pad_maximum_fusion.42), channel_id=1, source_target_pairs={{0,8},{4,12},{8,0},{12,4},{16,24},{20,28},{24,16},{28,20},{1,9},{5... | collective-permute-start | bytes 1327112 | tf_op jit(solution)/shard_map/ppermute | solution.py:24
  111.2 21.1 %collective-permute-start.16 = (bf16[3,96,768]{2,1,0:T(8,128)(2,1)S(1)}, bf16[3,96,768]{2,1,0:T(8,128)(2,1)S(1)}, u32[]{:S(2)}, u32[]{:S(2)}) collective-permute-start(bf16[3,96,768]{2,1,0:T(8,128)(2,1)S(1)} %pad_maximum_fusion.41), channel_id=1, source_target_pairs={{0,16},{4,20},{8,24},{12,28},{16,0},{20,4},{24,8},{28,12},{1,17},{... | collective-permute-start | bytes 1327112 | tf_op jit(solution)/shard_map/ppermute | solution.py:24
  115.4 23.6 %collective-permute-start.5 = (bf16[3,96,768]{2,1,0:T(8,128)(2,1)S(1)}, bf16[3,96,768]{2,1,0:T(8,128)(2,1)S(1)}, u32[]{:S(2)}, u32[]{:S(2)}) collective-permute-start(bf16[3,96,768]{2,1,0:T(8,128)(2,1)S(1)} %pad_maximum_fusion.40), channel_id=1, source_target_pairs={{0,16},{4,20},{8,24},{12,28},{16,0},{20,4},{24,8},{28,12},{1,17},{... | collective-permute-start | bytes 1327112 | tf_op jit(solution)/shard_map/ppermute | solution.py:24
  117.2 26.5 %collective-permute-start.47 = (bf16[3,48,768]{2,1,0:T(8,128)(2,1)S(1)}, bf16[3,48,768]{2,1,0:T(8,128)(2,1)S(1)}, u32[]{:S(2)}, u32[]{:S(2)}) collective-permute-start(bf16[3,48,768]{2,1,0:T(8,128)(2,1)S(1)} %slice.605), channel_id=1, source_target_pairs={{0,16},{4,20},{8,24},{12,28},{16,0},{20,4},{24,8},{28,12},{1,17},{... | collective-permute-start | bytes 663560 | tf_op jit(solution)/shard_map/ppermute | solution.py:24
  122.3 23.9 %collective-permute-start.39 = (bf16[3,48,768]{2,1,0:T(8,128)(2,1)S(1)}, bf16[3,48,768]{2,1,0:T(8,128)(2,1)S(1)}, u32[]{:S(2)}, u32[]{:S(2)}) collective-permute-start(bf16[3,48,768]{2,1,0:T(8,128)(2,1)S(1)} %slice.603), channel_id=1, source_target_pairs={{0,16},{4,20},{8,24},{12,28},{16,0},{20,4},{24,8},{28,12},{1,17},{... | collective-permute-start | bytes 663560 | tf_op jit(solution)/shard_map/ppermute | solution.py:24
  125.3 22.4 %collective-permute-start.49 = (bf16[3,48,768]{2,1,0:T(8,128)(2,1)S(1)}, bf16[3,48,768]{2,1,0:T(8,128)(2,1)S(1)}, u32[]{:S(2)}, u32[]{:S(2)}) collective-permute-start(bf16[3,48,768]{2,1,0:T(8,128)(2,1)S(1)} %slice.606), channel_id=1, source_target_pairs={{0,8},{4,12},{8,0},{12,4},{16,24},{20,28},{24,16},{28,20},{1,9},{5... | collective-permute-start | bytes 663560 | tf_op jit(solution)/shard_map/ppermute | solution.py:24
  139.1 34.1 %collective-permute-start.31 = (bf16[3,48,768]{2,1,0:T(8,128)(2,1)S(1)}, bf16[3,48,768]{2,1,0:T(8,128)(2,1)S(1)}, u32[]{:S(2)}, u32[]{:S(2)}) collective-permute-start(bf16[3,48,768]{2,1,0:T(8,128)(2,1)S(1)} %slice.589), channel_id=1, source_target_pairs={{0,16},{4,20},{8,24},{12,28},{16,0},{20,4},{24,8},{28,12},{1,17},{... | collective-permute-start | bytes 663560 | tf_op jit(solution)/shard_map/ppermute | solution.py:24
  143.7 30.1 %collective-permute-start.33 = (bf16[3,48,768]{2,1,0:T(8,128)(2,1)S(1)}, bf16[3,48,768]{2,1,0:T(8,128)(2,1)S(1)}, u32[]{:S(2)}, u32[]{:S(2)}) collective-permute-start(bf16[3,48,768]{2,1,0:T(8,128)(2,1)S(1)} %slice.590), channel_id=1, source_target_pairs={{0,8},{4,12},{8,0},{12,4},{16,24},{20,28},{24,16},{28,20},{1,9},{5... | collective-permute-start | bytes 663560 | tf_op jit(solution)/shard_map/ppermute | solution.py:24
  146.2 27.6 %collective-permute-start.23 = (bf16[3,48,768]{2,1,0:T(8,128)(2,1)S(1)}, bf16[3,48,768]{2,1,0:T(8,128)(2,1)S(1)}, u32[]{:S(2)}, u32[]{:S(2)}) collective-permute-start(bf16[3,48,768]{2,1,0:T(8,128)(2,1)S(1)} %slice.585), channel_id=1, source_target_pairs={{0,16},{4,20},{8,24},{12,28},{16,0},{20,4},{24,8},{28,12},{1,17},{... | collective-permute-start | bytes 663560 | tf_op jit(solution)/shard_map/ppermute | solution.py:24
  147.7 26.2 %collective-permute-start.25 = (bf16[3,48,768]{2,1,0:T(8,128)(2,1)S(1)}, bf16[3,48,768]{2,1,0:T(8,128)(2,1)S(1)}, u32[]{:S(2)}, u32[]{:S(2)}) collective-permute-start(bf16[3,48,768]{2,1,0:T(8,128)(2,1)S(1)} %slice.586), channel_id=1, source_target_pairs={{0,8},{4,12},{8,0},{12,4},{16,24},{20,28},{24,16},{28,20},{1,9},{5... | collective-permute-start | bytes 663560 | tf_op jit(solution)/shard_map/ppermute | solution.py:24
  172.3 100.9 %collective-permute-start.42 = (bf16[3,384,768]{2,1,0:T(8,128)(2,1)}, bf16[3,384,768]{2,1,0:T(8,128)(2,1)}, u32[]{:S(2)}, u32[]{:S(2)}) collective-permute-start(bf16[3,384,768]{2,1,0:T(8,128)(2,1)} %pad_maximum_fusion.7), channel_id=1, source_target_pairs={{0,4},{4,0},{8,12},{12,8},{16,20},{20,16},{24,28},{28,24},{1,5},{5... | collective-permute-start | bytes 5308424 | tf_op jit(solution)/shard_map/ppermute | solution.py:24
  176.2 58.1 %collective-permute-start.34 = (bf16[3,384,768]{2,1,0:T(8,128)(2,1)}, bf16[3,384,768]{2,1,0:T(8,128)(2,1)}, u32[]{:S(2)}, u32[]{:S(2)}) collective-permute-start(bf16[3,384,768]{2,1,0:T(8,128)(2,1)} %pad_maximum_fusion.6), channel_id=1, source_target_pairs={{0,4},{4,0},{8,12},{12,8},{16,20},{20,16},{24,28},{28,24},{1,5},{5... | collective-permute-start | bytes 5308424 | tf_op jit(solution)/shard_map/ppermute | solution.py:24
  177.6 37.0 %collective-permute-start.18 = (bf16[3,384,768]{2,1,0:T(8,128)(2,1)}, bf16[3,384,768]{2,1,0:T(8,128)(2,1)}, u32[]{:S(2)}, u32[]{:S(2)}) collective-permute-start(bf16[3,384,768]{2,1,0:T(8,128)(2,1)} %pad_maximum_fusion.4), channel_id=1, source_target_pairs={{0,4},{4,0},{8,12},{12,8},{16,20},{20,16},{24,28},{28,24},{1,5},{5... | collective-permute-start | bytes 5308424 | tf_op jit(solution)/shard_map/ppermute | solution.py:24
  179.4 46.0 %collective-permute-start.26 = (bf16[3,384,768]{2,1,0:T(8,128)(2,1)}, bf16[3,384,768]{2,1,0:T(8,128)(2,1)}, u32[]{:S(2)}, u32[]{:S(2)}) collective-permute-start(bf16[3,384,768]{2,1,0:T(8,128)(2,1)} %pad_maximum_fusion.5), channel_id=1, source_target_pairs={{0,4},{4,0},{8,12},{12,8},{16,20},{20,16},{24,28},{28,24},{1,5},{5... | collective-permute-start | bytes 5308424 | tf_op jit(solution)/shard_map/ppermute | solution.py:24
  180.8 85.9 %collective-permute-start.50 = (bf16[3,384,768]{2,1,0:T(8,128)(2,1)}, bf16[3,384,768]{2,1,0:T(8,128)(2,1)}, u32[]{:S(2)}, u32[]{:S(2)}) collective-permute-start(bf16[3,384,768]{2,1,0:T(8,128)(2,1)} %pad_maximum_fusion.8), channel_id=1, source_target_pairs={{0,4},{4,0},{8,12},{12,8},{16,20},{20,16},{24,28},{28,24},{1,5},{5... | collective-permute-start | bytes 5308424 | tf_op jit(solution)/shard_map/ppermute | solution.py:24
  307.5 24.2 %collective-permute-start.54 = (f32[8,4,768]{2,1,0:T(4,128)}, f32[8,4,768]{2,1,0:T(4,128)}, u32[]{:S(2)}, u32[]{:S(2)}) collective-permute-start(f32[8,4,768]{2,1,0:T(4,128)} %pad_maximum_fusion.73), channel_id=1, source_target_pairs={{0,8},{4,12},{8,0},{12,4},{16,24},{20,28},{24,16},{28,20},{1,9},{5... | collective-permute-start | bytes 294920 | tf_op jit(solution)/shard_map/ppermute | solution.py:24
  533.6 97.2 %collective-permute-start.69 = (bf16[4,2,2,96,768]{4,3,0,2,1:T(8,128)(2,1)}, bf16[4,2,2,96,768]{4,3,0,2,1:T(8,128)(2,1)}, u32[]{:S(2)}, u32[]{:S(2)}) collective-permute-start(bf16[4,2,2,96,768]{4,3,0,2,1:T(8,128)(2,1)} %bitcast.667), channel_id=1, source_target_pairs={{0,4},{4,0},{8,12},{12,8},{16,20},{20,16},{24,28},{28,24},{1,5},{5... | collective-permute-start | bytes 7077896 | tf_op jit(solution)/shard_map/ppermute | solution.py:24
  540.0 93.6 %collective-permute-start.56 = (bf16[4,2,2,96,768]{4,3,0,2,1:T(8,128)(2,1)}, bf16[4,2,2,96,768]{4,3,0,2,1:T(8,128)(2,1)}, u32[]{:S(2)}, u32[]{:S(2)}) collective-permute-start(bf16[4,2,2,96,768]{4,3,0,2,1:T(8,128)(2,1)} %bitcast.668), channel_id=1, source_target_pairs={{0,4},{4,0},{8,12},{12,8},{16,20},{20,16},{24,28},{28,24},{1,5},{5... | collective-permute-start | bytes 7077896 | tf_op jit(solution)/shard_map/ppermute | solution.py:24
  564.5 32.0 %collective-permute-start.82 = (f32[12,768]{1,0:T(8,128)}, f32[12,768]{1,0:T(8,128)}, u32[]{:S(2)}, u32[]{:S(2)}) collective-permute-start(f32[12,768]{1,0:T(8,128)} %reshape.1192), channel_id=1, source_target_pairs={{0,4},{4,0},{8,12},{12,8},{16,20},{20,16},{24,28},{28,24},{1,5},{5... | collective-permute-start | bytes 110600 | tf_op jit(solution)/shard_map/ppermute | solution.py:24
  617.6 20.3 %collective-permute-start.105 = (bf16[4,2,2,96,768]{4,3,0,2,1:T(8,128)(2,1)S(1)}, bf16[4,2,2,96,768]{4,3,0,2,1:T(8,128)(2,1)S(1)}, u32[]{:S(2)}, u32[]{:S(2)}) collective-permute-start(bf16[4,2,2,96,768]{4,3,0,2,1:T(8,128)(2,1)S(1)} %bitcast.730), channel_id=1, source_target_pairs={{0,4},{4,0},{8,12},{12,8},{16,20},{20,16},{24,28},{28,24},{1,5},{5... | collective-permute-start | bytes 7077896 | tf_op jit(solution)/shard_map/ppermute | solution.py:24
  637.9 26.0 %collective-permute-start.72 = (bf16[4,2,96,384]{3,2,0,1:T(8,128)(2,1)S(1)}, bf16[4,2,96,384]{3,2,0,1:T(8,128)(2,1)S(1)}, u32[]{:S(2)}, u32[]{:S(2)}) collective-permute-start(bf16[4,2,96,384]{3,2,0,1:T(8,128)(2,1)S(1)} %dynamic-slice_bitcast_fusion.8), channel_id=1, source_target_pairs={{0,16},{4,20},{8,24},{12,28},{16,0},{20,4},{24,8},{28,12},{1,17},{... | collective-permute-start | bytes 1769480 | tf_op jit(solution)/shard_map/ppermute | solution.py:24
  640.5 21.9 %collective-permute-start.57 = (bf16[4,2,96,384]{3,2,0,1:T(8,128)(2,1)S(1)}, bf16[4,2,96,384]{3,2,0,1:T(8,128)(2,1)S(1)}, u32[]{:S(2)}, u32[]{:S(2)}) collective-permute-start(bf16[4,2,96,384]{3,2,0,1:T(8,128)(2,1)S(1)} %dynamic-slice_bitcast_fusion.11), channel_id=1, source_target_pairs={{0,8},{4,12},{8,0},{12,4},{16,24},{20,28},{24,16},{28,20},{1,9},{5... | collective-permute-start | bytes 1769480 | tf_op jit(solution)/shard_map/ppermute | solution.py:24
  643.0 23.7 %collective-permute-start.59 = (bf16[4,2,96,384]{3,2,0,1:T(8,128)(2,1)S(1)}, bf16[4,2,96,384]{3,2,0,1:T(8,128)(2,1)S(1)}, u32[]{:S(2)}, u32[]{:S(2)}) collective-permute-start(bf16[4,2,96,384]{3,2,0,1:T(8,128)(2,1)S(1)} %dynamic-slice_bitcast_fusion.10), channel_id=1, source_target_pairs={{0,16},{4,20},{8,24},{12,28},{16,0},{20,4},{24,8},{28,12},{1,17},{... | collective-permute-start | bytes 1769480 | tf_op jit(solution)/shard_map/ppermute | solution.py:24
  645.6 29.5 %collective-permute-start.106 = (bf16[4,2,96,384]{3,2,0,1:T(8,128)(2,1)S(1)}, bf16[4,2,96,384]{3,2,0,1:T(8,128)(2,1)S(1)}, u32[]{:S(2)}, u32[]{:S(2)}) collective-permute-start(bf16[4,2,96,384]{3,2,0,1:T(8,128)(2,1)S(1)} %dynamic-slice_bitcast_fusion.5), channel_id=1, source_target_pairs={{0,8},{4,12},{8,0},{12,4},{16,24},{20,28},{24,16},{28,20},{1,9},{5... | collective-permute-start | bytes 1769480 | tf_op jit(solution)/shard_map/ppermute | solution.py:24
  649.8 29.5 %collective-permute-start.108 = (bf16[4,2,96,384]{3,2,0,1:T(8,128)(2,1)S(1)}, bf16[4,2,96,384]{3,2,0,1:T(8,128)(2,1)S(1)}, u32[]{:S(2)}, u32[]{:S(2)}) collective-permute-start(bf16[4,2,96,384]{3,2,0,1:T(8,128)(2,1)S(1)} %dynamic-slice_bitcast_fusion.4), channel_id=1, source_target_pairs={{0,16},{4,20},{8,24},{12,28},{16,0},{20,4},{24,8},{28,12},{1,17},{... | collective-permute-start | bytes 1769480 | tf_op jit(solution)/shard_map/ppermute | solution.py:24
  662.5 25.3 %collective-permute-start.93 = (bf16[4,2,96,384]{3,2,0,1:T(8,128)(2,1)S(1)}, bf16[4,2,96,384]{3,2,0,1:T(8,128)(2,1)S(1)}, u32[]{:S(2)}, u32[]{:S(2)}) collective-permute-start(bf16[4,2,96,384]{3,2,0,1:T(8,128)(2,1)S(1)} %dynamic-slice_bitcast_fusion.7), channel_id=1, source_target_pairs={{0,8},{4,12},{8,0},{12,4},{16,24},{20,28},{24,16},{28,20},{1,9},{5... | collective-permute-start | bytes 1769480 | tf_op jit(solution)/shard_map/ppermute | solution.py:24
  663.9 28.1 %collective-permute-start.95 = (bf16[4,2,96,384]{3,2,0,1:T(8,128)(2,1)S(1)}, bf16[4,2,96,384]{3,2,0,1:T(8,128)(2,1)S(1)}, u32[]{:S(2)}, u32[]{:S(2)}) collective-permute-start(bf16[4,2,96,384]{3,2,0,1:T(8,128)(2,1)S(1)} %dynamic-slice_bitcast_fusion.6), channel_id=1, source_target_pairs={{0,16},{4,20},{8,24},{12,28},{16,0},{20,4},{24,8},{28,12},{1,17},{... | collective-permute-start | bytes 1769480 | tf_op jit(solution)/shard_map/ppermute | solution.py:24
  666.7 33.7 %collective-permute-start.132 = (bf16[4,2,96,384]{3,2,0,1:T(8,128)(2,1)S(1)}, bf16[4,2,96,384]{3,2,0,1:T(8,128)(2,1)S(1)}, u32[]{:S(2)}, u32[]{:S(2)}) collective-permute-start(bf16[4,2,96,384]{3,2,0,1:T(8,128)(2,1)S(1)} %dynamic-slice_bitcast_fusion.1), channel_id=1, source_target_pairs={{0,8},{4,12},{8,0},{12,4},{16,24},{20,28},{24,16},{28,20},{1,9},{5... | collective-permute-start | bytes 1769480 | tf_op jit(solution)/shard_map/ppermute | solution.py:24
  675.1 29.5 %collective-permute-start.134 = (bf16[4,2,96,384]{3,2,0,1:T(8,128)(2,1)S(1)}, bf16[4,2,96,384]{3,2,0,1:T(8,128)(2,1)S(1)}, u32[]{:S(2)}, u32[]{:S(2)}) collective-permute-start(bf16[4,2,96,384]{3,2,0,1:T(8,128)(2,1)S(1)} %dynamic-slice_bitcast_fusion), channel_id=1, source_target_pairs={{0,16},{4,20},{8,24},{12,28},{16,0},{20,4},{24,8},{28,12},{1,17},{... | collective-permute-start | bytes 1769480 | tf_op jit(solution)/shard_map/ppermute | solution.py:24
  679.4 33.7 %collective-permute-start.119 = (bf16[4,2,96,384]{3,2,0,1:T(8,128)(2,1)S(1)}, bf16[4,2,96,384]{3,2,0,1:T(8,128)(2,1)S(1)}, u32[]{:S(2)}, u32[]{:S(2)}) collective-permute-start(bf16[4,2,96,384]{3,2,0,1:T(8,128)(2,1)S(1)} %dynamic-slice_bitcast_fusion.3), channel_id=1, source_target_pairs={{0,8},{4,12},{8,0},{12,4},{16,24},{20,28},{24,16},{28,20},{1,9},{5... | collective-permute-start | bytes 1769480 | tf_op jit(solution)/shard_map/ppermute | solution.py:24
  687.8 29.5 %collective-permute-start.121 = (bf16[4,2,96,384]{3,2,0,1:T(8,128)(2,1)S(1)}, bf16[4,2,96,384]{3,2,0,1:T(8,128)(2,1)S(1)}, u32[]{:S(2)}, u32[]{:S(2)}) collective-permute-start(bf16[4,2,96,384]{3,2,0,1:T(8,128)(2,1)S(1)} %dynamic-slice_bitcast_fusion.2), channel_id=1, source_target_pairs={{0,16},{4,20},{8,24},{12,28},{16,0},{20,4},{24,8},{28,12},{1,17},{... | collective-permute-start | bytes 1769480 | tf_op jit(solution)/shard_map/ppermute | solution.py:24
  692.0 31.6 %collective-permute-start.71 = (bf16[4,96,384]{2,1,0:T(8,128)(2,1)S(1)}, bf16[4,96,384]{2,1,0:T(8,128)(2,1)S(1)}, u32[]{:S(2)}, u32[]{:S(2)}) collective-permute-start(bf16[4,96,384]{2,1,0:T(8,128)(2,1)S(1)} %dynamic-slice_bitcast_fusion.21), channel_id=1, source_target_pairs={{0,16},{4,20},{8,24},{12,28},{16,0},{20,4},{24,8},{28,12},{1,17},{... | collective-permute-start | bytes 884744 | tf_op jit(solution)/shard_map/ppermute | solution.py:24
  700.4 24.5 %collective-permute-start.73 = (bf16[4,96,384]{2,1,0:T(8,128)(2,1)S(1)}, bf16[4,96,384]{2,1,0:T(8,128)(2,1)S(1)}, u32[]{:S(2)}, u32[]{:S(2)}) collective-permute-start(bf16[4,96,384]{2,1,0:T(8,128)(2,1)S(1)} %dynamic-slice_bitcast_fusion.20), channel_id=1, source_target_pairs={{0,8},{4,12},{8,0},{12,4},{16,24},{20,28},{24,16},{28,20},{1,9},{5... | collective-permute-start | bytes 884744 | tf_op jit(solution)/shard_map/ppermute | solution.py:24
  704.7 25.3 %collective-permute-start.58 = (bf16[4,96,384]{2,1,0:T(8,128)(2,1)S(1)}, bf16[4,96,384]{2,1,0:T(8,128)(2,1)S(1)}, u32[]{:S(2)}, u32[]{:S(2)}) collective-permute-start(bf16[4,96,384]{2,1,0:T(8,128)(2,1)S(1)} %dynamic-slice_bitcast_fusion.23), channel_id=1, source_target_pairs={{0,16},{4,20},{8,24},{12,28},{16,0},{20,4},{24,8},{28,12},{1,17},{... | collective-permute-start | bytes 884744 | tf_op jit(solution)/shard_map/ppermute | solution.py:24
  713.0 18.2 %collective-permute-start.60 = (bf16[4,96,384]{2,1,0:T(8,128)(2,1)S(1)}, bf16[4,96,384]{2,1,0:T(8,128)(2,1)S(1)}, u32[]{:S(2)}, u32[]{:S(2)}) collective-permute-start(bf16[4,96,384]{2,1,0:T(8,128)(2,1)S(1)} %dynamic-slice_bitcast_fusion.22), channel_id=1, source_target_pairs={{0,8},{4,12},{8,0},{12,4},{16,24},{20,28},{24,16},{28,20},{1,9},{5... | collective-permute-start | bytes 884744 | tf_op jit(solution)/shard_map/ppermute | solution.py:24
  717.3 19.0 %collective-permute-start.107 = (bf16[4,96,384]{2,1,0:T(8,128)(2,1)S(1)}, bf16[4,96,384]{2,1,0:T(8,128)(2,1)S(1)}, u32[]{:S(2)}, u32[]{:S(2)}) collective-permute-start(bf16[4,96,384]{2,1,0:T(8,128)(2,1)S(1)} %dynamic-slice_bitcast_fusion.17), channel_id=1, source_target_pairs={{0,16},{4,20},{8,24},{12,28},{16,0},{20,4},{24,8},{28,12},{1,17},{... | collective-permute-start | bytes 884744 | tf_op jit(solution)/shard_map/ppermute | solution.py:24
  724.9 17.7 %collective-permute-start.94 = (bf16[4,96,384]{2,1,0:T(8,128)(2,1)S(1)}, bf16[4,96,384]{2,1,0:T(8,128)(2,1)S(1)}, u32[]{:S(2)}, u32[]{:S(2)}) collective-permute-start(bf16[4,96,384]{2,1,0:T(8,128)(2,1)S(1)} %dynamic-slice_bitcast_fusion.19), channel_id=1, source_target_pairs={{0,16},{4,20},{8,24},{12,28},{16,0},{20,4},{24,8},{28,12},{1,17},{... | collective-permute-start | bytes 884744 | tf_op jit(solution)/shard_map/ppermute | solution.py:24
  798.1 22.5 %collective-permute-start.79 = (bf16[96,768]{1,0:T(8,128)(2,1)S(1)}, bf16[96,768]{1,0:T(8,128)(2,1)S(1)}, u32[]{:S(2)}, u32[]{:S(2)}) collective-permute-start(bf16[96,768]{1,0:T(8,128)(2,1)S(1)} %fusion.194), channel_id=1, source_target_pairs={{0,16},{4,20},{8,24},{12,28},{16,0},{20,4},{24,8},{28,12},{1,17},{... | collective-permute-start | bytes 442376 | tf_op jit(solution)/shard_map/ppermute | solution.py:24
  807.5 18.3 %collective-permute-start.115 = (bf16[96,768]{1,0:T(8,128)(2,1)S(1)}, bf16[96,768]{1,0:T(8,128)(2,1)S(1)}, u32[]{:S(2)}, u32[]{:S(2)}) collective-permute-start(bf16[96,768]{1,0:T(8,128)(2,1)S(1)} %fusion.188), channel_id=1, source_target_pairs={{0,16},{4,20},{8,24},{12,28},{16,0},{20,4},{24,8},{28,12},{1,17},{... | collective-permute-start | bytes 442376 | tf_op jit(solution)/shard_map/ppermute | solution.py:24
  (352 other events, 3333.5 us)

commit v2 on v1

--- a/solution.py
+++ b/solution.py
@@ -1,8 +1,11 @@
+import functools
 import math
 
 import jax
 import jax.numpy as jnp
 from jax import lax
+from jax.experimental import pallas as pl
+from jax.experimental.pallas import tpu as pltpu
 from jax.sharding import PartitionSpec as P
 
 HEAD_DIM = 64
@@ -15,8 +18,339 @@
 F32 = jnp.float32
 BF16 = jnp.bfloat16
 
-CORE, XBIT, YBIT = 1, 2, 4
-GROUP = 8
+
+ANY = pl.BlockSpec(memory_space=pl.ANY)
+
+def place():
+    d = lax.axis_index("dp")
+    z = lax.axis_index("mp")
+    nz = lax.axis_size("mp")
+    core, px, py = d % 2, (d // 2) % 2, (d // 4) % 2
+    peers = {
+        "core": {"dp": d + 1 - 2 * core},
+        "x": {"dp": d + 2 - 4 * px},
+        "y": {"dp": d + 4 - 8 * py},
+        "up": {"mp": lax.rem(z + 1, nz)},
+        "down": {"mp": lax.rem(z + nz - 1, nz)},
+    }
+    return core, px, py, peers
+
+def greet(names, peers):
+    sem = pltpu.get_barrier_semaphore()
+    for n in names:
+        pl.semaphore_signal(sem, inc=1, device_id=peers[n], device_id_type=pl.DeviceIdType.MESH)
+    pl.semaphore_wait(sem, len(names))
+
+def spot(core, px, py):
+    return core * 4 + py * 2 + px
+
+def gather_kernel(kinds, ways, srcs, out, z_send, z_recv, p_send, p_recv, own_send, own_recv):
+    core, px, py, peers = place()
+    rows = out.shape[2] // 8
+    part = out.shape[2] // ways
+
+    def region(g, k, slot, lo=0, n=None):
+        n = rows if n is None else n
+        if kinds[g][2]:
+            return out.at[g, slot // 2, pl.ds(pl.multiple_of(k * part + (slot % 2) * rows + lo, 16), n)]
+        return out.at[g, k, pl.ds(pl.multiple_of(slot * rows + lo, 16), n)]
+
+    def source(g):
+        ref, layer, _ = kinds[g]
+        return srcs[ref].at[layer]
+
+    me = spot(core, px, py)
+    slot_x, slot_y, slot_d = spot(core, 1 - px, py), spot(core, px, 1 - py), spot(core, 1 - px, 1 - py)
+    other = spot(1 - core, px, py)
+
+    def remote(src, dst, sems, index, peer):
+        return pltpu.make_async_remote_copy(
+            src_ref=src, dst_ref=dst, send_sem=sems[0].at[index], recv_sem=sems[1].at[index],
+            device_id=peers[peer], device_id_type=pl.DeviceIdType.MESH)
+
+    zs, ps = (z_send, z_recv), (p_send, p_recv)
+    started = []
+
+    def go(copy):
+        copy.start()
+        started.append(copy)
+
+    def z_copy(g, k):
+        src = source(g).at[pl.ds(pl.multiple_of(me * rows, 16), rows)] if k == 1 else region(g, k - 1, me)
+        return remote(src, region(g, k, me), zs, g * (ways - 1) + k - 1, "up")
+
+    half = rows // 2
+    plane = [
+        ("x", me, slot_x, 0, rows),
+        ("y", me, slot_y, 0, rows),
+        ("y", slot_x, slot_d, 0, half),
+        ("x", slot_y, slot_d, half, half),
+        ("core", me, other, 0, rows),
+        ("core", slot_x, spot(1 - core, 1 - px, py), 0, rows),
+        ("core", slot_y, spot(1 - core, px, 1 - py), 0, rows),
+        ("core", slot_d, spot(1 - core, 1 - px, 1 - py), 0, rows),
+    ]
+    count = len(plane)
+
+    def p_copy(g, k, i, received=False):
+        peer, sent, got, lo, n = plane[i]
+        slot = got if received else sent
+        reg = region(g, k, slot, lo, n)
+        return remote(reg, reg, ps, (g * (ways - 1) + k - 1) * count + i, peer)
+
+    groups = len(kinds)
+    def own_copy(g, m):
+        if kinds[g][2]:
+            src, dst = source(g).at[pl.ds(m * part, part)], out.at[g, m, pl.ds(0, part)]
+        else:
+            src, dst = source(g), out.at[g, 0]
+        return remote(src, dst, (own_send, own_recv), g * 4 + m, "core")
+
+    own = [(g, m) for g in range(groups) for m in range(4 if kinds[g][2] else 1)]
+    greet(("core", "x", "y", "up", "down"), peers)
+    work = [(g, k) for g in range(groups) for k in range(1, ways)]
+    go(z_copy(0, 1))
+    for item in own:
+        go(own_copy(*item))
+
+    def second(g, k):
+        p_copy(g, k, 0, True).wait_recv()
+        go(p_copy(g, k, 2)); go(p_copy(g, k, 5))
+        p_copy(g, k, 1, True).wait_recv()
+        go(p_copy(g, k, 3)); go(p_copy(g, k, 6))
+
+    def third(g, k):
+        p_copy(g, k, 2, True).wait_recv()
+        p_copy(g, k, 3, True).wait_recv()
+        go(p_copy(g, k, 7))
+
+    lag2, lag3 = 1, 2
+    for i in range(len(work) + lag3):
+        if i < len(work):
+            g, k = work[i]
+            z_copy(g, k).wait_recv()
+            if k + 1 < ways:
+                go(z_copy(g, k + 1))
+            elif g + 1 < groups:
+                go(z_copy(g + 1, 1))
+            go(p_copy(g, k, 0)); go(p_copy(g, k, 1)); go(p_copy(g, k, 4))
+        if 0 <= i - lag2 < len(work):
+            second(*work[i - lag2])
+        if 0 <= i - lag3 < len(work):
+            third(*work[i - lag3])
+    for g, k in work:
+        for i in range(4, 8):
+            p_copy(g, k, i, True).wait_recv()
+    for c in started:
+        c.wait_send()
+    for item in own:
+        own_copy(*item).wait_recv()
+
+def gather_weights(sources, kinds, ways, collective_id):
+    width = sources[0].shape[-1]
+    rows = sources[0].shape[-2]
+    groups = len(kinds)
+    n = groups * (ways - 1)
+    def kern(*refs):
+        gather_kernel(kinds, ways, refs[:len(sources)], *refs[len(sources):])
+    return pl.pallas_call(
+        kern,
+        out_shape=jax.ShapeDtypeStruct((groups, ways, rows, width), BF16),
+        in_specs=[ANY] * len(sources), out_specs=ANY,
+        scratch_shapes=[pltpu.SemaphoreType.DMA((n,)), pltpu.SemaphoreType.DMA((n,)),
+                        pltpu.SemaphoreType.DMA((n * 8,)), pltpu.SemaphoreType.DMA((n * 8,)),
+                        pltpu.SemaphoreType.DMA((groups * 4,)), pltpu.SemaphoreType.DMA((groups * 4,))],
+        compiler_params=pltpu.CompilerParams(collective_id=collective_id, has_side_effects=True),
+        name="gather_weights",
+    )(*sources)
+
+
+def add_low(a, b):
+    return (a.astype(F32) + b.astype(F32)).astype(BF16)
+
+def far_peers(names):
+    d = lax.axis_index("dp")
+    found = {}
+    bit = 8
+    while bit < lax.axis_size("dp"):
+        high = (d // bit) % 2
+        found[f"far{bit}"] = {"dp": d + bit - 2 * bit * high}
+        bit *= 2
+    return found
+
+def reduce_kernel(attn, ways, grads, out, own, got, got_a, got_b, got_c, got_d, mix, zin, zout, far,
+                  l_sem, r_send, r_recv, g_send, g_recv):
+    core, px, py, peers = place()
+    extra = far_peers(None)
+    peers.update(extra)
+    groups = len(attn)
+    rows = out.shape[1] // 8
+    half = rows // 2
+    def remote(src, dst, sems, index, peer):
+        return pltpu.make_async_remote_copy(
+            src_ref=src, dst_ref=dst, send_sem=sems[0].at[index], recv_sem=sems[1].at[index],
+            device_id=peers[peer], device_id_type=pl.DeviceIdType.MESH)
+    rs, gs = (r_send, r_recv), (g_send, g_recv)
+    per = 6 + ways - 1 + len(extra)
+    started = []
+    def go(c):
+        c.start(); started.append(c)
+
+    def share(g, c, j):
+        ref = grads[g]
+        return ref.at[2 * c + j] if attn[g] else ref.at[:, 2 * c + j]
+
+    def load(g, j):
+        return pltpu.make_async_copy(share(g, core, j), own.at[g, :, j], l_sem.at[g * 2 + j])
+    def core_copy(g, j):
+        return remote(share(g, 1 - core, j), got.at[g, :, j], rs, g * per + j, "core")
+    def a1(g):
+        return remote(own.at[g, :, :, pl.ds((1 - px) * rows, half)], got_a.at[g], rs, g * per + 2, "x")
+    def b1(g):
+        return remote(mix.at[g, :, 1 - py], got_b.at[g], rs, g * per + 3, "y")
+    def a2(g):
+        return remote(got_a.at[g, :, 1 - py], got_c.at[g], rs, g * per + 4, "y")
+    def b2(g):
+        return remote(got_b.at[g, :, pl.ds((1 - px) * half, half)], got_d.at[g], rs, g * per + 5, "x")
+    def zc(g, s):
+        return remote(zout.at[g, s - 1], zin.at[g, s - 1], rs, g * per + 5 + s, "up")
+    def fc(g, i, name):
+        return remote(zout.at[g, ways - 1 + i], far.at[g, i], rs, g * per + 5 + ways + i, name)
+
+    last = ways - 1 + len(extra)
+    me = spot(core, px, py)
+    slot_x, slot_y, slot_d = spot(core, 1 - px, py), spot(core, px, 1 - py), spot(core, 1 - px, 1 - py)
+    plane = [
+        ("x", me, slot_x, 0, rows), ("y", me, slot_y, 0, rows),
+        ("y", slot_x, slot_d, 0, half), ("x", slot_y, slot_d, half, half),
+        ("core", me, spot(1 - core, px, py), 0, rows),
+        ("core", slot_x, spot(1 - core, 1 - px, py), 0, rows),
+        ("core", slot_y, spot(1 - core, px, 1 - py), 0, rows),
+        ("core", slot_d, spot(1 - core, 1 - px, 1 - py), 0, rows),
+    ]
+    def pc(g, i, received=False):
+        peer, sent, got_slot, lo, n = plane[i]
+        slot = got_slot if received else sent
+        dst = out.at[g, pl.ds(pl.multiple_of(slot * rows + lo, 16), n)]
+        src = zout.at[g, last] if sent is me else dst
+        return remote(src, dst, gs, g * 8 + i, peer)
+    def mine_out(g):
+        return pltpu.make_async_copy(zout.at[g, last], out.at[g, pl.ds(pl.multiple_of(me * rows, 16), rows)], l_sem.at[groups * 2 + g])
+
+    def s0(g):
+        for j in range(2):
+            load(g, j).start()
+            go(core_copy(g, j))
+    def s1(g):
+        for j in range(2):
+            load(g, j).wait()
+            core_copy(g, j).wait_recv()
+        def body(k, _):
+            for j in range(2):
+                for x in range(2):
+                    lo = slice(x * rows, x * rows + half)
+                    own[g, k, j, lo] = add_low(own[g, k, j, lo], got[g, k, j, lo])
+                    hi = slice(x * rows + half, (x + 1) * rows)
+                    mix[g, k, j, x * half:(x + 1) * half] = add_low(own[g, k, j, hi], got[g, k, j, hi])
+            return 0
+        lax.fori_loop(0, ways, body, 0)
+        go(a1(g)); go(b1(g))
+    def s2(g):
+        a1(g).wait_recv()
+        def body(k, _):
+            for j in range(2):
+                got_a[g, k, j] = add_low(own[g, k, j, pl.ds(pl.multiple_of(px * rows, 16), half)], got_a[g, k, j])
+            return 0
+        lax.fori_loop(0, ways, body, 0)
+        go(a2(g))
+        b1(g).wait_recv()
+        def body(k, _):
+            got_b[g, k] = add_low(mix[g, k, py], got_b[g, k])
+            return 0
+        lax.fori_loop(0, ways, body, 0)
+        go(b2(g))
+    def part(g, k):
+        left = add_low(got_a[g, k, py], got_c[g, k])
+        right = add_low(got_b[g, k, pl.ds(pl.multiple_of(px * half, 16), half)], got_d[g, k])
+        return left, right
+    def s3(g):
+        a2(g).wait_recv(); b2(g).wait_recv()
+        left, right = part(g, 1)
+        zout[g, 0, :half] = left
+        zout[g, 0, half:] = right
+        go(zc(g, 1))
+    def sz(g, s):
+        zc(g, s).wait_recv()
+        left, right = part(g, (s + 1) % ways)
+        zout[g, s, :half] = add_low(zin[g, s - 1, :half], left)
+        zout[g, s, half:] = add_low(zin[g, s - 1, half:], right)
+        if s < ways - 1:
+            go(zc(g, s + 1))
+    def sfar(g):
+        for i, name in enumerate(extra):
+            go(fc(g, i, name))
+            fc(g, i, name).wait_recv()
+            zout[g, ways + i] = add_low(zout[g, ways - 1 + i], far[g, i])
+    def sp(g):
+        sz(g, ways - 1)
+        sfar(g)
+        mine_out(g).start()
+        for i in (0, 1, 4):
+            go(pc(g, i))
+    def sq(g):
+        pc(g, 0, True).wait_recv()
+        go(pc(g, 2)); go(pc(g, 5))
+        pc(g, 1, True).wait_recv()
+        go(pc(g, 3)); go(pc(g, 6))
+    def sr(g):
+        pc(g, 2, True).wait_recv()
+        pc(g, 3, True).wait_recv()
+        go(pc(g, 7))
+    stages = [s1, s2, s3] + [functools.partial(lambda s, g: sz(g, s), s) for s in range(1, ways - 1)] + [sp, sq, sr]
+    greet(("core", "x", "y", "up", "down") + tuple(extra), peers)
+    for g in range(groups):
+        s0(g)
+    for wave in range(groups + len(stages) - 1):
+        for s in range(len(stages)):
+            g = wave - s
+            if 0 <= g < groups:
+                stages[s](g)
+    for g in range(groups):
+        for i in range(4, 8):
+            pc(g, i, True).wait_recv()
+        mine_out(g).wait()
+    for c in started:
+        c.wait_send()
+
+def reduce_gradients(grads, attn, ways, collective_id):
+    groups = len(grads)
+    quarter, width = grads[0].shape[2:]
+    R = quarter * 4
+    rows = R // 8
+    half = rows // 2
+    nfar = 0
+    while 8 << nfar < lax.axis_size("dp"):
+        nfar += 1
+    per = 6 + ways - 1 + nfar
+    def kern(*refs):
+        reduce_kernel(attn, ways, refs[:groups], *refs[groups:])
+    V = lambda *s: pltpu.VMEM(s, BF16)
+    return pl.pallas_call(
+        kern,
+        out_shape=jax.ShapeDtypeStruct((groups, R, width), BF16),
+        in_specs=[ANY] * groups, out_specs=ANY,
+        scratch_shapes=[V(groups, ways, 2, 2 * rows, width), V(groups, ways, 2, 2 * rows, width),
+                        V(groups, ways, 2, half, width), V(groups, ways, 2 * half, width),
+                        V(groups, ways, half, width), V(groups, ways, half, width),
+                        V(groups, ways, 2, 2 * half, width),
+                        V(groups, ways - 1, rows, width), V(groups, ways + nfar, rows, width),
+                        V(groups, max(nfar, 1), rows, width),
+                        pltpu.SemaphoreType.DMA((groups * 3,)),
+                        pltpu.SemaphoreType.DMA((groups * per,)), pltpu.SemaphoreType.DMA((groups * per,)),
+                        pltpu.SemaphoreType.DMA((groups * 8,)), pltpu.SemaphoreType.DMA((groups * 8,))],
+        compiler_params=pltpu.CompilerParams(collective_id=collective_id, has_side_effects=True, vmem_limit_bytes=60 << 20),
+        name="reduce_gradients",
+    )(*grads)
 
 
 def flip(value, bit):
@@ -34,80 +368,8 @@
     return lax.ppermute(value, "mp", [(i, (i + 1) % size) for i in range(size)])
 
 
-def spots():
-    index = lax.axis_index("dp")
-    return index % 2, (index // 2) % 2, (index // 4) % 2
-
-
 def swap_if(cond, first, second):
     return jnp.where(cond, second, first), jnp.where(cond, first, second)
-
-
-def gather_plane(piece):
-    core, px, py = spots()
-    half = piece.shape[-2] // 2
-    along_x = flip(piece, XBIT)
-    along_y = flip(piece, YBIT)
-    diag_a = flip(along_x[..., :half, :], YBIT)
-    diag_b = flip(along_y[..., half:, :], XBIT)
-    diag = jnp.concatenate([diag_a, diag_b], axis=-2)
-    q0, q1 = swap_if(px == 1, piece, along_x)
-    q2, q3 = swap_if(px == 1, along_y, diag)
-    low = jnp.concatenate([q0, q1], axis=-2)
-    high = jnp.concatenate([q2, q3], axis=-2)
-    low, high = swap_if(py == 1, low, high)
-    mine = jnp.concatenate([low, high], axis=-2)
-    other = flip(mine, CORE)
-    first, second = swap_if(core == 1, mine, other)
-    return jnp.concatenate([first, second], axis=-2)
-
-
-def gather_weights(shard):
-    core, px, py = spots()
-    rows = shard.shape[0] // GROUP
-    mine = lax.dynamic_slice_in_dim(shard, (core * 4 + py * 2 + px) * rows, rows)
-    pieces = []
-    current = mine
-    for _ in range(lax.axis_size("mp") - 1):
-        current = ring(current)
-        pieces.append(current)
-    foreign = gather_plane(jnp.stack(pieces))
-    return jnp.concatenate([shard[None], foreign])
-
-
-def add_low(left, right):
-    return (left.astype(F32) + right.astype(F32)).astype(BF16)
-
-
-def pick(value, axis, index):
-    return lax.dynamic_index_in_dim(value, index, axis=axis, keepdims=False)
-
-
-def reduce_gradient(grad):
-    core, px, py = spots()
-    ways, rows, width = grad.shape
-    split = width // 2
-    blocks = grad.reshape(ways, 2, 2, 2, rows // GROUP, width)
-    got = flip(pick(blocks, 1, 1 - core), CORE)
-    blocks = add_low(pick(blocks, 1, core), got)
-    left, right = blocks[..., :split], blocks[..., split:]
-    got_left = flip(pick(left, 2, 1 - px), XBIT)
-    got_right = flip(pick(right, 1, 1 - py), YBIT)
-    left = add_low(pick(left, 2, px), got_left)
-    right = add_low(pick(right, 1, py), got_right)
-    got_left = flip(pick(left, 1, 1 - py), YBIT)
-    got_right = flip(pick(right, 1, 1 - px), XBIT)
-    left = add_low(pick(left, 1, py), got_left)
-    right = add_low(pick(right, 1, px), got_right)
-    block = jnp.concatenate([left, right], axis=-1)
-    total = block[1]
-    for step in range(2, ways + 1):
-        total = add_low(ring(total), block[step % ways])
-    bit = GROUP
-    while bit < lax.axis_size("dp"):
-        total = add_low(total, flip(total, bit))
-        bit *= 2
-    return gather_plane(total).astype(F32)
 
 
 def gather_all(rows):
@@ -211,14 +473,10 @@
 
 
 def layer_forward(x, attn_w, up_w, down_w, small, shapes, lengths):
-    ways, rows, width = attn_w.shape
-    part = rows // 4
+    width = x.shape[-1]
     xr = x.astype(BF16)
     tokens = x.shape[0]
-    q, k, v = (
-        mm("td,zkd->tzk", xr, attn_w[:, i * part : (i + 1) * part]).reshape(tokens, -1)
-        for i in range(3)
-    )
+    q, k, v = (mm("td,kd->tk", xr, attn_w[i]) for i in range(3))
     q = (q + small["q_bias"]).astype(BF16)
     k = k.astype(BF16)
     v = (v + small["v_bias"]).astype(BF16)
@@ -230,7 +488,7 @@
         contexts.append(context)
         logs.append(log_total)
     ctx = unbucket(contexts)
-    attn = mm("tc,cd->td", ctx, attn_w[:, 3 * part :].reshape(-1, width)) + small["out_bias"]
+    attn = mm("tc,cd->td", ctx, attn_w[3]) + small["out_bias"]
     h, n1, r1 = norm_forward(x + attn, small["gain"][0], small["bias"][0])
     hr = h.astype(BF16)
     u = mm("td,zdk->tzk", hr, up_w).reshape(tokens, -1) + small["up_bias"]
@@ -242,9 +500,8 @@
 
 def layer_backward(dy, saved, attn_w, up_w, down_w, small, shapes, lengths):
     xr, q, k, v, logs, ctx, n1, r1, hr, u, a, n2, r2 = saved
-    ways, rows, width = attn_w.shape
-    part = rows // 4
-    tokens = dy.shape[0]
+    ways = up_w.shape[0]
+    tokens, width = dy.shape
     dz2, gain_two, bias_two = norm_backward(dy, n2, r2, small["gain"][1])
     df = dz2.astype(BF16)
     down_b = jnp.sum(df, axis=0, dtype=F32)
@@ -259,8 +516,8 @@
     dz1, gain_one, bias_one = norm_backward(dh, n1, r1, small["gain"][0])
     dattn = dz1.astype(BF16)
     out_b = jnp.sum(dattn, axis=0, dtype=F32)
-    out_g = mm("tzk,td->zkd", ctx.reshape(tokens, ways, -1), dattn)
-    dctx = mm("td,cd->tc", dattn, attn_w[:, 3 * part :].reshape(-1, width)).astype(BF16)
+    out_g = mm("tk,td->kd", ctx, dattn)
+    dctx = mm("td,cd->tc", dattn, attn_w[3]).astype(BF16)
     grads = ([], [], [])
     for qs, ks, vs, lens, log_total, gs in zip(
         buckets(q, shapes),
@@ -272,14 +529,13 @@
     ):
         for store, value in zip(grads, attention_backward(qs, ks, vs, lens, log_total, gs)):
             store.append(value)
-    dq, dk, dv = (unbucket(store).reshape(tokens, ways, -1) for store in grads)
-    attn_g = jnp.concatenate(
-        [mm("tzk,td->zkd", dq, xr), mm("tzk,td->zkd", dk, xr), mm("tzk,td->zkd", dv, xr), out_g],
-        axis=1,
+    dq, dk, dv = (unbucket(store) for store in grads)
+    attn_g = jnp.stack(
+        [mm("tk,td->kd", dq, xr), mm("tk,td->kd", dk, xr), mm("tk,td->kd", dv, xr), out_g]
     ).astype(BF16)
     dx = dz1
     for i, grad in enumerate((dq, dk, dv)):
-        dx = dx + mm("tzk,zkd->td", grad, attn_w[:, i * part : (i + 1) * part])
+        dx = dx + mm("tk,kd->td", grad, attn_w[i])
     qv_b = jnp.stack(
         [jnp.sum(dq, axis=0, dtype=F32).reshape(-1), jnp.sum(dv, axis=0, dtype=F32).reshape(-1)]
     )
@@ -335,11 +591,12 @@
     tiny_all = jnp.stack(tiny_all).astype(F32)
 
     weights = []
+    qkv_t = jnp.swapaxes(query_key_value_matrix, 2, 3).reshape(layers, 3 * part, width)
+    attn_pack = jnp.concatenate([qkv_t, out_weight], axis=1)
+    kinds = tuple((i, l, i == 0) for l in range(layers) for i in range(3))
+    gathered = gather_weights((attn_pack, up_matrix, down_matrix), kinds, ways, 0)
     for l in range(layers):
-        qkv_t = jnp.swapaxes(query_key_value_matrix[l], 1, 2).reshape(3 * part, width)
-        attn_w = gather_weights(jnp.concatenate([qkv_t, out_weight[l]]))
-        up_w = gather_weights(up_matrix[l])
-        down_w = gather_weights(down_matrix[l])
+        attn_w, up_w, down_w = (gathered[3 * l + i] for i in range(3))
         small = {
             "q_bias": tiny_all[:, 2 * l].reshape(-1),
             "v_bias": tiny_all[:, 2 * l + 1].reshape(-1),
@@ -408,7 +665,8 @@
         dy, big, (qv_b, up_b, shared) = layer_backward(
             dy, kept[l], *weights[l], shapes, lengths
         )
-        summed[l] = tuple(reduce_gradient(item) for item in big)
+        big = [item.reshape(4, 4, -1, width) for item in (big[2], big[1], big[0])]
+        summed[l] = reduce_gradients(big, (False, False, True), ways, 1 + l).astype(F32)
         qv_abs = to_absolute(qv_b.reshape(2, ways, part)).reshape(-1)
         up_abs = to_absolute(up_b.reshape(ways, -1)).reshape(-1)
         flat = jnp.concatenate([qv_abs, up_abs] + [item.reshape(-1) for item in shared])
@@ -416,11 +674,11 @@
 
     query_grad = dy[: q_slots * q_len].reshape(query_states.shape)
     passage_grad = dy[q_slots * q_len :].reshape(passage_states.shape)
-    attn_out = jnp.stack([s[0] for s in summed])
+    attn_out = jnp.stack([s[2] for s in summed])
     qkv_grad = jnp.swapaxes(attn_out[:, : 3 * part].reshape(layers, 3, part, width), 2, 3)
     out_grad = attn_out[:, 3 * part :]
     up_grad = jnp.stack([s[1] for s in summed])
-    down_grad = jnp.stack([s[2] for s in summed])
+    down_grad = jnp.stack([s[0] for s in summed])
     small_all = jnp.stack(smalls)
     hidden = up_bias.shape[-1]
     cut = lambda lo, hi: small_all[:, lo:hi]

time: 862 us -> 782 us (0.907)
  Pallas kernels: 0 us -> 311 us
  waiting for transfers between devices: 233 us -> 11.6 us
  starting transfers between devices: 132 us -> 19.2 us
  other arithmetic: 122 us -> 86.6 us
  local copies, waits for them, and re-layouts: 164 us -> 130 us
  matrix products: 193 us -> 209 us
    pallas_call x0 -> x3, Pallas kernels: none -> 311 us  [the longest x2 202 us: reduce_gradients(): pl.pallas_call(kern, out_shape=jax.ShapeDtypeStruct((groups, R, width), B...]
    ppermute x99 -> x9, waiting for transfers between devices: 160 us -> 5.48 us  [flip(): return lax.ppermute(value, 'dp', [(i, i ^ bit) for i in range(size)])]
    ppermute x99 -> x9, starting transfers between devices: 97 us -> 6.82 us  [flip(): return lax.ppermute(value, 'dp', [(i, i ^ bit) for i in range(size)])]
    ppermute x39 -> x3, waiting for transfers between devices: 71 us -> 3.57 us  [ring(): return lax.ppermute(value, 'mp', [(i, (i + 1) % size) for i in range(size)])]
    ppermute x39 -> x3, starting transfers between devices: 27.8 us -> 3.95 us  [ring(): return lax.ppermute(value, 'mp', [(i, (i + 1) % size) for i in range(size)])]
    dynamic_slice x16 -> x0, local copies, waits for them, and re-layouts: 20.7 us -> none  [the longest x12 20.6 us: pick(): return lax.dynamic_index_in_dim(value, index, axis=axis, keepdims=False)]
    select_n x44 -> x5, other arithmetic: 18.3 us -> 0.19 us  [swap_if(): return (jnp.where(cond, second, first), jnp.where(cond, first, second))]
    dot_general x60, matrix products: 191 us -> 207 us  [mm(): return jnp.einsum(spec, left, right, preferred_element_type=F32)]
  transfers between devices with their start and end apart: 144 -> 18, of which waited for: 69 -> 8; matrix products, arithmetic and copies ran while one was open for 28% -> 16% of each run, Pallas kernels for 0% -> 40%
where the time goes in v2:
time: 782 us; the launch traced here: 774 us
  Pallas kernels  311 us (40%)
  matrix products  209 us (27%)
  local copies, waits for them, and re-layouts  130 us (17%)
  other arithmetic  86.6 us (11%)
  starting transfers between devices  19.2 us (2%)
  waiting for transfers between devices  11.6 us (1%)
    dot_general x60, matrix products, mm(): return jnp.einsum(spec, left, right, preferred_element_type=F32)  207 us
    pallas_call x2, Pallas kernels, reduce_gradients(): pl.pallas_call(kern, out_shape=jax.ShapeDtypeStruct((groups, R, width), B...  202 us
    pallas_call x1, Pallas kernels, gather_weights(): pl.pallas_call(kern, out_shape=jax.ShapeDtypeStruct((groups, ways, rows,...  108 us
    unnamed x343, local copies, waits for them, and re-layouts  30.4 us
  transfers between devices with their start and end apart: 18, of which 8 were waited for; matrix products, arithmetic and copies ran while one was open for 16% of the time, Pallas kernels for 40%

profile of v2, /device:TPU:0, one launch (start us, length us, event | category | flops | bytes accessed | tf_op | source)
XLA Modules:
  0.0 773.7 jit_solution(5887675469489701732)
XLA Ops:
  2.1 3.1 collective-permute-start
  11.9 3.2 pad_maximum_fusion.4.refs_0_
  15.1 108.5 %gather_weights.1 = bf16[6,4,768,768]{3,2,1,0:T(8,128)(2,1)} custom-call(bf16[2,768,768]{2,1,0:T(8,128)(2,1)} %pad_maximum_fusion.4.refs_0_, bf16[2,768,768]{2,1,0:T(8,128)(2,1)} %refs_1_.1, bf16[2,768,768]{2,1,0:T(8,128)(2,1)} %refs_2_.1), custom_call_target="tpu_custom_call" | custom-call | tf_op jit(solution)/shard_map/gather_weights/pallas_call | solution.py:156
  123.7 14.5 %fusion.198 = (bf16[1,4,768,768]{3,2,1,0:T(8,128)(2,1)}, bf16[4,768,768]{1,2,0:T(8,128)(2,1)}, bf16[4,768,768]{1,2,0:T(8,128)(2,1)}, bf16[1,4,768,768]{3,2,1,0:T(8,128)(2,1)}) fusion(bf16[6,4,768,768]{3,2,1,0:T(8,128)(2,1)} %gather_weights.1), kind=kLoop, calls=%fused_computation.443 | loop fusion | bytes 37748736 | tf_op jit(solution)/shard_map/slice | solution.py:599
  146.9 3.6 collective-permute-done.1
  152.1 7.0 copy.79
  159.1 6.7 copy.86
  170.4 2.7 add_convert_fusion.3
  181.1 3.0 fusion.201
  186.0 2.6 copy-done
  191.2 2.9 fusion.203
  194.8 9.0 %multiply_convert_fusion.3 = (bf16[768,3072]{1,0:T(8,128)(2,1)S(1)}, f32[768,3072]{1,0:T(8,128)}) fusion(f32[3072]{0:T(1024)S(1)} %copy-done.110, bf16[3072,768]{1,0:T(8,128)(2,1)S(1)} %bitcast.398, f32[768,768]{1,0:T(8,128)S(1)} %get-tuple-element.137, f32[768]{0:T(1024)S(1)} %copy-done.116, f32[768]{0:T(1024)S(1)} %get-tuple-element.171, ...), kind=kOutput, calls=%fused_computation.34 | convolution fusion | flops 3640983552 | bytes 21258240 | tf_op jit(solution)/shard_map/td,zdk->tzk/dot_general | solution.py:432
  203.9 4.1 fusion.204
  209.2 2.8 add_convert_fusion
  213.1 2.8 add_convert_fusion.1
  229.5 3.0 fusion.205
  239.7 3.2 fusion.207
  243.6 8.7 %multiply_convert_fusion.2 = (bf16[768,3072]{1,0:T(8,128)(2,1)S(1)}, f32[768,3072]{1,0:T(8,128)}) fusion(f32[3072]{0:T(1024)S(1)} %copy-done.112, bf16[3072,768]{1,0:T(8,128)(2,1)S(1)} %bitcast.395, f32[768,768]{1,0:T(8,128)S(1)} %get-tuple-element.147, f32[768]{0:T(1024)S(1)} %copy-done.118, f32[768]{0:T(1024)S(1)} %copy-done.93, ...), kind=kOutput, calls=%fused_computation.32 | convolution fusion | flops 3640983552 | bytes 21258240 | tf_op jit(solution)/shard_map/td,zdk->tzk/dot_general | solution.py:432
  252.3 4.1 fusion.208
  266.7 3.3 collective-permute-start.4
  274.7 6.6 copy.144
  281.3 6.8 copy.146
  290.3 4.7 collective-permute-done.7
  310.7 10.9 %convert_reduce_fusion = (f32[3072]{0:T(1024)}, bf16[768,3072]{1,0:T(8,128)(2,1)S(1)}) fusion(f32[768,3072]{1,0:T(8,128)} %get-tuple-element.149, f32[3072]{0:T(1024)S(1)} %copy-done.113, bf16[3072,768]{1,0:T(8,128)(2,1)} %bitcast.387, f32[768,768]{1,0:T(8,128)S(1)} %get-tuple-element.89), kind=kOutput, calls=%fused_computation.30 | convolution fusion | flops 3655136256 | bytes 21258240 | tf_op jit(solution)/shard_map/td,kd->tk/dot_general | solution.py:432
  321.6 7.5 multiply_reduce_fusion.3
  329.1 6.4 fusion.41
  348.0 6.8 fusion.59
  358.4 5.9 multiply_reduce_fusion.1
  364.3 7.1 multiply_convert_fusion.1
  385.7 4.1 multiply_reduce_fusion.4
  391.3 10.9 %convert_reduce_fusion.1 = (f32[3072]{0:T(1024)}, bf16[768,3072]{1,0:T(8,128)(2,1)S(1)}) fusion(f32[768,3072]{1,0:T(8,128)} %get-tuple-element.139, f32[3072]{0:T(1024)S(1)} %copy-done.111, bf16[3072,768]{1,0:T(8,128)(2,1)S(1)} %bitcast.386, f32[768,768]{1,0:T(8,128)S(1)} %get-tuple-element.85), kind=kOutput, calls=%fused_computation.31 | convolution fusion | flops 3655136256 | bytes 21258240 | tf_op jit(solution)/shard_map/td,kd->tk/dot_general | solution.py:432
  402.2 7.5 multiply_reduce_fusion.5
  409.7 6.4 fusion.44
  427.3 6.8 fusion.62
  437.7 6.0 multiply_reduce_fusion
  443.8 7.4 multiply_convert_fusion
  456.9 3.8 fusion.99
  464.1 3.9 fusion.102
  469.9 7.8 %convolution_convert_fusion = bf16[4,768,768]{2,1,0:T(8,128)(2,1)} fusion(bf16[768,4,768]{0,2,1:T(8,128)(2,1)} %bitcast.392, f32[768,768]{1,0:T(8,128)S(1)} %copy-done.32), kind=kOutput, calls=%fused_computation.69 | convolution fusion | flops 3626827776 | bytes 11796480 | tf_op jit(solution)/shard_map/tzk,td->zkd/dot_general | solution.py:432
  494.4 9.3 %convolution_convert_fusion.1 = bf16[4,768,768]{2,1,0:T(8,128)(2,1)} fusion(bf16[768,4,768]{0,2,1:T(8,128)(2,1)} %bitcast.391, f32[768,768]{1,0:T(8,128)} %copy-done.34), kind=kOutput, calls=%fused_computation.70 | convolution fusion | flops 3626827776 | bytes 11796480 | tf_op jit(solution)/shard_map/tzk,td->zkd/dot_general | solution.py:432
  504.3 3.3 rev.15
  513.5 3.7 pad_maximum_fusion.1.refs_2_
  517.3 100.5 %reduce_gradients.3 = bf16[3,768,768]{2,1,0:T(8,128)(2,1)} custom-call(bf16[4,4,192,768]{3,2,1,0:T(8,128)(2,1)} %bitcast.401, bf16[4,4,192,768]{3,2,1,0:T(8,128)(2,1)} %bitcast.399, bf16[4,4,192,768]{3,2,1,0:T(8,128)(2,1)} %pad_maximum_fusion.1.refs_2_), custom_call_target="tpu_custom_call" | custom-call | tf_op jit(solution)/shard_map/reduce_gradients/pallas_call | solution.py:338
  617.7 4.8 fusion.200
  635.1 4.1 pad_maximum_fusion.refs_2_
  639.2 101.8 %reduce_gradients.2 = bf16[3,768,768]{2,1,0:T(8,128)(2,1)} custom-call(bf16[4,4,192,768]{3,2,1,0:T(8,128)(2,1)} %bitcast.402, bf16[4,4,192,768]{3,2,1,0:T(8,128)(2,1)} %bitcast.400, bf16[4,4,192,768]{3,2,1,0:T(8,128)(2,1)} %pad_maximum_fusion.refs_2_), custom_call_target="tpu_custom_call" | custom-call | tf_op jit(solution)/shard_map/reduce_gradients/pallas_call | solution.py:338
  741.0 2.7 fusion.199
  763.8 2.6 collective-permute-start.12
  (620 shorter events, 208.0 us)
Async XLA Ops:
  2.1 142.9 %collective-permute-start = (bf16[12,192]{1,0:T(8,128)(2,1)S(1)}, bf16[12,192]{1,0:T(8,128)(2,1)S(1)}, u32[]{:S(2)}, u32[]{:S(2)}) collective-permute-start(bf16[12,192]{1,0:T(8,128)(2,1)S(1)} %get-tuple-element.127), channel_id=1, source_target_pairs={{0,1},{1,2},{2,3},{3,0},{4,5},{5,6},{6,7},{7,4},{8,9},{9,10},{10,1... | collective-permute-start | bytes 13832 | tf_op jit(solution)/shard_map/ppermute | solution.py:368
  123.6 14.6 %copy-start.138 = (s32[2]{0:T(128)S(1)}, s32[2]{0:T(128)}, u32[]{:S(2)}) copy-start(s32[2]{0:T(128)} %param.25) | copy-start | bytes 28
  123.6 17.0 %copy-start.130 = (bf16[1,512,768]{2,1,0:T(8,128)(2,1)S(1)}, bf16[1,512,768]{2,1,0:T(8,128)(2,1)}, u32[]{:S(2)}) copy-start(bf16[1,512,768]{2,1,0:T(8,128)(2,1)} %param.20) | copy-start | bytes 2359300
  123.6 17.0 %copy-start.134 = (bf16[2,128,768]{2,1,0:T(8,128)(2,1)S(1)}, bf16[2,128,768]{2,1,0:T(8,128)(2,1)}, u32[]{:S(2)}) copy-start(bf16[2,128,768]{2,1,0:T(8,128)(2,1)} %param.19) | copy-start | bytes 1179652
  140.0 116.9 %copy-start.74 = (f32[768]{0:T(1024)}, f32[768]{0:T(1024)S(1)}, u32[]{:S(2)}) copy-start(f32[768]{0:T(1024)S(1)} %get-tuple-element.174) | copy-start | bytes 9220
  140.6 63.2 %copy-start.91 = (f32[768]{0:T(1024)}, f32[768]{0:T(1024)S(1)}, u32[]{:S(2)}) copy-start(f32[768]{0:T(1024)S(1)} %get-tuple-element.171) | copy-start | bytes 9220
  140.6 98.9 %copy-start.72 = (f32[768]{0:T(1024)}, f32[768]{0:T(1024)S(1)}, u32[]{:S(2)}) copy-start(f32[768]{0:T(1024)S(1)} %get-tuple-element.172) | copy-start | bytes 9220
  145.0 5.5 collective-permute-start.1
  150.5 15.3 %collective-permute-start.2 = (bf16[12,192]{1,0:T(8,128)(2,1)S(1)}, bf16[12,192]{1,0:T(8,128)(2,1)S(1)}, u32[]{:S(2)}, u32[]{:S(2)}) collective-permute-start(bf16[12,192]{1,0:T(8,128)(2,1)S(1)} %collective-permute-done.1), channel_id=1, source_target_pairs={{0,1},{1,2},{2,3},{3,0},{4,5},{5,6},{6,7},{7,4},{8,9},{9,10},{10,1... | collective-permute-start | bytes 13832 | tf_op jit(solution)/shard_map/ppermute | solution.py:368
  152.0 29.0 %copy-start.8 = (bf16[512,768]{0,1:T(8,128)(2,1)}, bf16[512,768]{0,1:T(8,128)(2,1)S(1)}, u32[]{:S(2)}) copy-start(bf16[512,768]{0,1:T(8,128)(2,1)S(1)} %slice.355) | copy-start | bytes 2359300
  152.1 25.6 %copy-start.36 = (bf16[2,128,12,64]{1,0,3,2:T(2,128)(2,1)}, bf16[2,128,12,64]{1,0,3,2:T(2,128)(2,1)S(1)}, u32[]{:S(2)}) copy-start(bf16[2,128,12,64]{1,0,3,2:T(2,128)(2,1)S(1)} %reshape.830) | copy-start | bytes 1179652
  173.2 12.8 %copy-start.27 = (bf16[512,768]{0,1:T(8,128)(2,1)}, bf16[512,768]{0,1:T(8,128)(2,1)S(1)}, u32[]{:S(2)}) copy-start(bf16[512,768]{0,1:T(8,128)(2,1)S(1)} %slice.353) | copy-start | bytes 2359300
  208.0 31.6 %copy-start.2 = (f32[768,768]{1,0:T(8,128)}, f32[768,768]{1,0:T(8,128)S(1)}, u32[]{:S(2)}) copy-start(f32[768,768]{1,0:T(8,128)S(1)} %get-tuple-element.141) | copy-start | bytes 7077892
  208.0 31.6 %copy-start.63 = (f32[768]{0:T(1024)}, f32[768]{0:T(1024)S(1)}, u32[]{:S(2)}) copy-start(f32[768]{0:T(1024)S(1)} %broadcast_multiply_fusion.14) | copy-start | bytes 9220
  208.5 31.1 %copy-start.76 = (f32[768]{0:T(1024)}, f32[768]{0:T(1024)S(1)}, u32[]{:S(2)}) copy-start(f32[768]{0:T(1024)S(1)} %add_rsqrt_fusion.2) | copy-start | bytes 9220
  239.7 12.6 %slice-start.10 = ((s8[4718592]{0:T(1024)(128)(4,1)}), s8[4194304]{0:T(1024)(128)(4,1)S(1)}, s32[]{:S(2)}) async-start(s8[4718592]{0:T(1024)(128)(4,1)} %bitcast.388), calls=%async_computation.10 | async-start | bytes 8388608
  259.4 15.3 %copy-start.81 = (f32[2,12,128]{2,1,0:T(8,128)S(1)}, f32[2,12,128]{2,1,0:T(8,128)}, u32[]{:S(2)}) copy-start(f32[2,12,128]{2,1,0:T(8,128)} %copy-done.80) | copy-start | bytes 36868
  259.4 15.3 %copy-start.83 = (f32[2,12,128]{2,1,0:T(8,128)S(1)}, f32[2,12,128]{2,1,0:T(8,128)}, u32[]{:S(2)}) copy-start(f32[2,12,128]{2,1,0:T(8,128)} %copy-done.82) | copy-start | bytes 36868
  259.6 21.7 %copy-start.67 = (f32[768]{0:T(1024)}, f32[768]{0:T(1024)S(1)}, u32[]{:S(2)}) copy-start(f32[768]{0:T(1024)S(1)} %fusion.58) | copy-start | bytes 9220
  262.9 18.4 %copy-start.70 = (f32[2,768]{1,0:T(2,128)}, f32[2,768]{1,0:T(2,128)S(1)}, u32[]{:S(2)}) copy-start(f32[2,768]{1,0:T(2,128)S(1)} %broadcast_multiply_fusion.2) | copy-start | bytes 18436
  262.9 3.8 collective-permute-start.3
  266.7 5.1 collective-permute-start.4
  271.8 1.3 collective-permute-start.5
  273.2 15.0 %collective-permute-start.6 = (f32[8,4,768]{2,1,0:T(4,128)S(1)}, f32[8,4,768]{2,1,0:T(4,128)S(1)}, u32[]{:S(2)}, u32[]{:S(2)}) collective-permute-start(f32[8,4,768]{2,1,0:T(4,128)S(1)} %pad_maximum_fusion.33), channel_id=1, source_target_pairs={{0,8},{4,12},{8,0},{12,4},{16,24},{20,28},{24,16},{28,20},{1,9},{5... | collective-permute-start | bytes 294920 | tf_op jit(solution)/shard_map/ppermute | solution.py:358
  288.3 6.8 collective-permute-start.7
  295.2 12.1 %copy-start.66 = (f32[768]{0:T(1024)S(1)}, f32[768]{0:T(1024)}, u32[]{:S(2)}) copy-start(f32[768]{0:T(1024)} %copy-done.65) | copy-start | bytes 9220
  295.2 12.1 %copy-start.75 = (f32[768]{0:T(1024)S(1)}, f32[768]{0:T(1024)}, u32[]{:S(2)}) copy-start(f32[768]{0:T(1024)} %copy-done.74) | copy-start | bytes 9220
  295.2 12.1 %copy-start.79 = (f32[768]{0:T(1024)S(1)}, f32[768]{0:T(1024)}, u32[]{:S(2)}) copy-start(f32[768]{0:T(1024)} %copy-done.78) | copy-start | bytes 9220
  310.6 10.9 %copy-start.31 = (f32[768,768]{1,0:T(8,128)}, f32[768,768]{1,0:T(8,128)S(1)}, u32[]{:S(2)}) copy-start(f32[768,768]{1,0:T(8,128)S(1)} %get-tuple-element.89) | copy-start | bytes 7077892
  310.6 10.9 %copy-start.16 = (f32[768,768]{1,0:T(8,128)S(1)}, f32[768,768]{1,0:T(8,128)}, u32[]{:S(2)}) copy-start(f32[768,768]{1,0:T(8,128)} %copy-done.15) | copy-start | bytes 7077892
  310.6 10.9 %copy-start.89 = (f32[768]{0:T(1024)S(1)}, f32[768]{0:T(1024)}, u32[]{:S(2)}) copy-start(f32[768]{0:T(1024)} %copy-done.88) | copy-start | bytes 9220
  310.6 10.9 %copy-start.94 = (f32[768]{0:T(1024)S(1)}, f32[768]{0:T(1024)}, u32[]{:S(2)}) copy-start(f32[768]{0:T(1024)} %get-tuple-element.173) | copy-start | bytes 9220
  391.2 10.9 %copy-start.34 = (f32[768,768]{1,0:T(8,128)}, f32[768,768]{1,0:T(8,128)S(1)}, u32[]{:S(2)}) copy-start(f32[768,768]{1,0:T(8,128)S(1)} %get-tuple-element.85) | copy-start | bytes 7077892
  391.2 10.9 %copy-start.14 = (f32[768,768]{1,0:T(8,128)S(1)}, f32[768,768]{1,0:T(8,128)}, u32[]{:S(2)}) copy-start(f32[768,768]{1,0:T(8,128)} %copy-done.13) | copy-start | bytes 7077892
  469.9 23.2 %copy-start.100 = (f32[768]{0:T(1024)S(1)}, f32[768]{0:T(1024)}, u32[]{:S(2)}) copy-start(f32[768]{0:T(1024)} %get-tuple-element.64) | copy-start | bytes 9220
  491.8 257.1 %collective-permute-start.13 = (f32[12,768]{1,0:T(8,128)}, f32[12,768]{1,0:T(8,128)}, u32[]{:S(2)}, u32[]{:S(2)}) collective-permute-start(f32[12,768]{1,0:T(8,128)} %reshape.888), channel_id=1, source_target_pairs={{0,4},{4,0},{8,12},{12,8},{16,20},{20,16},{24,28},{28,24},{1,5},{5... | collective-permute-start | bytes 110600 | tf_op jit(solution)/shard_map/ppermute | solution.py:358
  494.4 18.5 %copy-start.105 = (f32[768]{0:T(1024)S(1)}, f32[768]{0:T(1024)}, u32[]{:S(2)}) copy-start(f32[768]{0:T(1024)} %convert_reduce_fusion.8) | copy-start | bytes 9220
  494.4 19.2 %copy-start.46 = (bf16[768,768]{1,0:T(8,128)(2,1)S(1)}, bf16[768,768]{1,0:T(8,128)(2,1)}, u32[]{:S(2)}) copy-start(bf16[768,768]{1,0:T(8,128)(2,1)} %convolution_convert_fusion.2) | copy-start | bytes 3538948
  494.4 19.2 %copy-start.47 = (bf16[768,768]{1,0:T(8,128)(2,1)S(1)}, bf16[768,768]{1,0:T(8,128)(2,1)}, u32[]{:S(2)}) copy-start(bf16[768,768]{1,0:T(8,128)(2,1)} %convolution_convert_fusion.3) | copy-start | bytes 3538948
  634.7 115.4 %collective-permute-start.8 = (f32[12,768]{1,0:T(8,128)}, f32[12,768]{1,0:T(8,128)S(1)}, u32[]{:S(2)}, u32[]{:S(2)}) collective-permute-start(f32[12,768]{1,0:T(8,128)} %reshape.882), channel_id=1, source_target_pairs={{0,4},{4,0},{8,12},{12,8},{16,20},{20,16},{24,28},{28,24},{1,5},{5... | collective-permute-start | bytes 110600 | tf_op jit(solution)/shard_map/ppermute | solution.py:358
  749.8 4.6 collective-permute-start.14
  750.1 4.8 collective-permute-start.9
  754.4 4.7 collective-permute-start.15
  754.9 4.2 collective-permute-start.10
  759.1 4.2 collective-permute-start.16
  759.2 4.6 collective-permute-start.11
  763.3 5.7 collective-permute-start.17
  763.8 5.4 collective-permute-start.12
  (131 other events, 568.2 us)

commit v3 on v2

--- a/solution.py
+++ b/solution.py
@@ -178,12 +178,12 @@
         bit *= 2
     return found
 
-def reduce_kernel(attn, ways, grads, out, own, got, got_a, got_b, got_c, got_d, mix, zin, zout, far,
+def reduce_kernel(plan, ways, grads, out, own, got, got_a, got_b, got_c, got_d, mix, zin, zout, far,
                   l_sem, r_send, r_recv, g_send, g_recv):
     core, px, py, peers = place()
     extra = far_peers(None)
     peers.update(extra)
-    groups = len(attn)
+    groups = len(plan)
     rows = out.shape[1] // 8
     half = rows // 2
     def remote(src, dst, sems, index, peer):
@@ -197,8 +197,9 @@
         c.start(); started.append(c)
 
     def share(g, c, j):
-        ref = grads[g]
-        return ref.at[2 * c + j] if attn[g] else ref.at[:, 2 * c + j]
+        number, layer, attn = plan[g]
+        ref = grads[number].at[layer]
+        return ref.at[2 * c + j] if attn else ref.at[:, 2 * c + j]
 
     def load(g, j):
         return pltpu.make_async_copy(share(g, core, j), own.at[g, :, j], l_sem.at[g * 2 + j])
@@ -322,9 +323,9 @@
     for c in started:
         c.wait_send()
 
-def reduce_gradients(grads, attn, ways, collective_id):
-    groups = len(grads)
-    quarter, width = grads[0].shape[2:]
+def reduce_gradients(grads, plan, ways, collective_id):
+    groups = len(plan)
+    quarter, width = grads[0].shape[3:]
     R = quarter * 4
     rows = R // 8
     half = rows // 2
@@ -333,12 +334,12 @@
         nfar += 1
     per = 6 + ways - 1 + nfar
     def kern(*refs):
-        reduce_kernel(attn, ways, refs[:groups], *refs[groups:])
+        reduce_kernel(plan, ways, refs[: len(grads)], *refs[len(grads) :])
     V = lambda *s: pltpu.VMEM(s, BF16)
     return pl.pallas_call(
         kern,
         out_shape=jax.ShapeDtypeStruct((groups, R, width), BF16),
-        in_specs=[ANY] * groups, out_specs=ANY,
+        in_specs=[ANY] * len(grads), out_specs=ANY,
         scratch_shapes=[V(groups, ways, 2, 2 * rows, width), V(groups, ways, 2, 2 * rows, width),
                         V(groups, ways, 2, half, width), V(groups, ways, 2 * half, width),
                         V(groups, ways, half, width), V(groups, ways, half, width),
@@ -400,155 +401,436 @@
     return value
 
 
-def norm_forward(summed, gain, bias):
-    average = jnp.mean(summed, axis=-1, keepdims=True)
-    centered = summed - average
-    inv_std = lax.rsqrt(jnp.mean(centered * centered, axis=-1, keepdims=True) + EPS_NORM)
-    normed = centered * inv_std
-    return normed * gain + bias, normed, inv_std
-
-
-def norm_backward(grad_out, normed, inv_std, gain):
-    grad_normed = grad_out * gain
-    grad_in = inv_std * (
-        grad_normed
-        - jnp.mean(grad_normed, axis=-1, keepdims=True)
-        - normed * jnp.mean(grad_normed * normed, axis=-1, keepdims=True)
-    )
-    return grad_in, jnp.sum(grad_out * normed, axis=0), jnp.sum(grad_out, axis=0)
-
-
-def gelu_value(inner):
-    return 0.5 * inner * (1.0 + lax.erf(inner * RSQRT_TWO))
-
-
-def gelu_slope(inner):
-    return 0.5 * (1.0 + lax.erf(inner * RSQRT_TWO)) + inner * jnp.exp(
-        -0.5 * inner * inner
-    ) * RSQRT_TWOPI
-
-
-def mm(spec, left, right):
-    return jnp.einsum(spec, left, right, preferred_element_type=F32)
-
-
-def scores_of(q, k, lengths):
-    scores = mm("sqhe,skhe->shqk", q, k) * HEAD_DIM ** (-0.5)
-    keep = jnp.arange(k.shape[1], dtype=jnp.int32)[None, :] < lengths[:, None]
-    return jnp.where(keep[:, None, None, :], scores, NEG_FILL)
-
-
-def attention_forward(q, k, v, lengths):
-    scores = scores_of(q, k, lengths)
-    top = jnp.max(scores, axis=-1, keepdims=True)
-    expo = jnp.exp(scores - top)
-    total = jnp.sum(expo, axis=-1, keepdims=True)
-    probs = (expo / total).astype(BF16)
-    return mm("shqk,skhe->sqhe", probs, v).astype(BF16), top + jnp.log(total)
-
-
-def attention_backward(q, k, v, lengths, log_total, grad_context):
-    scale = HEAD_DIM ** (-0.5)
-    probs = jnp.exp(scores_of(q, k, lengths) - log_total)
-    dv = mm("shqk,sqhe->skhe", probs.astype(BF16), grad_context).astype(BF16)
-    dp = mm("sqhe,skhe->shqk", grad_context, v)
-    ds = (probs * (dp - jnp.sum(probs * dp, axis=-1, keepdims=True))).astype(BF16)
-    dq = (mm("shqk,skhe->sqhe", ds, k) * scale).astype(BF16)
-    dk = (mm("shqk,sqhe->skhe", ds, q) * scale).astype(BF16)
-    return dq, dk, dv
-
-
-def buckets(rows, shapes):
-    parts = []
-    start = 0
-    for count, length in shapes:
-        stop = start + count * length
-        parts.append(rows[start:stop].reshape(count, length, -1, HEAD_DIM))
-        start = stop
-    return parts
-
-
-def unbucket(parts):
-    return jnp.concatenate([part.reshape(-1, part.shape[2] * HEAD_DIM) for part in parts])
-
-
-def layer_forward(x, attn_w, up_w, down_w, small, shapes, lengths):
-    width = x.shape[-1]
-    xr = x.astype(BF16)
-    tokens = x.shape[0]
-    q, k, v = (mm("td,kd->tk", xr, attn_w[i]) for i in range(3))
-    q = (q + small["q_bias"]).astype(BF16)
-    k = k.astype(BF16)
-    v = (v + small["v_bias"]).astype(BF16)
-    contexts, logs = [], []
-    for qs, ks, vs, lens in zip(
-        buckets(q, shapes), buckets(k, shapes), buckets(v, shapes), lengths
-    ):
-        context, log_total = attention_forward(qs, ks, vs, lens)
-        contexts.append(context)
-        logs.append(log_total)
-    ctx = unbucket(contexts)
-    attn = mm("tc,cd->td", ctx, attn_w[3]) + small["out_bias"]
-    h, n1, r1 = norm_forward(x + attn, small["gain"][0], small["bias"][0])
-    hr = h.astype(BF16)
-    u = mm("td,zdk->tzk", hr, up_w).reshape(tokens, -1) + small["up_bias"]
-    a = gelu_value(u).astype(BF16)
-    f = mm("tk,kd->td", a, down_w.reshape(-1, width)) + small["down_bias"]
-    y, n2, r2 = norm_forward(h + f, small["gain"][1], small["bias"][1])
-    return y, (xr, q, k, v, logs, ctx, n1, r1, hr, u, a, n2, r2)
-
-
-def layer_backward(dy, saved, attn_w, up_w, down_w, small, shapes, lengths):
-    xr, q, k, v, logs, ctx, n1, r1, hr, u, a, n2, r2 = saved
-    ways = up_w.shape[0]
-    tokens, width = dy.shape
-    dz2, gain_two, bias_two = norm_backward(dy, n2, r2, small["gain"][1])
-    df = dz2.astype(BF16)
-    down_b = jnp.sum(df, axis=0, dtype=F32)
-    a4 = a.reshape(tokens, ways, -1)
-    down_g = mm("tzk,td->zkd", a4, df).astype(BF16)
-    da = mm("td,kd->tk", df, down_w.reshape(-1, width))
-    du = (da * gelu_slope(u)).astype(BF16)
-    up_b = jnp.sum(du, axis=0, dtype=F32)
-    du4 = du.reshape(tokens, ways, -1)
-    up_g = mm("td,tzk->zdk", hr, du4).astype(BF16)
-    dh = dz2 + mm("tzk,zdk->td", du4, up_w)
-    dz1, gain_one, bias_one = norm_backward(dh, n1, r1, small["gain"][0])
-    dattn = dz1.astype(BF16)
-    out_b = jnp.sum(dattn, axis=0, dtype=F32)
-    out_g = mm("tk,td->kd", ctx, dattn)
-    dctx = mm("td,cd->tc", dattn, attn_w[3]).astype(BF16)
-    grads = ([], [], [])
-    for qs, ks, vs, lens, log_total, gs in zip(
-        buckets(q, shapes),
-        buckets(k, shapes),
-        buckets(v, shapes),
-        lengths,
-        logs,
-        buckets(dctx, shapes),
-    ):
-        for store, value in zip(grads, attention_backward(qs, ks, vs, lens, log_total, gs)):
-            store.append(value)
-    dq, dk, dv = (unbucket(store) for store in grads)
-    attn_g = jnp.stack(
-        [mm("tk,td->kd", dq, xr), mm("tk,td->kd", dk, xr), mm("tk,td->kd", dv, xr), out_g]
-    ).astype(BF16)
-    dx = dz1
-    for i, grad in enumerate((dq, dk, dv)):
-        dx = dx + mm("tk,kd->td", grad, attn_w[i])
-    qv_b = jnp.stack(
-        [jnp.sum(dq, axis=0, dtype=F32).reshape(-1), jnp.sum(dv, axis=0, dtype=F32).reshape(-1)]
-    )
-    shared = (out_b, jnp.stack([gain_one, gain_two]), jnp.stack([bias_one, bias_two]), down_b)
-    return dx, (attn_g, up_g, down_g), (qv_b, up_b, shared)
-
-
-def to_absolute(rows):
-    me = lax.axis_index("mp")
-    ways = rows.shape[-2]
-    wide = jnp.concatenate([rows, rows], axis=-2)
-    flipped = jnp.flip(wide, axis=-2)
-    return lax.dynamic_slice_in_dim(flipped, ways - 1 - me, ways, axis=-2)
+def nn(a, b):
+    return lax.dot_general(a, b, (((1,), (0,)), ((), ())), preferred_element_type=F32)
+def nt(a, b):
+    return lax.dot_general(a, b, (((1,), (1,)), ((), ())), preferred_element_type=F32)
+def tn(a, b):
+    return lax.dot_general(a, b, (((0,), (0,)), ((), ())), preferred_element_type=F32)
+
+def gelu_both(u):
+    w = jnp.abs(u) * RSQRT_TWO
+    t = 1.0 / (1.0 + 0.3275911 * w)
+    e = jnp.exp(-0.5 * u * u)
+    poly = ((((1.061405429 * t - 1.453152027) * t + 1.421413741) * t - 0.284496736) * t + 0.254829592) * t
+    tail = 0.5 * poly * e
+    phi = jnp.where(u >= 0.0, 1.0 - tail, tail)
+    return u * phi, phi + u * e * RSQRT_TWOPI
+
+def norm_rows(z, gain, bias):
+    c = z - jnp.mean(z, axis=-1, keepdims=True)
+    r = lax.rsqrt(jnp.mean(c * c, axis=-1, keepdims=True) + EPS_NORM)
+    n = c * r
+    return n, r, n * gain + bias
+
+ROWS = 256
+
+class Forward:
+    def __init__(self, l, seqs, r):
+        self.l, self.seqs, self.r = l, seqs, r
+    def blocks(self):
+        T = self.r.x.shape[0]
+        return [slice(i, i + ROWS) for i in range(0, T, ROWS)]
+    def project(self, m):
+        r, l = self.r, self.l
+        acc = nt(r.xr[l], r.w_attn[m])
+        if m == 0:
+            r.q[l] = (acc + r.qv_b[l, 0:1]).astype(BF16) * jnp.bfloat16(0.125)
+        elif m == 1:
+            r.k[l] = acc.astype(BF16)
+        else:
+            r.v[l] = (acc + r.qv_b[l, 1:2]).astype(BF16)
+    def attend(self, s, i):
+        r, l = self.r, self.l
+        start, n = self.seqs[s]
+        rows, lanes = slice(start, start + n), slice(i * 128, i * 128 + 128)
+        kp, qp, vp = r.k[l, rows, lanes], r.q[l, rows, lanes], r.v[l, rows, lanes]
+        vt = vp.T
+        first = lax.broadcasted_iota(jnp.int32, (n, 128), 1) < HEAD_DIM
+        bias = jnp.concatenate([r.mask[rows]] * (n // 128), axis=1)
+        out = []
+        for h in range(2):
+            kh = jnp.where(first if h == 0 else ~first, kp, jnp.zeros_like(kp))
+            sc = nt(kh, qp) + bias
+            top = jnp.max(sc, axis=0, keepdims=True)
+            e = jnp.exp(sc - top)
+            tot = jnp.sum(e, axis=0, keepdims=True)
+            r.lse[l, 2 * i + h:2 * i + h + 1, rows] = top + jnp.log(tot)
+            ct = nn(vt[h * HEAD_DIM:(h + 1) * HEAD_DIM], e.astype(BF16))
+            out.append(ct * (1.0 / tot))
+        ct = jnp.concatenate(out, axis=0)
+        r.ctx[l, rows, lanes] = ct.T.astype(BF16)
+    def out_norm(self, b):
+        r, l = self.r, self.l
+        z = r.x[b] + nn(r.ctx[l, b], r.w_attn[3]) + r.out_b[l:l + 1]
+        n, inv, h = norm_rows(z, r.gain[l, 0:1], r.bias[l, 0:1])
+        r.n1[l, b] = n
+        r.r1[l, b] = jnp.broadcast_to(inv, (ROWS, 128))
+        r.h[b] = h
+        r.hr[l, b] = h.astype(BF16)
+    def ffn(self, c, b, slot):
+        r, l = self.r, self.l
+        u = nn(r.hr[l, b], r.w_up[c]) + r.up_b[l, c:c + 1]
+        a, slope = gelu_both(u)
+        a = a.astype(BF16)
+        r.a[slot, b] = a
+        r.slope[slot, b] = slope.astype(BF16)
+        f = nn(a, r.w_down[c])
+        if c == 0:
+            r.f[b] = f
+        else:
+            r.f[b] += f
+    def ffn_norm(self, b, last):
+        r, l = self.r, self.l
+        z = r.h[b] + r.f[b] + r.down_b[l:l + 1]
+        n, inv, y = norm_rows(z, r.gain[l, 1:2], r.bias[l, 1:2])
+        r.n2[l, b] = n
+        r.r2[l, b] = jnp.broadcast_to(inv, (ROWS, 128))
+        r.x[b] = y
+        if not last:
+            r.xr[l + 1, b] = y.astype(BF16)
+
+class Refs:
+    def __init__(self, **k):
+        self.__dict__.update(k)
+
+def forward_kernel(seqs, layers, names, *refs):
+    r = Refs(**dict(zip(names, refs)))
+    ways = r.w.shape[1]
+    T = r.x.shape[0]
+    for s, (start, n) in enumerate(seqs):
+        row = lax.broadcasted_iota(jnp.int32, (n, 128), 0)
+        r.mask[start:start + n] = jnp.where(row < r.lens[s], 0.0, NEG_FILL)
+    r.xr[0] = r.states[...]
+    r.x[...] = r.states[...].astype(F32)
+    bufs = [r.w_attn, r.w_up, r.w_down]
+    def load(g):
+        return pltpu.make_async_copy(r.w.at[g], bufs[g % 3], r.w_sem.at[g])
+    for g in range(3):
+        load(g).start()
+    pend = {}
+    outs = []
+    def save(l, c, slot):
+        for j, (src, dst) in enumerate(((r.a, r.a_out), (r.slope, r.slope_out))):
+            cp = pltpu.make_async_copy(src.at[slot], dst.at[l, c], r.s_sem.at[(l * ways + c) * 2 + j])
+            cp.start()
+            pend.setdefault(slot, []).append(cp)
+    for l in range(layers):
+        f = Forward(l, seqs, r)
+        load(3 * l).wait()
+        for m in range(3):
+            f.project(m)
+        for s in range(len(seqs)):
+            for i in range(r.ctx.shape[2] // 128):
+                f.attend(s, i)
+        for b in f.blocks():
+            f.out_norm(b)
+        if l + 1 < layers:
+            load(3 * l + 3).start()
+        load(3 * l + 1).wait()
+        load(3 * l + 2).wait()
+        for c in range(ways):
+            slot = c % 2
+            for cp in pend.pop(slot, []):
+                cp.wait()
+            for b in f.blocks():
+                f.ffn(c, b, slot)
+            save(l, c, slot)
+        if l + 1 < layers:
+            load(3 * l + 4).start()
+            load(3 * l + 5).start()
+        for b in f.blocks():
+            f.ffn_norm(b, l + 1 == layers)
+    for cps in pend.values():
+        for cp in cps:
+            cp.wait()
+
+def forward(states, w, lens, small, seqs):
+    T, D = states.shape
+    G, ways, R, _ = w.shape
+    L = G // 3
+    V = pl.BlockSpec(memory_space=pltpu.VMEM)
+    A = pl.BlockSpec(memory_space=pl.ANY)
+    S = pl.BlockSpec(memory_space=pltpu.SMEM)
+    snames = ("qv_b", "out_b", "gain", "bias", "up_b", "down_b")
+    heads = D // HEAD_DIM
+    outs = dict(
+        x=((T, D), F32), xr=((L, T, D), BF16), q=((L, T, D), BF16), k=((L, T, D), BF16), v=((L, T, D), BF16),
+        ctx=((L, T, D), BF16), n1=((L, T, D), F32), r1=((L, T, 128), F32), hr=((L, T, D), BF16),
+        n2=((L, T, D), F32), r2=((L, T, 128), F32), lse=((L, -(-heads // 8) * 8, T), F32),
+        a_out=((L, ways, T, R), BF16), slope_out=((L, ways, T, R), BF16))
+    scratch = dict(
+        mask=pltpu.VMEM((T, 128), F32), h=pltpu.VMEM((T, D), F32), f=pltpu.VMEM((T, D), F32),
+        a=pltpu.VMEM((2, T, R), BF16), slope=pltpu.VMEM((2, T, R), BF16),
+        w_attn=pltpu.VMEM((ways, R, D), BF16), w_up=pltpu.VMEM((ways, R, D), BF16), w_down=pltpu.VMEM((ways, R, D), BF16),
+        w_sem=pltpu.SemaphoreType.DMA((G,)), s_sem=pltpu.SemaphoreType.DMA((L * ways * 2,)))
+    names = ("lens", "states", "w") + snames + tuple(outs) + tuple(scratch)
+    res = pl.pallas_call(
+        functools.partial(forward_kernel, seqs, L, names),
+        out_shape=[jax.ShapeDtypeStruct(s, d) for s, d in outs.values()],
+        in_specs=[S, V, A] + [V] * len(snames),
+        out_specs=[A if n in ("a_out", "slope_out") else V for n in outs],
+        scratch_shapes=list(scratch.values()),
+        compiler_params=pltpu.CompilerParams(vmem_limit_bytes=62 << 20),
+        name="forward_layers",
+    )(lens, states, w, *[small[n] for n in snames])
+    return dict(zip(outs, res))
+
+
+def norm_back(g, n, r, gain):
+    gn = g * gain
+    return r * (gn - jnp.mean(gn, axis=-1, keepdims=True) - n * jnp.mean(gn * n, axis=-1, keepdims=True))
+
+def total(v):
+    return jnp.sum(v, axis=0, keepdims=True)
+
+QB, VB, UB, OB, GAIN, BIAS, DB = 0, 1, 2, 6, 7, 9, 11
+
+class Backward:
+    def __init__(self, l, seqs, r):
+        self.l, self.seqs, self.r = l, seqs, r
+        T = r.dy.shape[0]
+        self.blocks = [slice(i, i + ROWS) for i in range(0, T, ROWS)]
+    def add_row(self, row, value, first):
+        r, l = self.r, self.l
+        if first:
+            r.sums[l, row:row + 1] = value
+        else:
+            r.sums[l, row:row + 1] += value
+    def norm(self, b, which):
+        r, l = self.r, self.l
+        g = r.dy[b] if which else r.dz[b] + r.acc[b]
+        n, inv = r.n[which, b], r.inv[which, b]
+        inv = jnp.concatenate([inv] * (n.shape[1] // 128), axis=1)
+        dz = norm_back(g, n, inv, r.gain[l, which:which + 1])
+        low = dz.astype(BF16)
+        r.dz[b] = dz
+        r.low[b] = low
+        first = b.start == 0
+        self.add_row(GAIN + which, total(g * n), first)
+        self.add_row(BIAS + which, total(g), first)
+        self.add_row(DB if which else OB, total(low.astype(F32)), first)
+    def flip(self, dst, src):
+        dst[...] = src[...].T
+    def ffn_down(self, c, slot):
+        r = self.r
+        r.stage[0] = nn(r.low_t[...], r.a[slot]).astype(BF16)
+    def ffn_mid(self, c, b, slot, w):
+        r = self.r
+        da = nt(r.low[b], r.w[w])
+        du = (da * r.slope[slot, b].astype(F32)).astype(BF16)
+        r.du[b] = du
+        self.add_row(UB + c, total(du.astype(F32)), b.start == 0)
+    def ffn_up(self, c):
+        r = self.r
+        r.stage[1] = nn(r.hr_t[...], r.du[...]).astype(BF16)
+    def ffn_back(self, c, b, w):
+        r = self.r
+        dh = nt(r.du[b], r.w[w])
+        if c == 0:
+            r.acc[b] = dh
+        else:
+            r.acc[b] += dh
+    def context(self, b, w):
+        r = self.r
+        r.dctx[b] = nt(r.low[b], r.w[w]).astype(BF16)
+    def out_grad(self, slot):
+        r = self.r
+        r.stage[slot] = nn(r.ctx[...].T, r.low[...]).astype(BF16)
+    def attend(self, s, i):
+        r, l = self.r, self.l
+        start, n = self.seqs[s]
+        rows, lanes = slice(start, start + n), slice(i * 128, i * 128 + 128)
+        kp, qp, vp, gp = r.k[rows, lanes], r.q[rows, lanes], r.v[rows, lanes], r.dctx[rows, lanes]
+        kt = kp.T
+        first = lax.broadcasted_iota(jnp.int32, (n, 128), 1) < HEAD_DIM
+        bias = jnp.concatenate([r.mask[rows]] * (n // 128), axis=1)
+        dv, dk, dq = [], [], []
+        for h in range(2):
+            keep = first if h == 0 else ~first
+            kh = jnp.where(keep, kp, jnp.zeros_like(kp))
+            vh = jnp.where(keep, vp, jnp.zeros_like(vp))
+            p = jnp.exp(nt(kh, qp) + bias - r.lse[2 * i + h:2 * i + h + 1, rows])
+            dp = nt(vh, gp)
+            ds = (p * (dp - jnp.sum(p * dp, axis=0, keepdims=True))).astype(BF16)
+            dv.append(nn(p.astype(BF16), gp))
+            dk.append(nn(ds, qp))
+            dq.append(nn(kt[h * HEAD_DIM:(h + 1) * HEAD_DIM], ds) * 0.125)
+        r.dk[rows, lanes] = jnp.where(first, dk[0], dk[1]).astype(BF16)
+        r.dv[rows, lanes] = jnp.where(first, dv[0], dv[1]).astype(BF16)
+        r.dq[rows, lanes] = jnp.concatenate(dq, axis=0).T.astype(BF16)
+    def qkv_grad(self, m, slot):
+        r = self.r
+        g = (r.dq, r.dk, r.dv)[m][...]
+        r.stage[slot] = nn(g.T, r.xr[...]).astype(BF16)
+        if m != 1:
+            self.add_row(QB if m == 0 else VB, total(g.astype(F32)), True)
+    def back_in(self, b, m, w):
+        r = self.r
+        d = nn((r.dq, r.dk, r.dv)[m][b], r.w[w])
+        if m == 0:
+            r.dy[b] = r.dz[b] + d
+        else:
+            r.dy[b] += d
+
+def backward_kernel(seqs, layers, names, *refs):
+    r = Refs(**dict(zip(names, refs)))
+    ways = r.a_in.shape[1]
+    for s, (start, n) in enumerate(seqs):
+        row = lax.broadcasted_iota(jnp.int32, (n, 128), 0)
+        r.mask[start:start + n] = jnp.where(row < r.lens[s], 0.0, NEG_FILL)
+    r.dy[...] = r.dy_in[...]
+    nw = r.w.shape[0]
+    order = []
+    for l in reversed(range(layers)):
+        for c in range(ways):
+            order += [(3 * l + 2, c), (3 * l + 1, c)]
+        order += [(3 * l, m) for m in (3, 0, 1, 2)]
+    def wload(i):
+        return pltpu.make_async_copy(r.w_in.at[order[i]], r.w.at[i % nw], r.w_sem.at[i])
+    state = {"w": 0, "issued": 0}
+    def more():
+        while state["issued"] < len(order) and state["issued"] < state["w"] + nw:
+            wload(state["issued"]).start()
+            state["issued"] += 1
+    def take():
+        i = state["w"]
+        wload(i).wait()
+        return i % nw
+    def done():
+        state["w"] += 1
+        more()
+    items = ("n2", "r2", "hr", "n1", "r1", "ctx", "q", "k", "v", "lse", "xr")
+    dst = dict(n2=r.n.at[1], n1=r.n.at[0], r2=r.inv.at[1], r1=r.inv.at[0], hr=r.hr, ctx=r.ctx, q=r.q, k=r.k, v=r.v, lse=r.lse, xr=r.xr)
+    src = dict(n2=r.n2_in, n1=r.n1_in, r2=r.r2_in, r1=r.r1_in, hr=r.hr_in, ctx=r.ctx_in, q=r.q_in, k=r.k_in, v=r.v_in, lse=r.lse_in, xr=r.xr_in)
+    def load(l, name):
+        return pltpu.make_async_copy(src[name].at[l], dst[name], r.i_sem.at[l * len(items) + items.index(name)])
+    def aload(l, c, j):
+        return pltpu.make_async_copy((r.a_in, r.slope_in)[j].at[l, c], (r.a, r.slope)[j].at[c % 2], r.a_sem.at[(l * ways + c) * 2 + j])
+    more()
+    top = layers - 1
+    for name in items:
+        load(top, name).start()
+    for j in range(2):
+        aload(top, 0, j).start()
+        aload(top, 1, j).start()
+    pend = {}
+    count = [0]
+    def slot_for():
+        s = count[0] % 2
+        return s
+    def save(slot, dst_ref, sem):
+        cp = pltpu.make_async_copy(r.stage.at[slot], dst_ref, r.o_sem.at[sem])
+        cp.start()
+        pend[slot] = cp
+    def free(slot):
+        if slot in pend:
+            pend.pop(slot).wait()
+    for l in reversed(range(layers)):
+        f = Backward(l, seqs, r)
+        prev = l - 1
+        def again(*nm):
+            if prev >= 0:
+                for x in nm:
+                    load(prev, x).start()
+        base = l * (2 * ways + 4)
+        load(l, "n2").wait(); load(l, "r2").wait()
+        for b in f.blocks:
+            f.norm(b, 1)
+        again("n2", "r2")
+        f.flip(r.low_t, r.low)
+        load(l, "hr").wait()
+        f.flip(r.hr_t, r.hr)
+        again("hr")
+        for c in range(ways):
+            slot = c % 2
+            aload(l, c, 0).wait()
+            free(0)
+            f.ffn_down(c, slot)
+            save(0, r.g_down.at[l, c], base + 2 * c)
+            aload(l, c, 1).wait()
+            w = take()
+            for b in f.blocks:
+                f.ffn_mid(c, b, slot, w)
+            done()
+            nl, nc = (l, c + 2) if c + 2 < ways else (l - 1, c + 2 - ways)
+            if nl >= 0:
+                for j in range(2):
+                    aload(nl, nc, j).start()
+            free(1)
+            f.ffn_up(c)
+            save(1, r.g_up.at[l, c], base + 2 * c + 1)
+            w = take()
+            for b in f.blocks:
+                f.ffn_back(c, b, w)
+            done()
+        load(l, "n1").wait(); load(l, "r1").wait()
+        for b in f.blocks:
+            f.norm(b, 0)
+        again("n1", "r1")
+        w = take()
+        for b in f.blocks:
+            f.context(b, w)
+        done()
+        load(l, "ctx").wait()
+        free(0)
+        f.out_grad(0)
+        save(0, r.g_attn.at[l, 3], base + 2 * ways + 3)
+        again("ctx")
+        for nm in ("q", "k", "v", "lse"):
+            load(l, nm).wait()
+        for s in range(len(seqs)):
+            for i in range(r.q.shape[1] // 128):
+                f.attend(s, i)
+        again("q", "k", "v", "lse")
+        load(l, "xr").wait()
+        for m in range(3):
+            slot = (m + 1) % 2
+            free(slot)
+            f.qkv_grad(m, slot)
+            save(slot, r.g_attn.at[l, m], base + 2 * ways + m)
+            w = take()
+            for b in f.blocks:
+                f.back_in(b, m, w)
+            done()
+        again("xr")
+    for s in (0, 1):
+        free(s)
+
+def backward(dy, saved, w, lens, small, seqs):
+    T, D = dy.shape
+    G, ways, R, _ = w.shape
+    L = G // 3
+    V = pl.BlockSpec(memory_space=pltpu.VMEM)
+    A = pl.BlockSpec(memory_space=pl.ANY)
+    S = pl.BlockSpec(memory_space=pltpu.SMEM)
+    ins = dict(lens=(lens, S), dy_in=(dy, V), w_in=(w, A), gain=(small["gain"], V))
+    for n in ("n2", "r2", "hr", "n1", "r1", "ctx", "q", "k", "v", "lse", "xr"):
+        ins[n + "_in"] = (saved[n], A)
+    ins["a_in"] = (saved["a_out"], A)
+    ins["slope_in"] = (saved["slope_out"], A)
+    outs = dict(dy=((T, D), F32, V), sums=((L, 16, D), F32, V), g_down=((L, ways, D, R), BF16, A), g_up=((L, ways, D, R), BF16, A), g_attn=((L, 4, D, D), BF16, A))
+    H = saved["lse"].shape[1]
+    VM = pltpu.VMEM
+    scratch = dict(
+        mask=VM((T, 128), F32), n=VM((2, T, D), F32), inv=VM((2, T, 128), F32), hr=VM((T, D), BF16), hr_t=VM((D, T), BF16),
+        low=VM((T, D), BF16), low_t=VM((D, T), BF16), dz=VM((T, D), F32), acc=VM((T, D), F32), du=VM((T, R), BF16),
+        a=VM((2, T, R), BF16), slope=VM((2, T, R), BF16), ctx=VM((T, D), BF16), q=VM((T, D), BF16), k=VM((T, D), BF16), v=VM((T, D), BF16),
+        xr=VM((T, D), BF16), lse=VM((H, T), F32), dctx=VM((T, D), BF16), dq=VM((T, D), BF16), dk=VM((T, D), BF16), dv=VM((T, D), BF16),
+        stage=VM((2, D, R), BF16), w=VM((4, R, D), BF16),
+        w_sem=pltpu.SemaphoreType.DMA((L * (2 * ways + 4),)), i_sem=pltpu.SemaphoreType.DMA((L * 11,)), a_sem=pltpu.SemaphoreType.DMA((L * ways * 2,)),
+        o_sem=pltpu.SemaphoreType.DMA((L * (2 * ways + 4),)))
+    names = tuple(ins) + tuple(outs) + tuple(scratch)
+    res = pl.pallas_call(
+        functools.partial(backward_kernel, seqs, L, names),
+        out_shape=[jax.ShapeDtypeStruct(s, d) for s, d, _ in outs.values()],
+        in_specs=[s for _, s in ins.values()],
+        out_specs=[s for _, _, s in outs.values()],
+        scratch_shapes=list(scratch.values()),
+        compiler_params=pltpu.CompilerParams(vmem_limit_bytes=62 << 20),
+        name="backward_layers",
+    )(*[v for v, _ in ins.values()])
+    return dict(zip(outs, res))
 
 
 def local(
@@ -590,31 +872,32 @@
         tiny_all.append(ring(tiny_all[-1]))
     tiny_all = jnp.stack(tiny_all).astype(F32)
 
-    weights = []
     qkv_t = jnp.swapaxes(query_key_value_matrix, 2, 3).reshape(layers, 3 * part, width)
     attn_pack = jnp.concatenate([qkv_t, out_weight], axis=1)
     kinds = tuple((i, l, i == 0) for l in range(layers) for i in range(3))
     gathered = gather_weights((attn_pack, up_matrix, down_matrix), kinds, ways, 0)
-    for l in range(layers):
-        attn_w, up_w, down_w = (gathered[3 * l + i] for i in range(3))
-        small = {
-            "q_bias": tiny_all[:, 2 * l].reshape(-1),
-            "v_bias": tiny_all[:, 2 * l + 1].reshape(-1),
-            "up_bias": tiny_all[:, 2 * layers + 4 * l : 2 * layers + 4 * (l + 1)].reshape(-1),
-            "out_bias": out_bias[l].astype(F32),
-            "down_bias": down_bias[l].astype(F32),
-            "gain": norm_gain[l].astype(F32),
-            "bias": norm_bias[l].astype(F32),
-        }
-        weights.append((attn_w, up_w, down_w, small))
-
-    x = jnp.concatenate(
+    small = {
+        "qv_b": jnp.stack(
+            [tiny_all[:, i].reshape(-1) for i in range(2 * layers)]
+        ).reshape(layers, 2, width),
+        "up_b": jnp.swapaxes(tiny_all[:, 2 * layers :].reshape(ways, layers, -1), 0, 1),
+        "out_b": out_bias.astype(F32),
+        "down_b": down_bias.astype(F32),
+        "gain": norm_gain.astype(F32),
+        "bias": norm_bias.astype(F32),
+    }
+    seqs, at = [], 0
+    for count, length in shapes:
+        for _ in range(count):
+            seqs.append((at, length))
+            at += length
+    seqs = tuple(seqs)
+    all_lens = jnp.concatenate(lengths)
+    states = jnp.concatenate(
         [query_states.reshape(-1, width), passage_states.reshape(-1, width)]
-    ).astype(F32)
-    kept = []
-    for l in range(layers):
-        x, saved = layer_forward(x, *weights[l], shapes, lengths)
-        kept.append(saved)
+    )
+    saved = forward(states, gathered, all_lens, small, seqs)
+    x = saved["x"]
 
     masks, embeds, invs = [], [], []
     start = 0
@@ -659,28 +942,45 @@
         dys.append((mask[:, :, None] * pooled_grad[:, None, :]).reshape(-1, width))
     dy = jnp.concatenate(dys)
 
-    summed = [None] * layers
-    smalls = [None] * layers
-    for l in reversed(range(layers)):
-        dy, big, (qv_b, up_b, shared) = layer_backward(
-            dy, kept[l], *weights[l], shapes, lengths
+    back = backward(dy, saved, gathered, all_lens, small, seqs)
+    dy = back["dy"]
+    parts = [
+        back[name].reshape(layers, 4, 4, -1, width) for name in ("g_down", "g_up", "g_attn")
+    ]
+    plan = tuple((i, l, i == 2) for l in reversed(range(layers)) for i in range(3))
+    reduced = reduce_gradients(parts, plan, ways, 1)
+    in_order = lambda i: jnp.stack(
+        [reduced[plan.index((i, l, i == 2))] for l in range(layers)]
+    ).astype(F32)
+    sums = back["sums"]
+    hidden = up_bias.shape[-1]
+    qv_rel = sums[:, QB : VB + 1].reshape(layers, 2, ways, part)
+    up_rel = sums[:, UB : UB + ways]
+    turn = lambda rel, axis: jnp.concatenate(
+        [
+            lax.dynamic_slice_in_dim(rel, (mp_rank - j) % ways, 1, axis=axis)
+            for j in range(ways)
+        ],
+        axis=axis,
+    )
+    small_all = sum_all(
+        jnp.concatenate(
+            [
+                turn(qv_rel, 2).reshape(layers, 2, width),
+                turn(up_rel, 1),
+                sums[:, UB + ways : DB + 1],
+            ],
+            axis=1,
         )
-        big = [item.reshape(4, 4, -1, width) for item in (big[2], big[1], big[0])]
-        summed[l] = reduce_gradients(big, (False, False, True), ways, 1 + l).astype(F32)
-        qv_abs = to_absolute(qv_b.reshape(2, ways, part)).reshape(-1)
-        up_abs = to_absolute(up_b.reshape(ways, -1)).reshape(-1)
-        flat = jnp.concatenate([qv_abs, up_abs] + [item.reshape(-1) for item in shared])
-        smalls[l] = sum_all(flat.reshape(-1, width))
+    )
 
     query_grad = dy[: q_slots * q_len].reshape(query_states.shape)
     passage_grad = dy[q_slots * q_len :].reshape(passage_states.shape)
-    attn_out = jnp.stack([s[2] for s in summed])
+    attn_out = in_order(2)
     qkv_grad = jnp.swapaxes(attn_out[:, : 3 * part].reshape(layers, 3, part, width), 2, 3)
     out_grad = attn_out[:, 3 * part :]
-    up_grad = jnp.stack([s[1] for s in summed])
-    down_grad = jnp.stack([s[0] for s in summed])
-    small_all = jnp.stack(smalls)
-    hidden = up_bias.shape[-1]
+    up_grad = in_order(1)
+    down_grad = jnp.swapaxes(in_order(0), 1, 2)
     cut = lambda lo, hi: small_all[:, lo:hi]
     qv_rows = cut(0, 2)
     qv_grad = lax.dynamic_slice_in_dim(qv_rows, mp_rank * part, part, axis=2)

time: 782 us -> 563 us (0.72)
  matrix products: 209 us -> 0.94 us
  Pallas kernels: 311 us -> 455 us
  local copies, waits for them, and re-layouts: 130 us -> 25.4 us
  other arithmetic: 86.6 us -> 28.5 us
  waiting for transfers between devices: 11.6 us -> 24.5 us
    dot_general x60 -> x0, matrix products: 207 us -> none  [mm(): return jnp.einsum(spec, left, right, preferred_element_type=F32)]
    pallas_call x0 -> x2, Pallas kernels: none -> 181 us  [the longest x1 109 us: backward(): pl.pallas_call(functools.partial(backward_kernel, seqs, L, names), out_sh...]
    pallas_call x2 -> x1, Pallas kernels: 202 us -> 163 us  [reduce_gradients(): pl.pallas_call(kern, out_shape=jax.ShapeDtypeStruct((groups, R, width), B...]
    reshape x22 -> x5, local copies, waits for them, and re-layouts: 25.7 us -> 1.49 us  [the longest x2 0.69 us: local(): tiny_all[:, 2 * layers:].reshape(ways, layers, -1)]
    unnamed x343 -> x24, local copies, waits for them, and re-layouts: 30.4 us -> 6.71 us
    reduce_sum x20 -> x0, other arithmetic: 19.7 us -> none  [the longest x4 4.42 us: attention_forward(): total = jnp.sum(expo, axis=-1, keepdims=True)]
    another operation x15 -> x3, other arithmetic: 20.7 us -> 1.96 us  [the longest x2 7.8 us: layer_backward(): jnp.stack([mm('tk,td->kd', dq, xr), mm('tk,td->kd', dk, xr), mm('tk,td->k...]
    slice x22 -> x7, local copies, waits for them, and re-layouts: 29.3 us -> 10.7 us  [the longest x1 4.03 us: local(): attn_out[:, :3 * part].reshape(layers, 3, part, width)]
  transfers between devices with their start and end apart: 18 -> 13, of which waited for: 8 -> 9; matrix products, arithmetic and copies ran while one was open for 16% -> 7% of each run, Pallas kernels for 40% -> 49%
where the time goes in v3:
time: 563 us; the launch traced here: 553 us
  Pallas kernels  455 us (81%)
  other arithmetic  28.5 us (5%)
  local copies, waits for them, and re-layouts  25.4 us (5%)
  waiting for transfers between devices  24.5 us (4%)
  starting transfers between devices  14.2 us (3%)
    pallas_call x1, Pallas kernels, reduce_gradients(): pl.pallas_call(kern, out_shape=jax.ShapeDtypeStruct((groups, R, width), B...  163 us
    pallas_call x1, Pallas kernels, gather_weights(): pl.pallas_call(kern, out_shape=jax.ShapeDtypeStruct((groups, ways, rows,...  110 us
    pallas_call x1, Pallas kernels, backward(): pl.pallas_call(functools.partial(backward_kernel, seqs, L, names), out_sh...  109 us
    pallas_call x1, Pallas kernels, forward(): pl.pallas_call(functools.partial(forward_kernel, seqs, L, names), out_sha...  72.7 us
  transfers between devices with their start and end apart: 13, of which 9 were waited for; matrix products, arithmetic and copies ran while one was open for 7% of the time, Pallas kernels for 49%

profile of v3, /device:TPU:0, one launch (start us, length us, event | category | flops | bytes accessed | tf_op | source)
XLA Modules:
  0.0 553.3 jit_solution(9224966012450261582)
XLA Ops:
  0.6 0.8 reshape.298
  1.4 0.7 reshape.297
  2.1 3.1 collective-permute-start
  5.2 0.6 compare_reduce_fusion
  5.8 1.3 fusion.15
  7.1 0.7 fusion.18
  7.9 3.3 pad_maximum_fusion.refs_0_
  11.3 1.1 pad_maximum_fusion.2.refs_1_
  13.7 1.6 collective-permute-start.1
  15.3 0.6 fusion.13
  16.0 3.2 collective-permute-done.1
  19.2 1.2 pad_add_fusion.refs_0_
  22.8 110.2 %gather_weights.1.refs_2_ = bf16[6,4,768,768]{3,2,1,0:T(8,128)(2,1)} custom-call(bf16[2,768,768]{2,1,0:T(8,128)(2,1)} %pad_maximum_fusion.refs_0_, bf16[2,768,768]{2,1,0:T(8,128)(2,1)} %refs_1_.1, bf16[2,768,768]{2,1,0:T(8,128)(2,1)} %refs_2_.1), custom_call_target="tpu_custom_call" | custom-call | tf_op jit(solution)/shard_map/gather_weights/pallas_call | solution.py:156
  134.8 72.7 %forward_layers.1 = (f32[768,768]{1,0:T(8,128)}, bf16[2,768,768]{2,1,0:T(8,128)(2,1)}, bf16[2,768,768]{2,1,0:T(8,128)(2,1)}, bf16[2,768,768]{2,1,0:T(8,128)(2,1)...) custom-call(s32[3]{0:T(128)} %pad_add_fusion.refs_0_, ...), custom_call_target="tpu_custom_call" | custom-call | tf_op jit(solution)/shard_map/forward_layers/pallas_call | solution.py:568
  207.6 1.6 multiply_reduce_fusion
  210.5 1.3 multiply_reduce_fusion.1
  212.0 0.9 collective-permute-start.3
  212.9 2.8 collective-permute-done.3
  215.8 1.9 collective-permute-start.4
  217.6 2.9 collective-permute-done.4
  220.7 1.2 collective-permute-done.5
  222.0 1.6 collective-permute-start.6
  223.6 0.6 reduce_sum.97
  225.1 1.8 collective-permute-done.6
  227.0 1.6 collective-permute-start.7
  228.6 4.6 collective-permute-done.7
  235.8 0.7 subtract_multiply_fusion.2
  237.2 1.6 pad_maximum_fusion.1.refs_1_
  238.8 108.6 %backward_layers.1 = (f32[768,768]{1,0:T(8,128)}, f32[2,16,768]{2,1,0:T(8,128)}, bf16[2,4,768,768]{3,2,1,0:T(8,128)(2,1)}, bf16[2,4,768,768]{3,2,1,0:T(8,128)(2,1)}, bf16[2,4,768,768]{3,2,1,0:T(8,128)(2,1)}) custom-call(s32[3]{0:T(128)} %pad_add_fusion.refs_0_, f32[768,768]{1,0:T(8,128)} %pad_maximum_fusion.1.refs_1_, ...), custom_call_target="tpu_custom_call" | custom-call | tf_op jit(solution)/shard_map/backward_layers/pallas_call | solution.py:824
  347.4 0.8 slice.118
  348.2 0.8 slice.119
  349.0 0.9 slice.120
  350.6 163.1 %reduce_gradients.1 = bf16[6,768,768]{2,1,0:T(8,128)(2,1)} custom-call(bf16[2,4,4,192,768]{4,3,2,1,0:T(8,128)(2,1)} %bitcast.59, bf16[2,4,4,192,768]{4,3,2,1,0:T(8,128)(2,1)} %bitcast.60, bf16[2,4,4,192,768]{4,3,2,1,0:T(8,128)(2,1)} %bitcast.61), custom_call_target="tpu_custom_call" | custom-call | tf_op jit(solution)/shard_map/reduce_gradients/pallas_call | solution.py:339
  513.7 3.5 fusion.19
  517.3 4.3 convert_bitcast_fusion
  521.7 0.9 collective-permute-done.9
  522.6 1.2 collective-permute-start.10
  523.8 1.2 slice_bitcast_fusion
  525.0 2.2 collective-permute-done.10
  527.3 1.4 collective-permute-start.11
  528.6 2.5 maximum_convert_fusion
  531.1 0.9 slice.113
  532.7 4.0 slice.136
  536.7 6.0 %copy.32 = f32[2,768,768]{2,1,0:T(8,128)} copy(f32[2,768,768]{1,2,0:T(8,128)} %get-tuple-element.136) | data formatting | bytes 9437184
  542.8 0.7 collective-permute-start.12
  543.5 1.1 maximum_convert_fusion.2
  544.6 4.9 collective-permute-done.12
  550.1 0.7 constant_dynamic-slice_fusion.1
  (96 shorter events, 12.1 us)
Async XLA Ops:
  2.1 11.5 %collective-permute-start = (bf16[12,192]{1,0:T(8,128)(2,1)S(1)}, bf16[12,192]{1,0:T(8,128)(2,1)S(1)}, u32[]{:S(2)}, u32[]{:S(2)}) collective-permute-start(bf16[12,192]{1,0:T(8,128)(2,1)S(1)} %get-tuple-element.127), channel_id=1, source_target_pairs={{0,1},{1,2},{2,3},{3,0},{4,5},{5,6},{6,7},{7,4},{8,9},{9,10},{10,1... | collective-permute-start | bytes 13832 | tf_op jit(solution)/shard_map/ppermute | solution.py:369
  7.9 3.4 copy-start.1
  7.9 3.4 copy-start.2
  11.2 1.2 copy-start.8
  11.2 9.2 %copy-start.5 = (bf16[2,768]{1,0:T(2,128)(2,1)S(1)}, bf16[2,768]{1,0:T(2,128)(2,1)}, u32[]{:S(2)}) copy-start(bf16[2,768]{1,0:T(2,128)(2,1)} %param.29) | copy-start | bytes 9220
  11.2 9.8 %copy-start.3 = (bf16[2,2,768]{2,1,0:T(2,128)(2,1)S(1)}, bf16[2,2,768]{2,1,0:T(2,128)(2,1)}, u32[]{:S(2)}) copy-start(bf16[2,2,768]{2,1,0:T(2,128)(2,1)} %param.30) | copy-start | bytes 18436
  11.2 10.4 %copy-start.4 = (bf16[2,2,768]{2,1,0:T(2,128)(2,1)S(1)}, bf16[2,2,768]{2,1,0:T(2,128)(2,1)}, u32[]{:S(2)}) copy-start(bf16[2,2,768]{2,1,0:T(2,128)(2,1)} %param.31) | copy-start | bytes 18436
  11.2 11.0 %copy-start.6 = (bf16[2,768]{1,0:T(2,128)(2,1)S(1)}, bf16[2,768]{1,0:T(2,128)(2,1)}, u32[]{:S(2)}) copy-start(bf16[2,768]{1,0:T(2,128)(2,1)} %param.35) | copy-start | bytes 9220
  13.7 5.5 collective-permute-start.1
  19.2 113.9 %collective-permute-start.2 = (bf16[12,192]{1,0:T(8,128)(2,1)S(1)}, bf16[12,192]{1,0:T(8,128)(2,1)S(1)}, u32[]{:S(2)}, u32[]{:S(2)}) collective-permute-start(bf16[12,192]{1,0:T(8,128)(2,1)S(1)} %collective-permute-done.1), channel_id=1, source_target_pairs={{0,1},{1,2},{2,3},{3,0},{4,5},{5,6},{6,7},{7,4},{8,9},{9,10},{10,1... | collective-permute-start | bytes 13832 | tf_op jit(solution)/shard_map/ppermute | solution.py:369
  207.5 16.0 %copy-start.7 = (s32[32]{0:T(128)S(1)}, s32[32]{0:T(128)}, u32[]{:S(2)}) copy-start(s32[32]{0:T(128)} %param.23) | copy-start | bytes 388
  207.5 21.0 %copy-start.9 = (s32[32]{0:T(128)S(1)}, s32[32]{0:T(128)}, u32[]{:S(2)}) copy-start(s32[32]{0:T(128)} %param.24) | copy-start | bytes 388
  212.0 3.8 collective-permute-start.3
  215.8 4.8 collective-permute-start.4
  220.6 1.3 collective-permute-start.5
  222.0 4.9 collective-permute-start.6
  227.0 6.2 %collective-permute-start.7 = (f32[16,4,768]{2,1,0:T(4,128)S(1)}, f32[16,4,768]{2,1,0:T(4,128)S(1)}, u32[]{:S(2)}, u32[]{:S(2)}) collective-permute-start(f32[16,4,768]{2,1,0:T(4,128)S(1)} %pad_maximum_fusion.3), channel_id=1, source_target_pairs={{0,16},{4,20},{8,24},{12,28},{16,0},{20,4},{24,8},{28,12},{1,17},{... | collective-permute-start | bytes 589832 | tf_op jit(solution)/shard_map/ppermute | solution.py:359
  350.5 166.7 %collective-permute-start.8 = (f32[2,12,768]{2,1,0:T(8,128)S(1)}, f32[2,12,768]{2,1,0:T(8,128)S(1)}, u32[]{:S(2)}, u32[]{:S(2)}) collective-permute-start(f32[2,12,768]{2,1,0:T(8,128)S(1)} %concatenate.53), channel_id=1, source_target_pairs={{0,4},{4,0},{8,12},{12,8},{16,20},{20,16},{24,28},{28,24},{1,5},{5... | collective-permute-start | bytes 221192 | tf_op jit(solution)/shard_map/ppermute | solution.py:359
  517.3 5.3 collective-permute-start.9
  517.3 6.4 %copy-start = (f32[768,768]{1,0:T(8,128)S(1)}, f32[768,768]{1,0:T(8,128)}, u32[]{:S(2)}) copy-start(f32[768,768]{1,0:T(8,128)} %get-tuple-element.58) | copy-start | bytes 7077892
  522.6 4.7 collective-permute-start.10
  527.3 15.5 %collective-permute-start.11 = (f32[2,12,768]{2,1,0:T(8,128)S(1)}, f32[2,12,768]{2,1,0:T(8,128)S(1)}, u32[]{:S(2)}, u32[]{:S(2)}) collective-permute-start(f32[2,12,768]{2,1,0:T(8,128)S(1)} %add.138), channel_id=1, source_target_pairs={{0,1},{1,0},{2,3},{3,2},{4,5},{5,4},{6,7},{7,6},{8,9},{9,8},{10,11... | collective-permute-start | bytes 221192 | tf_op jit(solution)/shard_map/ppermute | solution.py:364
  542.8 6.6 %collective-permute-start.12 = (f32[2,12,768]{2,1,0:T(8,128)S(1)}, f32[2,12,768]{2,1,0:T(8,128)S(1)}, u32[]{:S(2)}, u32[]{:S(2)}) collective-permute-start(f32[2,12,768]{2,1,0:T(8,128)S(1)} %add.139), channel_id=1, source_target_pairs={{0,2},{1,3},{2,0},{3,1},{4,6},{5,7},{6,4},{7,5},{8,10},{9,11},{10,... | collective-permute-start | bytes 221192 | tf_op jit(solution)/shard_map/ppermute | solution.py:364

commit v4 on v1

v4 whole, which is shorter than its diff:
```python
import functools
import math

import jax
import jax.numpy as jnp
from jax import lax
from jax.experimental import pallas as pl
from jax.experimental.pallas import tpu as pltpu
from jax.sharding import PartitionSpec as P

HEAD_DIM = 64
EPS_NORM = 1e-12
INV_TEMP = 50.0
PRECISE_MODE = lax.Precision.HIGHEST
NEG_FILL = -1e30
RSQRT_TWO = 1.0 / math.sqrt(2.0)
RSQRT_TWOPI = 1.0 / math.sqrt(2.0 * math.pi)
F32 = jnp.float32
BF16 = jnp.bfloat16


ANY = pl.BlockSpec(memory_space=pl.ANY)

def place():
    d = lax.axis_index("dp")
    z = lax.axis_index("mp")
    nz = lax.axis_size("mp")
    core, px, py = d % 2, (d // 2) % 2, (d // 4) % 2
    peers = {
        "core": {"dp": d + 1 - 2 * core},
        "x": {"dp": d + 2 - 4 * px},
        "y": {"dp": d + 4 - 8 * py},
        "up": {"mp": lax.rem(z + 1, nz)},
        "down": {"mp": lax.rem(z + nz - 1, nz)},
    }
    return core, px, py, peers

def greet(names, peers):
    sem = pltpu.get_barrier_semaphore()
    for n in names:
        pl.semaphore_signal(sem, inc=1, device_id=peers[n], device_id_type=pl.DeviceIdType.MESH)
    pl.semaphore_wait(sem, len(names))

def spot(core, px, py):
    return core * 4 + py * 2 + px


def nn(a, b):
    return lax.dot_general(a, b, (((1,), (0,)), ((), ())), preferred_element_type=F32)
def nt(a, b):
    return lax.dot_general(a, b, (((1,), (1,)), ((), ())), preferred_element_type=F32)
def tn(a, b):
    return lax.dot_general(a, b, (((0,), (0,)), ((), ())), preferred_element_type=F32)

def gelu_both(u):
    w = jnp.abs(u) * RSQRT_TWO
    t = 1.0 / (1.0 + 0.3275911 * w)
    e = jnp.exp(-0.5 * u * u)
    poly = ((((1.061405429 * t - 1.453152027) * t + 1.421413741) * t - 0.284496736) * t + 0.254829592) * t
    tail = 0.5 * poly * e
    phi = jnp.where(u >= 0.0, 1.0 - tail, tail)
    return u * phi, phi + u * e * RSQRT_TWOPI

def norm_rows(z, gain, bias):
    c = z - jnp.mean(z, axis=-1, keepdims=True)
    r = lax.rsqrt(jnp.mean(c * c, axis=-1, keepdims=True) + EPS_NORM)
    n = c * r
    return n, r, n * gain + bias

ROWS = 256

class Refs:
    def __init__(self, **k):
        self.__dict__.update(k)

def far_peers():
    d = lax.axis_index("dp")
    found = {}
    bit = 8
    while bit < lax.axis_size("dp"):
        high = (d // bit) % 2
        found[f"far{bit}"] = {"dp": d + bit - 2 * bit * high}
        bit *= 2
    return found


class Weights:
    def __init__(self, r, ways, layers):
        self.r, self.ways, self.layers = r, ways, layers
        self.core, self.px, self.py, self.peers = place()
        core, px, py = self.core, self.px, self.py
        self.rows = r.w.shape[3] // 2
        self.part = r.w.shape[3]
        self.me = spot(core, px, py)
        sx, sy, sd = spot(core, 1 - px, py), spot(core, px, 1 - py), spot(core, 1 - px, 1 - py)
        half = self.rows // 2
        self.plane = [
            ("x", self.me, sx, 0, self.rows), ("y", self.me, sy, 0, self.rows),
            ("y", sx, sd, 0, half), ("x", sy, sd, half, half),
            ("core", self.me, spot(1 - core, px, py), 0, self.rows),
            ("core", sx, spot(1 - core, 1 - px, py), 0, self.rows),
            ("core", sy, spot(1 - core, px, 1 - py), 0, self.rows),
            ("core", sd, spot(1 - core, 1 - px, 1 - py), 0, self.rows),
        ]
    def region(self, l, j, k, slot, lo=0, n=None):
        n = self.rows if n is None else n
        rows = pl.ds(pl.multiple_of((slot % 2) * self.rows + lo, 16), n)
        if j == 0:
            return self.r.w.at[3 * l, slot // 2, k, rows]
        return self.r.w.at[3 * l + j, k, slot // 2, rows]
    def source(self, l, j):
        return (self.r.pack, self.r.up_w, self.r.down_w)[j].at[l]
    def remote(self, src, dst, send, recv, index, peer):
        return pltpu.make_async_remote_copy(
            src_ref=src, dst_ref=dst, send_sem=send.at[index], recv_sem=recv.at[index],
            device_id=self.peers[peer], device_id_type=pl.DeviceIdType.MESH)
    def z_copy(self, l, j, k):
        if k == 1:
            src = self.source(l, j).at[pl.ds(pl.multiple_of(self.me * self.rows, 16), self.rows)]
        else:
            src = self.region(l, j, k - 1, self.me)
        return self.remote(src, self.region(l, j, k, self.me), self.r.z_send, self.r.z_recv, (l * 3 + j) * (self.ways - 1) + k - 1, "z1")
    def p_copy(self, l, j, k, i, received=False):
        peer, sent, got, lo, n = self.plane[i]
        reg = self.region(l, j, k, got if received else sent, lo, n)
        index = ((l * 3 + j) * (self.ways - 1) + k - 1) * len(self.plane) + i
        return self.remote(reg, reg, self.r.p_send, self.r.p_recv, index, peer)
    def own_copy(self, l, j):
        src, dst = self.source(l, j), self.r.w.at[3 * l + j, 0]
        if j == 0:
            dst = self.r.w.at[3 * l, :, 0]
        return self.remote(src.reshape(4, self.part, src.shape[-1]), dst, self.r.own_send, self.r.own_recv, l * 3 + j, "core")
    def first(self, l, j, k):
        self.z_copy(l, j, k).wait_recv()
        if k + 1 < self.ways:
            self.z_copy(l, j, k + 1).start()
        else:
            @pl.when(l + 1 < self.layers)
            def _():
                self.z_copy(l + 1, j, 1).start()
        for i in (0, 1, 4):
            self.p_copy(l, j, k, i).start()
    def second(self, l, j, k):
        self.p_copy(l, j, k, 0, True).wait_recv()
        self.p_copy(l, j, k, 2).start()
        self.p_copy(l, j, k, 5).start()
        self.p_copy(l, j, k, 1, True).wait_recv()
        self.p_copy(l, j, k, 3).start()
        self.p_copy(l, j, k, 6).start()
    def third(self, l, j, k):
        self.p_copy(l, j, k, 2, True).wait_recv()
        self.p_copy(l, j, k, 3, True).wait_recv()
        self.p_copy(l, j, k, 7).start()
    def tick(self, l, step):
        last = self.ways - 1
        def group(n):
            return l + n // 3, n % 3
        now = [(*group(step + i), last - i) for i in range(last)]
        before = [(*group(step - 1 + i), last - i) for i in range(last)]
        def op(kind, item):
            def go():
                if item[0] is l:
                    kind(*item)
                else:
                    @pl.when(item[0] < self.layers)
                    def _():
                        kind(*item)
            return go
        line = before[1:] + now
        ops = []
        for i, item in enumerate(now):
            ops.append(op(self.first, item))
            ops.append(op(self.second, line[last - 2 + i]))
            ops.append(op(self.third, line[last - 3 + i]))
        return ops
    def arrived(self, l, j):
        for k in range(1, self.ways):
            for i in range(4, 8):
                self.p_copy(l, j, k, i, True).wait_recv()
        self.own_copy(l, j).wait_recv()
    def sent(self, l, j):
        for k in range(1, self.ways):
            self.z_copy(l, j, k).wait_send()
            for i in range(len(self.plane)):
                self.p_copy(l, j, k, i).wait_send()
        self.own_copy(l, j).wait_send()

QB, VB, UB, OB, GAIN, BIAS, DB = 0, 1, 2, 6, 7, 9, 11

class Forward:
    def __init__(self, l, seqs, r):
        self.l, self.seqs, self.r = l, seqs, r
        T = r.x.shape[0]
        self.blocks = [slice(i, i + ROWS) for i in range(0, T, ROWS)]
    def par(self, row):
        return self.r.par[self.l, row:row + 1]
    def project(self, m):
        r, l = self.r, self.l
        acc = nt(r.xr[...], r.w_attn[m].reshape(-1, r.x.shape[1]))
        if m == 0:
            r.q[...] = (acc + self.par(QB)).astype(BF16) * jnp.bfloat16(0.125)
        elif m == 1:
            r.k[...] = acc.astype(BF16)
        else:
            r.v[...] = (acc + self.par(VB)).astype(BF16)
    def attend(self, s, i):
        r, l = self.r, self.l
        start, n = self.seqs[s]
        rows = slice(start, start + n)
        lanes = pl.ds(pl.multiple_of(i * 128, 128), 128)
        kp, qp, vp = r.k[rows, lanes], r.q[rows, lanes], r.v[rows, lanes]
        vt = vp.T
        first = lax.broadcasted_iota(jnp.int32, (n, 128), 1) < HEAD_DIM
        bias = jnp.concatenate([r.mask[rows]] * (n // 128), axis=1)
        out = []
        for h in range(2):
            kh = jnp.where(first if h == 0 else ~first, kp, jnp.zeros_like(kp))
            sc = nt(kh, qp) + bias
            top = jnp.max(sc, axis=0, keepdims=True)
            e = jnp.exp(sc - top)
            tot = jnp.sum(e, axis=0, keepdims=True)
            r.lse[i, h:h + 1, rows] = top + jnp.log(tot)
            ct = nn(vt[h * HEAD_DIM:(h + 1) * HEAD_DIM], e.astype(BF16))
            out.append(ct * (1.0 / tot))
        ct = jnp.concatenate(out, axis=0)
        r.ctx[rows, lanes] = ct.T.astype(BF16)
    def out_norm(self, b):
        r, l = self.r, self.l
        z = r.x[b] + nn(r.ctx[b], r.w_attn[3].reshape(-1, r.x.shape[1])) + self.par(OB)
        n, inv, h = norm_rows(z, self.par(GAIN), self.par(BIAS))
        r.n1[b] = n
        r.r1[b] = jnp.broadcast_to(inv, (ROWS, 128))
        r.hr[b] = h.astype(BF16)
        r.x[b] = h + self.par(DB)
    def ffn(self, c, b, slot):
        r, l = self.r, self.l
        u = nn(r.hr[b], r.w_up[c].reshape(r.x.shape[1], -1)) + r.up_b[l, c]
        a, slope = gelu_both(u)
        a = a.astype(BF16)
        r.a[slot, b] = a
        r.slope[slot, b] = slope.astype(BF16)
        r.x[b] += nn(a, r.w_down[c].reshape(-1, r.x.shape[1]))
    def ffn_norm(self, b):
        r, l = self.r, self.l
        n, inv, y = norm_rows(r.x[b], self.par(GAIN + 1), self.par(BIAS + 1))
        r.n2[b] = n
        r.r2[b] = jnp.broadcast_to(inv, (ROWS, 128))
        r.x[b] = y
        r.xr[b] = y.astype(BF16)

def contrast(r, z, seqs, ways, extra):
    d, me = lax.axis_index("dp"), lax.axis_index("mp")
    rank = d * ways + me
    q_slots, p_slots = r.q_in.shape[0], r.p_in.shape[0]
    width = r.x.shape[1]
    parts = width // 128
    shape = r.emb.shape
    count = 1
    for size in shape[:-2]:
        count *= size
    block = shape[-2]
    flat = r.emb.reshape(count * block, 128)
    invs, sizes = [], []
    lane = lax.broadcasted_iota(jnp.int32, (1, 128), 1)
    for s, (start, n) in enumerate(seqs):
        row = lax.broadcasted_iota(jnp.int32, (n, 128), 0)
        live = jnp.concatenate([row < r.lens[s]] * parts, axis=1)
        size = jnp.full((1, 1), r.lens[s], jnp.int32).astype(F32)
        pooled = jnp.sum(jnp.where(live, r.x[start:start + n], 0.0), axis=0, keepdims=True) / size
        inv = lax.rsqrt(jnp.sum(pooled * pooled, axis=1, keepdims=True) + 1e-06)
        normed = pooled * inv
        for c in range(parts):
            r.own_rows[s * parts + c:s * parts + c + 1] = normed[:, c * 128:(c + 1) * 128]
        invs.append(inv)
        sizes.append(size)
    at = len(seqs) * parts
    marks = jnp.zeros((1, 128), F32)
    values = [r.positive[j] for j in range(q_slots)] + [r.q_count[rank], r.p_count[rank]]
    for i, value in enumerate(values):
        marks = jnp.where(lane == i, jnp.full((1, 128), value, jnp.int32).astype(F32), marks)
    r.own_rows[at:] = jnp.zeros((block - at, 128), F32)
    r.own_rows[at:at + 1] = marks
    flat[pl.ds(pl.multiple_of(rank * block, 8), block)] = r.own_rows[...]
    bits = []
    bit = lax.axis_size("dp") // 2
    while bit:
        bits.append(bit)
        bit //= 2
    name_of = {1: "core", 2: "x", 4: "y"}
    mine = [(d // b) % 2 for b in bits]
    steps = []
    span = 1
    while span < ways:
        low = me - lax.rem(me, span)
        other = me + span - 2 * span * lax.rem(me // span, 2)
        steps.append((tuple(mine) + (pl.ds(low, span),), tuple(mine) + (pl.ds(other - lax.rem(other, span), span),), {"mp": other}))
        span *= 2
    held = list(mine)
    for i, b in enumerate(bits):
        there = list(held)
        there[i] = 1 - mine[i]
        steps.append((tuple(held), tuple(there), z.peers[name_of.get(b, f"far{b}")]))
        held[i] = slice(None)
    copies = []
    for i, (here, there, peer) in enumerate(steps):
        def move(where):
            return pltpu.make_async_remote_copy(
                src_ref=r.emb.at[where], dst_ref=r.emb.at[where], send_sem=r.e_send.at[i], recv_sem=r.e_recv.at[i],
                device_id=peer, device_id_type=pl.DeviceIdType.MESH)
        copies.append(move(here))
        copies[-1].start()
        move(there).wait_recv()
    def rows(i):
        return flat[pl.ds(i, count, stride=block), :]
    def precise(a, b, dims):
        return lax.dot_general(a, b, (dims, ((), ())), precision=PRECISE_MODE, preferred_element_type=F32)
    q = [[rows(j * parts + c) for c in range(parts)] for j in range(q_slots)]
    p = [[rows((q_slots + i) * parts + c) for c in range(parts)] for i in range(p_slots)]
    marks = rows(at)
    marks_t = marks.T
    down = lax.broadcasted_iota(jnp.int32, (count, count), 0)
    across = lax.broadcasted_iota(jnp.int32, (count, count), 1)
    live_total = jnp.sum(marks[:, q_slots:q_slots + 1], axis=0, keepdims=True)
    scale = float(count * q_slots * seqs[0][1])
    loss = jnp.zeros((1, 1), F32)
    dn = [[jnp.zeros((1, 128), F32) for _ in range(parts)] for _ in seqs]
    for j in range(q_slots):
        sims, masked, is_pos = [], [], []
        for i in range(p_slots):
            s = precise(q[j][0], p[i][0], ((1,), (1,)))
            for c in range(1, parts):
                s = s + precise(q[j][c], p[i][c], ((1,), (1,)))
            s = INV_TEMP * s
            sims.append(s)
            masked.append(jnp.where(marks_t[q_slots + 1:q_slots + 2] > i, s, NEG_FILL))
            is_pos.append(jnp.where((across * p_slots + i).astype(F32) == marks[:, j:j + 1], 1.0, 0.0))
        top = functools.reduce(jnp.maximum, [jnp.max(s, axis=1, keepdims=True) for s in masked])
        expo = [jnp.exp(s - top) for s in masked]
        tot = sum(jnp.sum(e, axis=1, keepdims=True) for e in expo)
        pos = sum(jnp.sum(m * s, axis=1, keepdims=True) for m, s in zip(is_pos, sims))
        live = jnp.where(marks[:, q_slots:q_slots + 1] > j, 1.0, 0.0)
        loss = loss + jnp.sum(live * (top + jnp.log(tot) - pos), axis=0, keepdims=True)
        for i in range(p_slots):
            ds = (scale * live / live_total) * (expo[i] / tot - is_pos[i])
            row = jnp.sum(jnp.where(down == rank, ds, 0.0), axis=0, keepdims=True)
            row = jnp.broadcast_to(row, (8, count))
            col = jnp.sum(jnp.where(across == rank, ds, 0.0), axis=1, keepdims=True)
            for c in range(parts):
                dn[j][c] = dn[j][c] + INV_TEMP * precise(row, p[i][c], ((1,), (0,)))[0:1]
                dn[q_slots + i][c] = dn[q_slots + i][c] + INV_TEMP * jnp.sum(col * q[j][c], axis=0, keepdims=True)
    r.loss[...] = jnp.broadcast_to(loss / live_total, r.loss.shape)
    r.token[...] = jnp.zeros(r.token.shape, F32)
    for s in range(len(seqs)):
        normed = [r.own_rows[s * parts + c:s * parts + c + 1] for c in range(parts)]
        along = sum(jnp.sum(a * b, axis=1, keepdims=True) for a, b in zip(normed, dn[s]))
        for c in range(parts):
            r.token[s:s + 1, c * 128:(c + 1) * 128] = invs[s] * (dn[s][c] - normed[c] * along) / sizes[s]
    for copy in copies:
        copy.wait_send()


def forward_kernel(seqs, layers, ways, names, *refs):
    r = Refs(**dict(zip(names, refs)))
    z = Weights(r, ways, layers)
    width = r.x.shape[1]
    zpeers = []
    for k in range(1, ways):
        zpeers.append(f"z{k}")
        z.peers[f"z{k}"] = {"mp": lax.rem(lax.axis_index("mp") + k, ways)}
    part = z.part
    for l in range(layers):
        for m in range(3):
            r.pack[l, m * part:(m + 1) * part] = r.qkv_w[l, m]
        r.pack[l, 3 * part:] = r.out_w[l]
    r.tiny[0] = r.tiny_in[...]
    extra = far_peers()
    z.peers.update(extra)
    greet(["core", "x", "y"] + zpeers + list(extra), z.peers)
    def tiny_copy(k):
        return z.remote(r.tiny.at[0], r.tiny.at[k], r.t_send, r.t_recv, k - 1, f"z{k}")
    z.z_copy(0, 0, 1).start()
    for k in range(1, ways):
        tiny_copy(k).start()
    for l in range(layers):
        for j in range(3):
            z.own_copy(l, j).start()
    for s, (start, n) in enumerate(seqs):
        row = lax.broadcasted_iota(jnp.int32, (n, 128), 0)
        r.mask[start:start + n] = jnp.where(row < r.lens[s], 0.0, NEG_FILL)
    at = 0
    for ref in (r.q_in, r.p_in):
        for i in range(ref.shape[0]):
            r.xr[at:at + ref.shape[1]] = ref[i]
            r.x[at:at + ref.shape[1]] = ref[i].astype(F32)
            at += ref.shape[1]
    out_b, down_b = r.out_b_in[...].astype(F32), r.down_b_in[...].astype(F32)
    for l in range(layers):
        r.par[l, OB:OB + 1] = out_b[l:l + 1]
        r.par[l, DB:DB + 1] = down_b[l:l + 1]
        r.par[l, GAIN:GAIN + 2] = r.gain_in[l].astype(F32)
        r.par[l, BIAS:BIAS + 2] = r.bias_in[l].astype(F32)
    z.first(0, 0, 1)
    z.z_copy(0, 1, 1).start()
    z.z_copy(0, 2, 1).start()
    z.first(0, 0, 2)
    z.second(0, 0, 1)
    z.first(0, 1, 1)
    z.second(0, 0, 2)
    z.third(0, 0, 1)
    z.first(0, 0, 3)
    z.second(0, 1, 1)
    z.third(0, 0, 2)
    z.first(0, 1, 2)
    z.second(0, 0, 3)
    z.third(0, 1, 1)
    for k in range(1, ways):
        tiny_copy(k).wait_recv()
    for l in range(layers):
        for i in range(2):
            row = r.tiny[0, 2 * l + i:2 * l + i + 1].astype(F32)
            for k in range(1, ways):
                row = row + pltpu.roll(r.tiny[k, 2 * l + i:2 * l + i + 1].astype(F32), k * part, 1)
            r.par[l, i:i + 1] = row
        for k in range(ways):
            r.up_b[l, k] = r.tiny[k, 2 * layers + l:2 * layers + l + 1].astype(F32)
    z.first(0, 2, 1)
    z.second(0, 1, 2)
    z.third(0, 0, 3)
    kept = ("xr", "q", "k", "v", "ctx", "lse", "n1", "r1", "hr", "n2", "r2")
    def keep(l, name):
        return pltpu.make_async_copy(getattr(r, name), getattr(r, name + "_out").at[l], r.k_sem.at[l * len(kept) + kept.index(name)])
    bufs = [r.w_attn, r.w_up, r.w_down]
    def load(l, j):
        return pltpu.make_async_copy(r.w.at[3 * l + j], bufs[j], r.w_sem.at[3 * l + j])
    def save(l, c, j):
        src, dst = ((r.a, r.a_out), (r.slope, r.slope_out))[j]
        return pltpu.make_async_copy(src.at[lax.rem(c, 2)], dst.at[l, c], r.s_sem.at[(l * ways + c) * 2 + j])
    z.arrived(0, 0)
    load(0, 0).start()
    pairs = width // 128
    def layer(l, _):
        f = Forward(l, seqs, r)
        more = l + 1 < layers
        early = z.tick(l, 1) + z.tick(l, 2)
        late = z.tick(l, 3)
        def run(ops, n):
            for _ in range(min(n, len(ops))):
                ops.pop(0)()
        keep(l, "xr").start()
        load(l, 0).wait()
        for m in range(3):
            f.project(m)
            keep(l, "qkv"[m]).start()
            run(early, 1)
        def pair(i, _):
            for s in range(len(seqs)):
                f.attend(s, i)
            for at in range(pairs):
                @pl.when(i == at)
                def _():
                    run(early, 2)
            return 0
        lax.fori_loop(0, pairs, pair, 0)
        keep(l, "ctx").start()
        keep(l, "lse").start()
        for b in f.blocks:
            f.out_norm(b)
            run(early, 1)
        for name in ("n1", "r1", "hr"):
            keep(l, name).start()
        run(early, len(early))
        z.arrived(l, 1)
        load(l, 1).start()
        z.arrived(l, 2)
        load(l, 2).start()
        load(l, 1).wait()
        load(l, 2).wait()
        def chunk(c, _):
            @pl.when(c >= 2)
            def _():
                for j in range(2):
                    save(l, c - 2, j).wait()
            for b in f.blocks:
                f.ffn(c, b, lax.rem(c, 2))
            for j in range(2):
                save(l, c, j).start()
            for at in range(ways):
                @pl.when(c == at)
                def _():
                    run(late, 3)
            return 0
        lax.fori_loop(0, ways, chunk, 0)
        for c in range(ways - 2, ways):
            for j in range(2):
                save(l, c, j).wait()
        @pl.when(more)
        def _():
            z.arrived(l + 1, 0)
            load(l + 1, 0).start()
        for name in kept[:-2]:
            keep(l, name).wait()
        @pl.when(l > 0)
        def _():
            for name in kept[-2:]:
                keep(l - 1, name).wait()
        for b in f.blocks:
            f.ffn_norm(b)
        for name in kept[-2:]:
            keep(l, name).start()
        return 0
    lax.fori_loop(0, layers, layer, 0)
    contrast(r, z, seqs, ways, extra)
    def finish(l, _):
        for j in range(3):
            z.sent(l, j)
        return 0
    lax.fori_loop(0, layers, finish, 0)
    for k in range(1, ways):
        tiny_copy(k).wait_send()
    for name in kept[-2:]:
        keep(layers - 1, name).wait()

def forward(query_states, passage_states, qkv_w, out_w, up_w, down_w, lens, targets, tiny, shared, seqs, ways, collective_id):
    D = query_states.shape[-1]
    T = sum(n for _, n in seqs)
    L = qkv_w.shape[0]
    R = up_w.shape[-1]
    G = 3 * L
    V = pl.BlockSpec(memory_space=pltpu.VMEM)
    S = pl.BlockSpec(memory_space=pltpu.SMEM)
    heads = D // HEAD_DIM
    ins = dict(lens=(lens, S), q_in=(query_states, V), p_in=(passage_states, V), qkv_w=(qkv_w, V), out_w=(out_w, V),
               up_w=(up_w, ANY), down_w=(down_w, ANY), tiny_in=(tiny, V))
    for name, value in zip(("out_b_in", "gain_in", "bias_in", "down_b_in"), shared):
        ins[name] = (value, V)
    for name, value in zip(("positive", "q_count", "p_count"), targets):
        ins[name] = (value, S)
    states = dict(xr=((T, D), BF16), q=((T, D), BF16), k=((T, D), BF16), v=((T, D), BF16), ctx=((T, D), BF16),
                  lse=((heads // 2, 8, T), F32), n1=((T, D), F32), r1=((T, 128), F32), hr=((T, D), BF16), n2=((T, D), F32), r2=((T, 128), F32))
    outs = dict(loss=((8, 128), F32, V), token=((-(-len(seqs) // 8) * 8, D), F32, V))
    for name, (shape, kind) in states.items():
        outs[name + "_out"] = ((L, *shape), kind, ANY)
    outs.update(a_out=((L, ways, T, R), BF16, ANY), slope_out=((L, ways, T, R), BF16, ANY), w=((G, ways, 4, R // 4, D), BF16, ANY))
    VM, DMA = pltpu.VMEM, pltpu.SemaphoreType.DMA
    waves = G * (ways - 1)
    scratch = {name: VM(shape, kind) for name, (shape, kind) in states.items()}
    nbits = 0
    while 1 << nbits < lax.axis_size("dp"):
        nbits += 1
    block = -(-(len(seqs) * (D // 128) + 1) // 8) * 8
    scratch.update(
        x=VM((T, D), F32), emb=VM((2,) * nbits + (ways, block, 128), F32), own_rows=VM((block, 128), F32),
        e_send=DMA((nbits + ways,)), e_recv=DMA((nbits + ways,)))
    scratch.update(
        mask=VM((T, 128), F32), par=VM((L, 16, D), F32), up_b=VM((L, ways, 1, R), F32), pack=VM((L, R, D), BF16), tiny=VM((ways, 16, D), BF16),
        a=VM((2, T, R), BF16), slope=VM((2, T, R), BF16),
        w_attn=VM((4, ways, R // 4, D), BF16), w_up=VM((ways, 4, R // 4, D), BF16), w_down=VM((ways, 4, R // 4, D), BF16),
        w_sem=DMA((G,)), s_sem=DMA((L * ways * 2,)), k_sem=DMA((L * 11,)), z_send=DMA((waves,)), z_recv=DMA((waves,)),
        p_send=DMA((waves * 8,)), p_recv=DMA((waves * 8,)), own_send=DMA((G,)), own_recv=DMA((G,)),
        t_send=DMA((ways - 1,)), t_recv=DMA((ways - 1,)))
    names = tuple(ins) + tuple(outs) + tuple(scratch)
    res = pl.pallas_call(
        functools.partial(forward_kernel, seqs, L, ways, names),
        out_shape=[jax.ShapeDtypeStruct(s, d) for s, d, _ in outs.values()],
        in_specs=[s for _, s in ins.values()],
        out_specs=[s for _, _, s in outs.values()],
        scratch_shapes=list(scratch.values()),
        compiler_params=pltpu.CompilerParams(collective_id=collective_id, has_side_effects=True, vmem_limit_bytes=62 << 20),
        name="forward_layers",
    )(*[v for v, _ in ins.values()])
    return {name.removesuffix("_out") if name[:-4] in states else name: value for name, value in zip(outs, res)}


def add_low(a, b):
    return a + b


class Reduce:
    def __init__(self, r, ways, layers):
        self.r, self.ways, self.layers = r, ways, layers
        self.core, self.px, self.py, self.peers = place()
        for k in range(1, ways):
            self.peers[f"z{k}"] = {"mp": lax.rem(lax.axis_index("mp") + k, ways)}
        self.extra = far_peers()
        self.peers.update(self.extra)
        core, px, py = self.core, self.px, self.py
        self.me = spot(core, px, py)
        sx, sy, sd = spot(core, 1 - px, py), spot(core, px, 1 - py), spot(core, 1 - px, 1 - py)
        self.plane = [
            ("x", self.me, sx, None), ("y", self.me, sy, None), ("y", sx, sd, 0), ("x", sy, sd, 1),
            ("core", self.me, spot(1 - core, px, py), None), ("core", sx, spot(1 - core, 1 - px, py), None),
            ("core", sy, spot(1 - core, px, 1 - py), None), ("core", sd, spot(1 - core, 1 - px, 1 - py), None),
        ]
        self.per = 8 + ways - 1 + len(self.extra)
    def remote(self, src, dst, sems, index, peer):
        return pltpu.make_async_remote_copy(
            src_ref=src, dst_ref=dst, send_sem=sems[0].at[index], recv_sem=sems[1].at[index],
            device_id=self.peers[peer], device_id_type=pl.DeviceIdType.MESH)
    def step(self, src, dst, t, j, i, peer):
        return self.remote(src, dst, (self.r.r_send, self.r.r_recv), (3 * t + j) * self.per + i, peer)
    def share(self, t, j, c, i):
        ref = (self.r.g_down, self.r.g_up, self.r.g_attn)[j].at[self.layers - 1 - t]
        return ref.at[2 * c + i] if j == 2 else ref.at[i, pl.ds(2 * c, 2)]
    def place_of(self, ref, j, i):
        return ref.at[:, i] if j == 2 else ref.at[i]
    def pieces(self, j):
        return range(2 if j == 2 else self.ways)
    def load(self, t, j, i):
        return pltpu.make_async_copy(self.share(t, j, self.core, i), self.place_of(self.r.own.at[j], j, i), self.r.l_sem.at[(3 * t + j) * 4 + i])
    def core_copy(self, t, j, i):
        return self.step(self.share(t, j, 1 - self.core, i), self.place_of(self.r.got.at[3 * t + j], j, i), t, j, i, "core")
    def fetch(self, t, j):
        return pltpu.make_async_copy(self.r.got.at[3 * t + j], self.r.got_v, self.r.f_sem.at[3 * t + j])
    def a1(self, t, j):
        return self.step(self.r.own.at[j, :, :, 1 - self.px, 0], self.r.got_a.at[3 * t + j], t, j, 4, "x")
    def b1(self, t, j):
        return self.step(self.r.own.at[j, :, 1 - self.py, :, 1], self.r.got_b.at[3 * t + j], t, j, 5, "y")
    def a2(self, t, j):
        return self.step(self.r.got_a.at[3 * t + j, :, 1 - self.py], self.r.got_c.at[3 * t + j], t, j, 6, "y")
    def b2(self, t, j):
        return self.step(self.r.got_b.at[3 * t + j, :, 1 - self.px], self.r.got_d.at[3 * t + j], t, j, 7, "x")
    def zc(self, t, j, s):
        return self.step(self.r.zout.at[3 * t + j, s - 1], self.r.zin.at[3 * t + j, s - 1], t, j, 7 + s, "z1")
    def slot(self, i):
        return self.ways - 1 if i == 0 else i - 1
    def fc(self, t, j, i, name):
        return self.step(self.r.zout.at[3 * t + j, self.slot(i)], self.r.far.at[3 * t + j, i], t, j, 7 + self.ways + i, name)
    def pc(self, t, j, i, received=False):
        peer, sent, got, h = self.plane[i]
        dst = self.r.reduced.at[3 * t + j, got if received else sent]
        src = self.r.zout.at[3 * t + j, self.slot(len(self.extra))] if i in (0, 1, 4) and not received else dst
        if h is not None:
            src, dst = src.at[h], dst.at[h]
        return self.remote(src, dst, (self.r.g_send, self.r.g_recv), (3 * t + j) * 8 + i, peer)
    def mine(self, t, j):
        return pltpu.make_async_copy(self.r.zout.at[3 * t + j, self.slot(len(self.extra))], self.r.reduced.at[3 * t + j, self.me], self.r.m_sem.at[3 * t + j])
    def s0(self, t, j, i):
        self.core_copy(t, j, i).start()
        self.load(t, j, i).start()
    def s1(self, t, j):
        r = self.r
        for i in self.pieces(j):
            self.core_copy(t, j, i).wait_recv()
        self.fetch(t, j).start()
        for i in self.pieces(j):
            self.load(t, j, i).wait()
        self.fetch(t, j).wait()
        def body(k, _):
            for y in range(2):
                r.own[j, k, y] = add_low(r.own[j, k, y], r.got_v[k, y])
            return 0
        lax.fori_loop(0, self.ways, body, 0)
        self.a1(t, j).start()
        self.b1(t, j).start()
    def s2(self, t, j):
        r, g, px, py = self.r, 3 * t + j, self.px, self.py
        self.a1(t, j).wait_recv()
        def body(k, _):
            for y in range(2):
                r.got_a[g, k, y] = add_low(r.own[j, k, y, px, 0], r.got_a[g, k, y])
            return 0
        lax.fori_loop(0, self.ways, body, 0)
        self.a2(t, j).start()
        self.b1(t, j).wait_recv()
        def body(k, _):
            for x in range(2):
                r.got_b[g, k, x] = add_low(r.own[j, k, py, x, 1], r.got_b[g, k, x])
            return 0
        lax.fori_loop(0, self.ways, body, 0)
        self.b2(t, j).start()
        self.a1(t, j).wait_send()
        self.b1(t, j).wait_send()
    def part(self, g, k):
        r = self.r
        left = add_low(r.got_a[g, k, self.py], r.got_c[g, k])
        right = add_low(r.got_b[g, k, self.px], r.got_d[g, k])
        return left, right
    def s3(self, t, j):
        g = 3 * t + j
        self.a2(t, j).wait_recv()
        self.b2(t, j).wait_recv()
        for h, value in enumerate(self.part(g, 1)):
            self.r.zout[g, 0, h] = value
        self.zc(t, j, 1).start()
    def sz(self, t, j, s):
        r, g = self.r, 3 * t + j
        self.zc(t, j, s).wait_recv()
        for h, value in enumerate(self.part(g, (s + 1) % self.ways)):
            r.zout[g, s, h] = add_low(r.zin[g, s - 1, h], value)
        if s < self.ways - 1:
            self.zc(t, j, s + 1).start()
    def sz1(self, t, j):
        self.sz(t, j, 1)
    def sz2(self, t, j):
        for s in range(2, self.ways - 1):
            self.sz(t, j, s)
    def sp(self, t, j):
        r, g = self.r, 3 * t + j
        self.sz(t, j, self.ways - 1)
        for s in range(1, self.ways):
            self.zc(t, j, s).wait_send()
        for i, name in enumerate(self.extra):
            self.fc(t, j, i, name).start()
            self.fc(t, j, i, name).wait_recv()
            r.zout[g, self.slot(i + 1)] = add_low(r.zout[g, self.slot(i)], r.far[g, i])
        self.mine(t, j).start()
        for i in (0, 1, 4):
            self.pc(t, j, i).start()
    def sq(self, t, j):
        self.pc(t, j, 0, True).wait_recv()
        self.pc(t, j, 2).start()
        self.pc(t, j, 5).start()
        self.pc(t, j, 1, True).wait_recv()
        self.pc(t, j, 3).start()
        self.pc(t, j, 6).start()
    def sr(self, t, j):
        self.pc(t, j, 2, True).wait_recv()
        self.pc(t, j, 3, True).wait_recv()
        self.pc(t, j, 7).start()
    def end(self, t, j):
        for i in range(4, 8):
            self.pc(t, j, i, True).wait_recv()
        self.mine(t, j).wait()
        for i in self.pieces(j):
            self.core_copy(t, j, i).wait_send()
        self.a2(t, j).wait_send()
        self.b2(t, j).wait_send()
        for i, name in enumerate(self.extra):
            self.fc(t, j, i, name).wait_send()
        for i in range(8):
            self.pc(t, j, i).wait_send()


def norm_back(g, n, r, gain):
    gn = g * gain
    return r * (gn - jnp.mean(gn, axis=-1, keepdims=True) - n * jnp.mean(gn * n, axis=-1, keepdims=True))


def total(v):
    return jnp.sum(v, axis=0, keepdims=True)


class Backward:
    def __init__(self, l, seqs, r):
        self.l, self.seqs, self.r = l, seqs, r
        T = r.dy.shape[0]
        self.blocks = [slice(i, i + ROWS) for i in range(0, T, ROWS)]
    def add_row(self, row, value, first):
        r, l = self.r, self.l
        if first:
            r.sums[l, row:row + 1] = value
        else:
            r.sums[l, row:row + 1] += value
    def norm(self, b, which):
        r, l = self.r, self.l
        g = r.dy[b] if which else r.dz[b]
        n, inv = r.n[b], r.inv[b]
        inv = jnp.concatenate([inv] * (n.shape[1] // 128), axis=1)
        dz = norm_back(g, n, inv, r.gain[l, which:which + 1])
        low = dz.astype(BF16)
        r.dz[b] = dz
        r.low[b] = low
        first = b.start == 0
        self.add_row(GAIN + which, total(g * n), first)
        self.add_row(BIAS + which, total(g), first)
        self.add_row(DB if which else OB, total(low.astype(F32)), first)
    def put(self, slot, value):
        stage = self.r.stage
        stage[slot] = value.astype(BF16).reshape(stage.shape[1:])
    def ffn_down(self, slot):
        self.put(0, nn(self.r.low_t[...], self.r.a[slot]))
    def ffn_mid(self, c, b, slot, w):
        r, l = self.r, self.l
        da = nt(r.low[b], r.w[w])
        du = (da * r.slope[slot, b].astype(F32)).astype(BF16)
        r.du[b] = du
        if b.start == 0:
            r.su[l, c] = total(du.astype(F32))
        else:
            r.su[l, c] += total(du.astype(F32))
    def ffn_up(self):
        self.put(1, nn(self.r.hr_t[...], self.r.du[...]))
    def ffn_back(self, b, w):
        r = self.r
        r.dz[b] += nt(r.du[b], r.w[w])
    def context(self, b, w):
        r = self.r
        r.dctx[b] = nt(r.low[b], r.w[w]).astype(BF16)
    def out_grad(self, slot):
        r = self.r
        self.put(slot, nn(r.hc[...].T, r.low[...]))
    def attend(self, s, i):
        r = self.r
        start, n = self.seqs[s]
        rows = slice(start, start + n)
        lanes = pl.ds(pl.multiple_of(i * 128, 128), 128)
        kp, qp, vp, gp = r.k[rows, lanes], r.q[rows, lanes], r.v[rows, lanes], r.dctx[rows, lanes]
        kt = kp.T
        first = lax.broadcasted_iota(jnp.int32, (n, 128), 1) < HEAD_DIM
        bias = jnp.concatenate([r.mask[rows]] * (n // 128), axis=1)
        dv, dk, dq = [], [], []
        for h in range(2):
            keep = first if h == 0 else ~first
            kh = jnp.where(keep, kp, jnp.zeros_like(kp))
            vh = jnp.where(keep, vp, jnp.zeros_like(vp))
            p = jnp.exp(nt(kh, qp) + bias - r.lse[i, h:h + 1, rows])
            dp = nt(vh, gp)
            ds = (p * (dp - jnp.sum(p * dp, axis=0, keepdims=True))).astype(BF16)
            dv.append(nn(p.astype(BF16), gp))
            dk.append(nn(ds, qp))
            dq.append(nn(kt[h * HEAD_DIM:(h + 1) * HEAD_DIM], ds) * 0.125)
        r.dk[rows, lanes] = jnp.where(first, dk[0], dk[1]).astype(BF16)
        r.dv[rows, lanes] = jnp.where(first, dv[0], dv[1]).astype(BF16)
        r.dq[rows, lanes] = jnp.concatenate(dq, axis=0).T.astype(BF16)
    def qkv_grad(self, m, slot):
        r = self.r
        g = (r.dq, r.dk, r.dv)[m][...]
        self.put(slot, nn(g.T, r.du[...]))
        if m != 1:
            self.add_row(QB if m == 0 else VB, total(g.astype(F32)), True)
    def back_in(self, b, m, w):
        r = self.r
        d = nn((r.dq, r.dk, r.dv)[m][b], r.w[w])
        if m == 0:
            r.dy[b] = r.dz[b] + d
        else:
            r.dy[b] += d


def backward_kernel(seqs, layers, ways, names, *refs):
    r = Refs(**dict(zip(names, refs)))
    if r.low_t.shape == r.dy.shape:
        r.dctx, r.dq = r.low_t, r.hr_t
    red = Reduce(r, ways, layers)
    far = list(red.extra)
    greet(["core", "x", "y"] + [f"z{k}" for k in range(1, ways)] + far, red.peers)
    for s, (start, n) in enumerate(seqs):
        row = lax.broadcasted_iota(jnp.int32, (n, 128), 0)
        r.mask[start:start + n] = jnp.where(row < r.lens[s], 0.0, NEG_FILL)
    each = 2 * ways + 4
    heads_order = (3, 0, 1, 2)
    def wload(t, local, group, block):
        return pltpu.make_async_copy(r.w_in.at[group, block], r.w.at[lax.rem(local, 4)], r.w_sem.at[t * each + local])
    def ffn_w(t, c, half):
        return wload(t, 2 * c + half, 3 * (layers - 1 - t) + 2 - half, c)
    def attn_w(t, i):
        return wload(t, 2 * ways + i, 3 * (layers - 1 - t), heads_order[i])
    items = ("n2", "r2", "hr", "n1", "r1", "ctx", "q", "k", "v", "lse", "xr")
    dst = dict(n2=r.n, n1=r.n, r2=r.inv, r1=r.inv, hr=r.hc, ctx=r.hc, q=r.q, k=r.k, v=r.v, lse=r.lse, xr=r.du)
    src = {name: getattr(r, name + "_in") for name in items}
    def load(l, name):
        return pltpu.make_async_copy(src[name].at[l], dst[name], r.i_sem.at[l * len(items) + items.index(name)])
    def aload(l, c, j):
        return pltpu.make_async_copy((r.a_in, r.slope_in)[j].at[l, c], (r.a, r.slope)[j].at[lax.rem(c, 2)], r.a_sem.at[(l * ways + c) * 2 + j])
    def ffn_save(l, c, j):
        return pltpu.make_async_copy(r.stage.at[j], (r.g_down, r.g_up)[j].at[l, c], r.o_sem.at[l * each + 2 * c + j])
    def attn_save(l, m, slot):
        return pltpu.make_async_copy(r.stage.at[slot], r.g_attn.at[l, m], r.o_sem.at[l * each + 2 * ways + m])
    top = layers - 1
    for c in range(2):
        for half in range(2):
            ffn_w(0, c, half).start()
    for name in ("n2", "r2", "hr"):
        load(top, name).start()
    for c in range(2):
        for j in range(2):
            aload(top, c, j).start()
    for name in ("q", "k", "v", "lse"):
        load(top, name).start()
    for s, (start, n) in enumerate(seqs):
        row = lax.broadcasted_iota(jnp.int32, (n, r.dy.shape[1]), 0)
        r.dy[start:start + n] = jnp.where(row < r.lens[s], r.token[s:s + 1], 0.0)
    pairs = r.q.shape[1] // 128

    def layer(t, _):
        l = layers - 1 - t
        f = Backward(l, seqs, r)
        after, more = t > 0, t + 1 < layers
        def old(kind, j):
            def go():
                @pl.when(after)
                def _():
                    kind(t - 1, j)
            return go
        def new(kind, j):
            return lambda: kind(t, j)
        def run(ops, n=1):
            for _ in range(min(n, len(ops))):
                ops.pop(0)()
        def again(*nm):
            @pl.when(more)
            def _():
                for x in nm:
                    load(l - 1, x).start()
        ops = [old(*x) for x in (
            (red.s2, 1), (red.sz1, 0), (red.s1, 2), (red.sz2, 0), (red.s3, 1), (red.sp, 0), (red.sz1, 1), (red.sq, 0), (red.s2, 2),
            (red.sz2, 1), (red.sr, 0), (red.s3, 2), (red.sp, 1), (red.sq, 1), (red.sr, 1))]
        load(l, "n2").wait()
        load(l, "r2").wait()
        for b in f.blocks:
            f.norm(b, 1)
            run(ops)
        load(l, "n1").start()
        load(l, "r1").start()
        r.low_t[...] = r.low[...].T
        load(l, "hr").wait()
        r.hr_t[...] = r.hc[...].T
        load(l, "ctx").start()
        def chunk(c, _):
            slot = lax.rem(c, 2)
            w = 2 * slot
            aload(l, c, 0).wait()
            @pl.when(c > 0)
            def _():
                ffn_save(l, c - 1, 0).wait()
                red.s0(t, 0, c - 1)
            f.ffn_down(slot)
            ffn_save(l, c, 0).start()
            aload(l, c, 1).wait()
            ffn_w(t, c, 0).wait()
            for b in f.blocks:
                f.ffn_mid(c, b, slot, w)
            for half in range(2):
                if half == 1:
                    @pl.when(c > 0)
                    def _():
                        ffn_save(l, c - 1, 1).wait()
                        red.s0(t, 1, c - 1)
                    f.ffn_up()
                    ffn_save(l, c, 1).start()
                    ffn_w(t, c, 1).wait()
                    for b in f.blocks:
                        f.ffn_back(b, w + 1)
                @pl.when(c + 2 < ways)
                def _():
                    ffn_w(t, c + 2, half).start()
                for late in range(2):
                    @pl.when(c == ways - 2 + late)
                    def _():
                        attn_w(t, 2 * late + half).start()
                if half == 0:
                    over = (c + 2) // ways
                    @pl.when(l - over >= 0)
                    def _():
                        for j in range(2):
                            aload(l - over, c + 2 - over * ways, j).start()
            for at in range(ways):
                @pl.when(c == at)
                def _():
                    run(ops, 3)
            return 0
        lax.fori_loop(0, ways, chunk, 0)
        load(l, "xr").start()
        ops = [new(red.s1, 0), new(red.s1, 1), old(red.sz1, 2), old(red.sz2, 2), old(red.sp, 2), new(red.s2, 0), old(red.sq, 2), new(red.s3, 0), old(red.sr, 2)]
        for j in range(2):
            ffn_save(l, ways - 1, j).wait()
            red.s0(t, j, ways - 1)
        load(l, "n1").wait()
        load(l, "r1").wait()
        for b in f.blocks:
            f.norm(b, 0)
        again("n2", "r2")
        run(ops)
        attn_w(t, 0).wait()
        for b in f.blocks:
            f.context(b, 0)
        @pl.when(more)
        def _():
            ffn_w(t + 1, 0, 0).start()
        run(ops)
        load(l, "ctx").wait()
        f.out_grad(0)
        attn_save(l, 3, 0).start()
        again("hr")
        for nm in ("q", "k", "v", "lse"):
            load(l, nm).wait()
        def pair(i, _):
            for s in range(len(seqs)):
                f.attend(s, i)
            for at in (0, 2, 4):
                @pl.when(i == at)
                def _():
                    run(ops)
            return 0
        lax.fori_loop(0, pairs, pair, 0)
        again("q", "k", "v", "lse")
        load(l, "xr").wait()
        for m in range(3):
            slot = (m + 1) % 2
            if m == 1:
                attn_save(l, 3, 0).wait()
            if m == 2:
                attn_save(l, 0, 1).wait()
            f.qkv_grad(m, slot)
            attn_save(l, m, slot).start()
            run(ops)
        run(ops, len(ops))
        attn_save(l, 1, 0).wait()
        attn_save(l, 2, 1).wait()
        for i in red.pieces(2):
            red.s0(t, 2, i)
        for m in range(3):
            attn_w(t, m + 1).wait()
            for b in f.blocks:
                f.back_in(b, m, m + 1)
            @pl.when(more)
            def _():
                ffn_w(t + 1, (m + 1) // 2, (m + 1) % 2).start()
        return 0
    lax.fori_loop(0, layers, layer, 0)

    names_dp = ["core", "x", "y"] + far
    for l in range(layers):
        r.small[0, l] = r.sums[l]
        for c in range(ways):
            r.small[0, l, UB + c:UB + c + 1] = r.su[l, c]
    def sd(i):
        return red.remote(r.small.at[i], r.small_in.at[i], (r.v_send, r.v_recv), i, names_dp[i])
    def sm(k):
        n = len(names_dp)
        return red.remote(r.small.at[n], r.small_in.at[n + k - 1], (r.v_send, r.v_recv), n + k - 1, f"z{k}")
    def small_step(i):
        def go():
            if i > 0:
                sd(i - 1).wait_recv()
                r.small[i] = r.small[i - 1] + r.small_in[i - 1]
            if i < len(names_dp):
                sd(i).start()
            else:
                for k in range(1, ways):
                    sm(k).start()
        return go
    def small_end():
        n = len(names_dp)
        for k in range(1, ways):
            sm(k).wait_recv()
        v = [r.small.at[n]] + [r.small_in.at[n + k - 1] for k in range(1, ways)]
        for l in range(layers):
            part = v[0].shape[-1] // ways
            even, odd = v[0][l], v[1][l]
            for k in range(2, ways):
                if k % 2:
                    odd = odd + v[k][l]
                else:
                    even = even + v[k][l]
            r.small_out[l] = even + odd
            split, up = None, None
            for k in range(ways):
                back = (ways - k) % ways
                row = v[k][l, QB:VB + 1]
                if back:
                    row = pltpu.roll(row, (ways - back) * part, 1)
                split = row if split is None else split + row
                one = v[k][l, UB + back:UB + back + 1]
                up = one if up is None else up + one
            r.small_out[l, QB:VB + 1] = split
            r.small_out[l, UB:UB + 1] = up
    t = layers - 1
    a, b, c = 0, 1, 2
    tail = [(red.s2, b), (red.sz1, a), (red.s1, c), (red.sz2, a), (red.s3, b), (red.sp, a), (red.sz1, b), (red.s2, c), (red.sq, a), (red.sz2, b),
            (red.s3, c), (red.sr, a), (red.sp, b), (red.sz1, c), (red.sq, b), (red.sz2, c), (red.sr, b), (red.sp, c), (red.sq, c), (red.sr, c)]
    smalls = [small_step(i) for i in range(len(names_dp) + 1)]
    for i, (kind, j) in enumerate(tail):
        kind(t, j)
        if smalls and i % 2 == 0:
            smalls.pop(0)()
    for go in smalls:
        go()
    small_end()
    def finish(t, _):
        for j in range(3):
            red.end(t, j)
        return 0
    lax.fori_loop(0, layers, finish, 0)
    for i in range(len(names_dp)):
        sd(i).wait_send()
    for k in range(1, ways):
        sm(k).wait_send()


def backward(saved, w, lens, gain, seqs, collective_id):
    T, D = saved["q"].shape[1:]
    G, ways, R, _ = w.shape
    L = G // 3
    V = pl.BlockSpec(memory_space=pltpu.VMEM)
    S = pl.BlockSpec(memory_space=pltpu.SMEM)
    ins = dict(lens=(lens, S), token=(saved["token"], V), w_in=(w, ANY), gain=(gain, V))
    for n in ("n2", "r2", "hr", "n1", "r1", "ctx", "q", "k", "v", "lse", "xr"):
        ins[n + "_in"] = (saved[n], ANY)
    ins["a_in"] = (saved["a_out"], ANY)
    ins["slope_in"] = (saved["slope_out"], ANY)
    half = R // 16
    block = (2, 2, half, D)
    outs = dict(
        dy=((T, D), F32, V), small_out=((L, 16, D), F32, V), reduced=((G, 8, 2, half, D), BF16, ANY),
        g_down=((L, ways, 4, *block), BF16, ANY), g_up=((L, ways, 4, *block), BF16, ANY), g_attn=((L, 4, ways, *block), BF16, ANY),
        got=((G, ways, 2, *block), BF16, ANY))
    H = saved["lse"].shape[1]
    nfar = 0
    while 8 << nfar < lax.axis_size("dp"):
        nfar += 1
    VM, DMA = pltpu.VMEM, pltpu.SemaphoreType.DMA
    per = 8 + ways - 1 + nfar
    steps = 3 + nfar
    each = 2 * ways + 4
    scratch = dict(
        mask=VM((T, 128), F32), n=VM((T, D), F32), inv=VM((T, 128), F32), hc=VM((T, D), BF16), hr_t=VM((D, T), BF16),
        low=VM((T, D), BF16), low_t=VM((D, T), BF16), dz=VM((T, D), F32), du=VM((T, R), BF16),
        a=VM((2, T, R), BF16), slope=VM((2, T, R), BF16), q=VM((T, D), BF16), k=VM((T, D), BF16), v=VM((T, D), BF16),
        lse=VM((H, 8, T), F32), dk=VM((T, D), BF16), dv=VM((T, D), BF16),
        stage=VM((2, 4, *block), BF16), w=VM((4, R, D), BF16), sums=VM((L, 16, D), F32), su=VM((L, ways, 1, R), F32),
        own=VM((3, ways, 2, *block), BF16), got_v=VM((ways, 2, *block), BF16),
        got_a=VM((G, ways, 2, half, D), BF16), got_b=VM((G, ways, 2, half, D), BF16),
        got_c=VM((G, ways, half, D), BF16), got_d=VM((G, ways, half, D), BF16),
        zin=VM((G, ways - 1, 2, half, D), BF16), zout=VM((G, ways, 2, half, D), BF16),
        small=VM((steps + 1, L, 16, D), F32), small_in=VM((steps + ways - 1, L, 16, D), F32),
        w_sem=DMA((L * each,)), i_sem=DMA((L * 11,)), a_sem=DMA((L * ways * 2,)), o_sem=DMA((L * each,)),
        l_sem=DMA((G * 4,)), f_sem=DMA((G,)), m_sem=DMA((G,)), r_send=DMA((G * per,)), r_recv=DMA((G * per,)),
        g_send=DMA((G * 8,)), g_recv=DMA((G * 8,)), v_send=DMA((steps + ways - 1,)), v_recv=DMA((steps + ways - 1,)))
    if T != D:
        scratch["dctx"] = VM((T, D), BF16)
        scratch["dq"] = VM((T, D), BF16)
    if nfar:
        scratch["far"] = VM((G, nfar, 2, half, D), BF16)
    names = tuple(ins) + tuple(outs) + tuple(scratch)
    res = pl.pallas_call(
        functools.partial(backward_kernel, seqs, L, ways, names),
        out_shape=[jax.ShapeDtypeStruct(s, d) for s, d, _ in outs.values()],
        in_specs=[s for _, s in ins.values()],
        out_specs=[s for _, _, s in outs.values()],
        scratch_shapes=list(scratch.values()),
        compiler_params=pltpu.CompilerParams(collective_id=collective_id, has_side_effects=True, vmem_limit_bytes=255 << 18),
        name="backward_layers",
    )(*[v for v, _ in ins.values()])
    return dict(zip(outs, res))


def finish_kernel(order, reduced, dy, qkv, out, up, down, q_grad, p_grad):
    layers = out.shape[0]
    part = out.shape[1]
    for l in range(layers):
        attn = reduced[order[l, 2]].astype(F32)
        qkv[l] = attn[:3 * part]
        out[l] = attn[3 * part:]
        up[l] = reduced[order[l, 1]].astype(F32)
        down[l] = reduced[order[l, 0]].astype(F32).T
    rows = q_grad.shape[0]
    q_grad[...] = dy[:rows]
    p_grad[...] = dy[rows:]


def finish(reduced, dy, layers, part, rows):
    G, R, D = reduced.shape
    T = dy.shape[0]
    order = {(l, j): 3 * (layers - 1 - l) + j for l in range(layers) for j in range(3)}
    V = pl.BlockSpec(memory_space=pltpu.VMEM)
    shapes = [(layers, 3 * part, D), (layers, part, D), (layers, D, R), (layers, R, D), (rows, D), (T - rows, D)]
    return pl.pallas_call(
        functools.partial(finish_kernel, order),
        out_shape=[jax.ShapeDtypeStruct(s, F32) for s in shapes],
        in_specs=[V, V], out_specs=[V] * 6,
        compiler_params=pltpu.CompilerParams(vmem_limit_bytes=60 << 20),
        name="finish",
    )(reduced, dy)


def local(
    query_states,
    passage_states,
    query_lengths,
    passage_lengths,
    query_count,
    passage_count,
    positive,
    query_key_value_matrix,
    qv_bias,
    out_weight,
    out_bias,
    norm_gain,
    norm_bias,
    up_matrix,
    up_bias,
    down_matrix,
    down_bias,
):
    layers = query_key_value_matrix.shape[0]
    width = query_states.shape[-1]
    ways = lax.axis_size("mp")
    mp_rank = lax.axis_index("mp")
    q_slots, q_len, _ = query_states.shape
    p_slots, p_len, _ = passage_states.shape
    shapes = ((q_slots, q_len), (p_slots, p_len))
    lengths = (
        lax.dynamic_slice_in_dim(query_lengths, mp_rank * q_slots, q_slots),
        lax.dynamic_slice_in_dim(passage_lengths, mp_rank * p_slots, p_slots),
    )
    part = qv_bias.shape[-1]

    hidden = up_bias.shape[-1]
    tiny = jnp.concatenate(
        [
            jnp.pad(qv_bias.reshape(2 * layers, part), ((0, 0), (0, width - part))),
            up_bias,
            jnp.zeros((16 - 3 * layers, width), BF16),
        ]
    )
    seqs, at = [], 0
    for count, length in shapes:
        for _ in range(count):
            seqs.append((at, length))
            at += length
    seqs = tuple(seqs)
    all_lens = jnp.concatenate(lengths)
    saved = forward(
        query_states, passage_states, jnp.swapaxes(query_key_value_matrix, 2, 3), out_weight, up_matrix, down_matrix,
        all_lens, (positive, query_count, passage_count), tiny, (out_bias, norm_gain, norm_bias, down_bias), seqs, ways, 0,
    )
    loss = saved["loss"][0, 0]
    back = backward(
        saved, saved["w"].reshape(3 * layers, 4, -1, width), all_lens, norm_gain.astype(F32), seqs, 1
    )
    reduced = back["reduced"].reshape(3 * layers, -1, width)
    qkv_grad, out_grad, up_grad, down_grad, query_grad, passage_grad = finish(
        reduced, back["dy"], layers, part, q_slots * q_len
    )
    qkv_grad = jnp.swapaxes(qkv_grad.reshape(layers, 3, part, width), 2, 3)
    query_grad = query_grad.reshape(query_states.shape)
    passage_grad = passage_grad.reshape(passage_states.shape)
    small = back["small_out"]

    return (
        loss,
        query_grad,
        passage_grad,
        qkv_grad,
        small[:, QB : VB + 1, :part],
        out_grad,
        small[:, OB],
        small[:, GAIN : GAIN + 2],
        small[:, BIAS : BIAS + 2],
        up_grad,
        small[:, UB, : up_bias.shape[-1]],
        down_grad,
        small[:, DB],
    )


def solution(mesh):
    placed = (
        P(("dp", "mp"), None, None),
        P(("dp", "mp"), None, None),
        P("dp"),
        P("dp"),
        P(),
        P(),
        P(("dp", "mp")),
        P(None, None, None, "mp"),
        P(None, None, "mp"),
        P(None, "mp", None),
        P(),
        P(),
        P(),
        P(None, None, "mp"),
        P(None, "mp"),
        P(None, "mp", None),
        P(),
    )
    return jax.shard_map(
        local,
        mesh=mesh,
        in_specs=placed,
        out_specs=(
            P(),
            P(("dp", "mp"), None, None),
            P(("dp", "mp"), None, None),
            P(None, None, None, "mp"),
            P(None, None, "mp"),
            P(None, "mp", None),
            P(),
            P(),
            P(),
            P(None, None, "mp"),
            P(None, "mp"),
            P(None, "mp", None),
            P(),
        ),
        check_vma=False,
    )
```

time: 862 us -> 423 us (0.49)
  Pallas kernels: 0 us -> 409 us
  waiting for transfers between devices: 233 us -> 0 us
  matrix products: 193 us -> 0 us
  local copies, waits for them, and re-layouts: 164 us -> 8.93 us
  starting transfers between devices: 132 us -> 0 us
  other arithmetic: 122 us -> 3.89 us
  between operations: 9.7 us -> 0.67 us
    pallas_call x0 -> x3, Pallas kernels: none -> 409 us  [the longest x1 233 us: backward(): pl.pallas_call(functools.partial(backward_kernel, seqs, L, ways, names),...]
    ppermute x144 -> x0, waiting for transfers between devices: 233 us -> none  [the longest x99 160 us: flip(): return lax.ppermute(value, 'dp', [(i, i ^ bit) for i in range(size)])]
    dot_general x63 -> x0, matrix products: 193 us -> none  [the longest x60 191 us: mm(): return jnp.einsum(spec, left, right, preferred_element_type=F32)]
    ppermute x144 -> x0, starting transfers between devices: 132 us -> none  [the longest x99 97 us: flip(): return lax.ppermute(value, 'dp', [(i, i ^ bit) for i in range(size)])]
    unnamed x531 -> x2, local copies, waits for them, and re-layouts: 45.7 us -> 1.2 us
    reshape x26 -> x1, local copies, waits for them, and re-layouts: 42.6 us -> 0.7 us  [local(): qv_bias.reshape(2 * layers, part)]
    convert_element_type x62 -> x1, other arithmetic: 30.4 us -> 1.3 us  [local(): norm_gain.astype(F32)]
    dynamic_slice x21 -> x1, local copies, waits for them, and re-layouts: 25.4 us -> 0.73 us  [local(): lax.dynamic_slice_in_dim(query_lengths, mp_rank * q_slots, q_slots)]
  transfers between devices with their start and end apart: 144 -> 0, of which waited for: 69 -> 0; matrix products, arithmetic and copies ran while one was open for 28% -> 0% of each run, Pallas kernels for 0% -> 0%
where the time goes in v4:
time: 423 us
  Pallas kernels  409 us (97%)
  local copies, waits for them, and re-layouts  8.93 us (2%)
    pallas_call x1, Pallas kernels, backward(): pl.pallas_call(functools.partial(backward_kernel, seqs, L, ways, names),...  233 us
    pallas_call x1, Pallas kernels, forward(): pl.pallas_call(functools.partial(forward_kernel, seqs, L, ways, names), o...  166 us
    pallas_call x1, Pallas kernels, finish(): pl.pallas_call(functools.partial(finish_kernel, order), out_shape=[jax.Sh...  10.2 us

profile of v4, /device:TPU:0, one launch (start us, length us, event | category | flops | bytes accessed | tf_op | source)
XLA Modules:
  0.0 422.6 jit_solution(18116476351095480870)
XLA Ops:
  0.6 1.2 dynamic_slice.7
  1.9 0.7 dynamic_slice.6
  2.6 1.2 pad_add_fusion.refs_0_
  3.9 0.1 pad.7.clone
  3.9 0.7 reshape.44
  4.6 1.3 convert_element_type.5.refs_3_
  5.9 1.4 fusion.2.refs_7_
  7.3 165.7 %forward_layers.1 = (f32[8,128]{1,0:T(8,128)}, f32[8,768]{1,0:T(8,128)}, bf16[2,768,768]{2,1,0:T(8,128)(2,1)}, bf16[2,768,768]{2,1,0:T(8,128)(2,1)}, bf16[2,768,...) custom-call(s32[3]{0:T(128)} %pad_add_fusion.refs_0_, ...), custom_call_target="tpu_custom_call" | custom-call | tf_op jit(solution)/shard_map/forward_layers/pallas_call | solution.py:562
  173.0 1.2 slice.21
  174.2 233.3 %backward_layers.1 = (f32[768,768]{1,0:T(8,128)}, f32[2,16,768]{2,1,0:T(8,128)}, bf16[6,8,2,48,768]{4,3,2,1,0:T(8,128)(2,1)}, bf16[2,4,4,2,2,48,768]{6,5,4,3,2,1...) custom-call(s32[3]{0:T(128)} %pad_add_fusion.refs_0_, ...), custom_call_target="tpu_custom_call" | custom-call | tf_op jit(solution)/shard_map/backward_layers/pallas_call | solution.py:1126
  407.5 1.3 slice.22
  408.8 0.9 fusion.3
  409.7 1.6 fusion.4
  411.3 0.6 copy_bitcast_fusion
  411.9 0.6 copy.36
  412.5 10.2 %finish.1 = (f32[2,576,768]{2,1,0:T(8,128)}, f32[2,192,768]{2,1,0:T(8,128)}, f32[2,768,768]{2,1,0:T(8,128)}, f32[2,768,768]{2,1,0:T(8,128)}, f32[256,768]{1,0:T(8,128)}, /*index=5*/f32[512,768]{1,0:T(8,128)}) custom-call(bf16[6,768,768]{2,1,0:T(8,128)(2,1)} %bitcast.17, f32[768,768]{1,0:T(8,128)} %get-tuple-element.55.dy), custom_call_target="tpu_custom_call" | custom-call | tf_op jit(solution)/shard_map/finish/pallas_call | solution.py:1158
  (1 shorter events, 0.0 us)

commit v5 on v4

--- a/solution.py
+++ b/solution.py
@@ -248,6 +248,12 @@
         r.x[b] = y
         r.xr[b] = y.astype(BF16)
 
+def length(r, ways, s):
+    me = lax.axis_index("mp")
+    q_slots, p_slots = r.q_lens.shape[0] // ways, r.p_lens.shape[0] // ways
+    return r.q_lens[me * q_slots + s] if s < q_slots else r.p_lens[me * p_slots + s - q_slots]
+
+
 def contrast(r, z, seqs, ways, extra):
     d, me = lax.axis_index("dp"), lax.axis_index("mp")
     rank = d * ways + me
@@ -264,8 +270,8 @@
     lane = lax.broadcasted_iota(jnp.int32, (1, 128), 1)
     for s, (start, n) in enumerate(seqs):
         row = lax.broadcasted_iota(jnp.int32, (n, 128), 0)
-        live = jnp.concatenate([row < r.lens[s]] * parts, axis=1)
-        size = jnp.full((1, 1), r.lens[s], jnp.int32).astype(F32)
+        live = jnp.concatenate([row < length(r, ways, s)] * parts, axis=1)
+        size = jnp.full((1, 1), length(r, ways, s), jnp.int32).astype(F32)
         pooled = jnp.sum(jnp.where(live, r.x[start:start + n], 0.0), axis=0, keepdims=True) / size
         inv = lax.rsqrt(jnp.sum(pooled * pooled, axis=1, keepdims=True) + 1e-06)
         normed = pooled * inv
@@ -386,7 +392,7 @@
             z.own_copy(l, j).start()
     for s, (start, n) in enumerate(seqs):
         row = lax.broadcasted_iota(jnp.int32, (n, 128), 0)
-        r.mask[start:start + n] = jnp.where(row < r.lens[s], 0.0, NEG_FILL)
+        r.mask[start:start + n] = jnp.where(row < length(r, ways, s), 0.0, NEG_FILL)
     at = 0
     for ref in (r.q_in, r.p_in):
         for i in range(ref.shape[0]):
@@ -520,7 +526,7 @@
     for name in kept[-2:]:
         keep(layers - 1, name).wait()
 
-def forward(query_states, passage_states, qkv_w, out_w, up_w, down_w, lens, targets, tiny, shared, seqs, ways, collective_id):
+def forward(query_states, passage_states, qkv_w, out_w, up_w, down_w, q_lens, p_lens, targets, tiny, shared, seqs, ways, collective_id):
     D = query_states.shape[-1]
     T = sum(n for _, n in seqs)
     L = qkv_w.shape[0]
@@ -529,7 +535,7 @@
     V = pl.BlockSpec(memory_space=pltpu.VMEM)
     S = pl.BlockSpec(memory_space=pltpu.SMEM)
     heads = D // HEAD_DIM
-    ins = dict(lens=(lens, S), q_in=(query_states, V), p_in=(passage_states, V), qkv_w=(qkv_w, V), out_w=(out_w, V),
+    ins = dict(q_lens=(q_lens, S), p_lens=(p_lens, S), q_in=(query_states, V), p_in=(passage_states, V), qkv_w=(qkv_w, V), out_w=(out_w, V),
                up_w=(up_w, ANY), down_w=(down_w, ANY), tiny_in=(tiny, V))
     for name, value in zip(("out_b_in", "gain_in", "bias_in", "down_b_in"), shared):
         ins[name] = (value, V)
@@ -836,7 +842,8 @@
     greet(["core", "x", "y"] + [f"z{k}" for k in range(1, ways)] + far, red.peers)
     for s, (start, n) in enumerate(seqs):
         row = lax.broadcasted_iota(jnp.int32, (n, 128), 0)
-        r.mask[start:start + n] = jnp.where(row < r.lens[s], 0.0, NEG_FILL)
+        r.mask[start:start + n] = jnp.where(row < length(r, ways, s), 0.0, NEG_FILL)
+    r.gain[...] = r.gain_in[...].astype(F32)
     each = 2 * ways + 4
     heads_order = (3, 0, 1, 2)
     def wload(t, local, group, block):
@@ -869,7 +876,7 @@
         load(top, name).start()
     for s, (start, n) in enumerate(seqs):
         row = lax.broadcasted_iota(jnp.int32, (n, r.dy.shape[1]), 0)
-        r.dy[start:start + n] = jnp.where(row < r.lens[s], r.token[s:s + 1], 0.0)
+        r.dy[start:start + n] = jnp.where(row < length(r, ways, s), r.token[s:s + 1], 0.0)
     pairs = r.q.shape[1] // 128
 
     def layer(t, _):
@@ -1078,13 +1085,13 @@
         sm(k).wait_send()
 
 
-def backward(saved, w, lens, gain, seqs, collective_id):
+def backward(saved, w, q_lens, p_lens, gain, seqs, collective_id):
     T, D = saved["q"].shape[1:]
     G, ways, R, _ = w.shape
     L = G // 3
     V = pl.BlockSpec(memory_space=pltpu.VMEM)
     S = pl.BlockSpec(memory_space=pltpu.SMEM)
-    ins = dict(lens=(lens, S), token=(saved["token"], V), w_in=(w, ANY), gain=(gain, V))
+    ins = dict(q_lens=(q_lens, S), p_lens=(p_lens, S), token=(saved["token"], V), w_in=(w, ANY), gain_in=(gain, V))
     for n in ("n2", "r2", "hr", "n1", "r1", "ctx", "q", "k", "v", "lse", "xr"):
         ins[n + "_in"] = (saved[n], ANY)
     ins["a_in"] = (saved["a_out"], ANY)
@@ -1104,7 +1111,7 @@
     steps = 3 + nfar
     each = 2 * ways + 4
     scratch = dict(
-        mask=VM((T, 128), F32), n=VM((T, D), F32), inv=VM((T, 128), F32), hc=VM((T, D), BF16), hr_t=VM((D, T), BF16),
+        gain=VM(gain.shape, F32), mask=VM((T, 128), F32), n=VM((T, D), F32), inv=VM((T, 128), F32), hc=VM((T, D), BF16), hr_t=VM((D, T), BF16),
         low=VM((T, D), BF16), low_t=VM((D, T), BF16), dz=VM((T, D), F32), du=VM((T, R), BF16),
         a=VM((2, T, R), BF16), slope=VM((2, T, R), BF16), q=VM((T, D), BF16), k=VM((T, D), BF16), v=VM((T, D), BF16),
         lse=VM((H, 8, T), F32), dk=VM((T, D), BF16), dv=VM((T, D), BF16),
@@ -1135,33 +1142,43 @@
     return dict(zip(outs, res))
 
 
-def finish_kernel(order, reduced, dy, qkv, out, up, down, q_grad, p_grad):
-    layers = out.shape[0]
+def finish_kernel(reduced, dy, small, qkv, out, up, down, q_grad, p_grad, qv_bias, out_bias, gain, bias, up_bias, down_bias):
     part = out.shape[1]
-    for l in range(layers):
-        attn = reduced[order[l, 2]].astype(F32)
-        qkv[l] = attn[:3 * part]
-        out[l] = attn[3 * part:]
-        up[l] = reduced[order[l, 1]].astype(F32)
-        down[l] = reduced[order[l, 0]].astype(F32).T
-    rows = q_grad.shape[0]
-    q_grad[...] = dy[:rows]
-    p_grad[...] = dy[rows:]
-
-
-def finish(reduced, dy, layers, part, rows):
+    attn = reduced[2].astype(F32)
+    qkv[0] = attn[:3 * part]
+    out[0] = attn[3 * part:]
+    up[0] = reduced[1].astype(F32)
+    down[0] = reduced[0].astype(F32).T
+
+    @pl.when(pl.program_id(0) == 0)
+    def _():
+        rows = q_grad.shape[0]
+        q_grad[...] = dy[:rows]
+        p_grad[...] = dy[rows:]
+        for l in range(small.shape[0]):
+            qv_bias[l] = small[l, QB:VB + 1, :part]
+            out_bias[l:l + 1] = small[l, OB:OB + 1]
+            gain[l] = small[l, GAIN:GAIN + 2]
+            bias[l] = small[l, BIAS:BIAS + 2]
+            up_bias[l:l + 1] = small[l, UB:UB + 1, :up_bias.shape[1]]
+            down_bias[l:l + 1] = small[l, DB:DB + 1]
+
+
+def finish(reduced, dy, small, layers, part, rows):
     G, R, D = reduced.shape
     T = dy.shape[0]
-    order = {(l, j): 3 * (layers - 1 - l) + j for l in range(layers) for j in range(3)}
-    V = pl.BlockSpec(memory_space=pltpu.VMEM)
-    shapes = [(layers, 3 * part, D), (layers, part, D), (layers, D, R), (layers, R, D), (rows, D), (T - rows, D)]
+    per_layer = [(3 * part, D), (part, D), (D, R), (R, D)]
+    once = [(rows, D), (T - rows, D), (layers, 2, part), (layers, D), (layers, 2, D), (layers, 2, D), (layers, R), (layers, D)]
+    whole = lambda shape: pl.BlockSpec(shape, lambda l: (0,) * len(shape))
     return pl.pallas_call(
-        functools.partial(finish_kernel, order),
-        out_shape=[jax.ShapeDtypeStruct(s, F32) for s in shapes],
-        in_specs=[V, V], out_specs=[V] * 6,
+        finish_kernel,
+        grid=(layers,),
+        out_shape=[jax.ShapeDtypeStruct((layers, *s), F32) for s in per_layer] + [jax.ShapeDtypeStruct(s, F32) for s in once],
+        in_specs=[pl.BlockSpec((3, R, D), lambda l: (layers - 1 - l, 0, 0)), whole(dy.shape), whole(small.shape)],
+        out_specs=[pl.BlockSpec((1, *s), lambda l: (l, 0, 0)) for s in per_layer] + [whole(s) for s in once],
         compiler_params=pltpu.CompilerParams(vmem_limit_bytes=60 << 20),
         name="finish",
-    )(reduced, dy)
+    )(reduced, dy, small)
 
 
 def local(
@@ -1186,14 +1203,9 @@
     layers = query_key_value_matrix.shape[0]
     width = query_states.shape[-1]
     ways = lax.axis_size("mp")
-    mp_rank = lax.axis_index("mp")
     q_slots, q_len, _ = query_states.shape
     p_slots, p_len, _ = passage_states.shape
     shapes = ((q_slots, q_len), (p_slots, p_len))
-    lengths = (
-        lax.dynamic_slice_in_dim(query_lengths, mp_rank * q_slots, q_slots),
-        lax.dynamic_slice_in_dim(passage_lengths, mp_rank * p_slots, p_slots),
-    )
     part = qv_bias.shape[-1]
 
     hidden = up_bias.shape[-1]
@@ -1210,38 +1222,23 @@
             seqs.append((at, length))
             at += length
     seqs = tuple(seqs)
-    all_lens = jnp.concatenate(lengths)
     saved = forward(
         query_states, passage_states, jnp.swapaxes(query_key_value_matrix, 2, 3), out_weight, up_matrix, down_matrix,
-        all_lens, (positive, query_count, passage_count), tiny, (out_bias, norm_gain, norm_bias, down_bias), seqs, ways, 0,
+        query_lengths, passage_lengths, (positive, query_count, passage_count), tiny, (out_bias, norm_gain, norm_bias, down_bias), seqs, ways, 0,
     )
     loss = saved["loss"][0, 0]
     back = backward(
-        saved, saved["w"].reshape(3 * layers, 4, -1, width), all_lens, norm_gain.astype(F32), seqs, 1
+        saved, saved["w"].reshape(3 * layers, 4, -1, width), query_lengths, passage_lengths, norm_gain, seqs, 1
     )
     reduced = back["reduced"].reshape(3 * layers, -1, width)
-    qkv_grad, out_grad, up_grad, down_grad, query_grad, passage_grad = finish(
-        reduced, back["dy"], layers, part, q_slots * q_len
+    qkv_grad, out_grad, up_grad, down_grad, query_grad, passage_grad, qv_b, out_b, gain_g, bias_g, up_b, down_b = finish(
+        reduced, back["dy"], back["small_out"], layers, part, q_slots * q_len
     )
     qkv_grad = jnp.swapaxes(qkv_grad.reshape(layers, 3, part, width), 2, 3)
     query_grad = query_grad.reshape(query_states.shape)
     passage_grad = passage_grad.reshape(passage_states.shape)
-    small = back["small_out"]
-
     return (
-        loss,
-        query_grad,
-        passage_grad,
-        qkv_grad,
-        small[:, QB : VB + 1, :part],
-        out_grad,
-        small[:, OB],
-        small[:, GAIN : GAIN + 2],
-        small[:, BIAS : BIAS + 2],
-        up_grad,
-        small[:, UB, : up_bias.shape[-1]],
-        down_grad,
-        small[:, DB],
+        loss, query_grad, passage_grad, qkv_grad, qv_b, out_grad, out_b, gain_g, bias_g, up_grad, up_b, down_grad, down_b
     )
 
 

time: 423 us -> 414 us (0.979)
  local copies, waits for them, and re-layouts: 8.93 us -> 1.96 us
where the time goes in v5:
time: 414 us; the launch traced here: 413 us
  Pallas kernels  409 us (99%)
    pallas_call x1, Pallas kernels, backward(): pl.pallas_call(functools.partial(backward_kernel, seqs, L, ways, names),...  234 us
    pallas_call x1, Pallas kernels, forward(): pl.pallas_call(functools.partial(forward_kernel, seqs, L, ways, names), o...  165 us
    pallas_call x1, Pallas kernels, finish(): pl.pallas_call(finish_kernel, grid=(layers,), out_shape=[jax.ShapeDtypeSt...  9.38 us

profile of v5, /device:TPU:0, one launch (start us, length us, event | category | flops | bytes accessed | tf_op | source)
XLA Modules:
  0.0 413.0 jit_solution(18366283601281800674)
XLA Ops:
  0.7 0.1 pad.7.clone
  0.7 0.7 reshape.44
  1.4 1.4 fusion.2.refs_8_
  2.8 165.5 %forward_layers.1 = (f32[8,128]{1,0:T(8,128)}, f32[8,768]{1,0:T(8,128)}, bf16[2,768,768]{2,1,0:T(8,128)(2,1)}, bf16[2,768,768]{2,1,0:T(8,128)(2,1)}, bf16[2,768,...) custom-call(s32[8]{0:T(128)} %refs_0_.3, ...), custom_call_target="tpu_custom_call" | custom-call | tf_op jit(solution)/shard_map/forward_layers/pallas_call | solution.py:568
  168.3 1.2 slice.3
  169.5 234.0 %backward_layers.1 = (f32[768,768]{1,0:T(8,128)}, f32[2,16,768]{2,1,0:T(8,128)}, bf16[6,8,2,48,768]{4,3,2,1,0:T(8,128)(2,1)}, bf16[2,4,4,2,2,48,768]{6,5,4,3,2,1...) custom-call(s32[8]{0:T(128)} %refs_0_.3, ...), custom_call_target="tpu_custom_call" | custom-call | tf_op jit(solution)/shard_map/backward_layers/pallas_call | solution.py:1133
  403.5 9.4 %finish.1 = (f32[2,576,768]{2,1,0:T(8,128)}, f32[2,192,768]{2,1,0:T(8,128)}, f32[2,768,768]{2,1,0:T(8,128)}, f32[2,768,768]{2,1,0:T(8,128)}, f32[256,768]{1,0:T(...) custom-call(bf16[6,768,768]{2,1,0:T(8,128)(2,1)} %bitcast.10, ...), custom_call_target="tpu_custom_call" | custom-call | tf_op jit(solution)/shard_map/finish/pallas_call | solution.py:1173
  (1 shorter events, 0.0 us)

commit v6 on v5

--- a/solution.py
+++ b/solution.py
@@ -374,10 +374,11 @@
         zpeers.append(f"z{k}")
         z.peers[f"z{k}"] = {"mp": lax.rem(lax.axis_index("mp") + k, ways)}
     part = z.part
-    for l in range(layers):
+    def build(l):
         for m in range(3):
             r.pack[l, m * part:(m + 1) * part] = r.qkv_w[l, m]
         r.pack[l, 3 * part:] = r.out_w[l]
+    build(0)
     r.tiny[0] = r.tiny_in[...]
     extra = far_peers()
     z.peers.update(extra)
@@ -387,6 +388,8 @@
     z.z_copy(0, 0, 1).start()
     for k in range(1, ways):
         tiny_copy(k).start()
+    for l in range(1, layers):
+        build(l)
     for l in range(layers):
         for j in range(3):
             z.own_copy(l, j).start()
@@ -448,6 +451,10 @@
         f = Forward(l, seqs, r)
         more = l + 1 < layers
         early = z.tick(l, 1) + z.tick(l, 2)
+        def up_here():
+            z.arrived(l, 1)
+            load(l, 1).start()
+        early.insert(13, up_here)
         late = z.tick(l, 3)
         def run(ops, n):
             for _ in range(min(n, len(ops))):
@@ -475,8 +482,6 @@
         for name in ("n1", "r1", "hr"):
             keep(l, name).start()
         run(early, len(early))
-        z.arrived(l, 1)
-        load(l, 1).start()
         z.arrived(l, 2)
         load(l, 2).start()
         load(l, 1).wait()

time: 414 us -> 410 us (level)
  no operation moved by 1% of the time
where the time goes in v6:
time: 410 us; the launch traced here: 409 us
  Pallas kernels  405 us (99%)
    pallas_call x1, Pallas kernels, backward(): pl.pallas_call(functools.partial(backward_kernel, seqs, L, ways, names),...  234 us
    pallas_call x1, Pallas kernels, forward(): pl.pallas_call(functools.partial(forward_kernel, seqs, L, ways, names), o...  162 us
    pallas_call x1, Pallas kernels, finish(): pl.pallas_call(finish_kernel, grid=(layers,), out_shape=[jax.ShapeDtypeSt...  9.38 us

profile of v6, /device:TPU:0, one launch (start us, length us, event | category | flops | bytes accessed | tf_op | source)
XLA Modules:
  0.0 409.1 jit_solution(13473346913671686859)
XLA Ops:
  0.7 0.1 pad.7.clone
  0.7 0.7 reshape.44
  1.4 1.4 fusion.2.refs_8_
  2.8 161.6 %forward_layers.1 = (f32[8,128]{1,0:T(8,128)}, f32[8,768]{1,0:T(8,128)}, bf16[2,768,768]{2,1,0:T(8,128)(2,1)}, bf16[2,768,768]{2,1,0:T(8,128)(2,1)}, bf16[2,768,...) custom-call(s32[8]{0:T(128)} %refs_0_.3, ...), custom_call_target="tpu_custom_call" | custom-call | tf_op jit(solution)/shard_map/forward_layers/pallas_call | solution.py:573
  164.4 1.2 slice.3
  165.6 233.9 %backward_layers.1 = (f32[768,768]{1,0:T(8,128)}, f32[2,16,768]{2,1,0:T(8,128)}, bf16[6,8,2,48,768]{4,3,2,1,0:T(8,128)(2,1)}, bf16[2,4,4,2,2,48,768]{6,5,4,3,2,1...) custom-call(s32[8]{0:T(128)} %refs_0_.3, ...), custom_call_target="tpu_custom_call" | custom-call | tf_op jit(solution)/shard_map/backward_layers/pallas_call | solution.py:1138
  399.5 9.4 %finish.1 = (f32[2,576,768]{2,1,0:T(8,128)}, f32[2,192,768]{2,1,0:T(8,128)}, f32[2,768,768]{2,1,0:T(8,128)}, f32[2,768,768]{2,1,0:T(8,128)}, f32[256,768]{1,0:T(...) custom-call(bf16[6,768,768]{2,1,0:T(8,128)(2,1)} %bitcast.10, ...), custom_call_target="tpu_custom_call" | custom-call | tf_op jit(solution)/shard_map/finish/pallas_call | solution.py:1178
  (1 shorter events, 0.0 us)
